TPU v7x, 32 devices: a whole 2x2x4 slice. The times are simulated.
32 devices in a mesh: rows: 8 (over y, x, core), ang: 4 (over z).
Axes of the slice: x: 2, y: 2, z: 4, core: 2. Of those that a mesh axis runs over, the one named last changes fastest.
Arguments:
- delta_obj: float32 [1088, 2, 512], P('rows', None, 'ang'), may hold values from -4 to 4
- beta_obj: float32 [1088, 2, 512], P('rows', None, 'ang'), may hold values from 0 to 0.15
- layer_shifts: int32 [4, 2], replicated, may hold values from -8 to 8
- illumination_field: float32 [2, 128, 128], replicated, may hold values from -6 to 6
- amplitudes: float32 [4, 32, 128, 128], P('ang', 'rows'), may hold values from 0.2 to 3
- positions: int32 [4, 32, 2], P('ang', 'rows'), may hold values from 0 to 384, as said below
- scan_counts: int32 [4, 8], P('ang', 'rows'), may hold values from 1 to 4, as said below
Outputs:
- grad_delta: float32 [1088, 2, 512], P('rows', None, 'ang')
- grad_beta: float32 [1088, 2, 512], P('rows', None, 'ang')
Inputs may be any that keep to these rules, and one draw needn't show every extreme that they name: `positions`: within each tile at each angle the slots come in order: a first group, at most 1 of them, has row offsets above 8; all later slots have row offsets of at most 8. Columns are at most 384. `scan_counts`: slots of a tile from this number on are not used.
All inputs are finite; a program needn't handle non-finite values.
Results may differ from a plain program's by a relative error of at most 0.0046.
Values may be sent and summed in bfloat16 or wider, within the bound.
No kernel may reach another device: no remote copies, remote signals or barrier semaphores. Data moves between devices by JAX's collectives and lax.ppermute only.
A program may use at most 64 MiB of HBM per device.

v0:
```python
import math

import jax
import jax.numpy as jnp
from jax import lax
from jax.sharding import PartitionSpec as P

PATTERN_PIXELS = 128
SHIFT = 8


best_prec = lax.Precision.HIGHEST
amp_floor = 0.1
scan_group_batch = 4


def from_behind(value, axis, steps):
    count = lax.axis_size(axis)
    initial, last = (max(0, -steps), min(count, count - steps))
    return lax.ppermute(value, axis, [(source, source + steps) for source in range(initial, last)])


def dft_tables():
    counter = jnp.arange(PATTERN_PIXELS, dtype=jnp.int32)
    product = counter[:, None] * counter[None, :] % PATTERN_PIXELS
    angle_table = product.astype(jnp.float32) * (2.0 * math.pi / PATTERN_PIXELS)
    factor = 1.0 / math.sqrt(PATTERN_PIXELS)
    return (jnp.cos(angle_table) * factor, -jnp.sin(angle_table) * factor)


def transform(real_in, imag_in, fourier_real, fourier_imaginary):
    left_re = jnp.matmul(fourier_real, real_in, precision=best_prec) - jnp.matmul(
        fourier_imaginary, imag_in, precision=best_prec
    )
    left_im = jnp.matmul(fourier_real, imag_in, precision=best_prec) + jnp.matmul(
        fourier_imaginary, real_in, precision=best_prec
    )
    out_re = jnp.matmul(left_re, fourier_real, precision=best_prec) - jnp.matmul(
        left_im, fourier_imaginary, precision=best_prec
    )
    out_im = jnp.matmul(left_re, fourier_imaginary, precision=best_prec) + jnp.matmul(
        left_im, fourier_real, precision=best_prec
    )
    return (out_re, out_im)


def scan_gradients(
    object_patches,
    illumination_field,
    measured_patterns,
    misfit_weight,
    fourier_real,
    fourier_imaginary,
):
    probe_re = illumination_field[0]
    probe_im = illumination_field[1]
    patch_re = object_patches[:, 0]
    patch_im = object_patches[:, 1]
    exit_re = probe_re * patch_re - probe_im * patch_im
    exit_im = probe_re * patch_im + probe_im * patch_re
    far_re, far_im = transform(exit_re, exit_im, fourier_real, fourier_imaginary)
    modulus = jnp.sqrt(far_re * far_re + far_im * far_im)
    factor = (1.0 - measured_patterns / jnp.maximum(modulus, amp_floor)) * misfit_weight[
        :, None, None
    ]
    back_re, back_im = transform(far_re * factor, far_im * factor, fourier_real, -fourier_imaginary)
    return jnp.stack(
        [probe_re * back_re + probe_im * back_im, probe_re * back_im - probe_im * back_re], axis=1
    )


def transmit(phase_in, absorb_in):
    damping = jnp.exp(-absorb_in)
    return (damping * jnp.cos(phase_in), damping * jnp.sin(phase_in))


def chain_back(trans_re, trans_im, grad_re, grad_im):
    return (trans_re * grad_im - trans_im * grad_re, -(trans_re * grad_re + trans_im * grad_im))


def assemble(windows, columns, margin):
    leading = windows.shape[:2]
    groups = windows.shape[2]
    centre = windows[..., margin : margin + columns]
    from_left = jnp.roll(windows[..., columns + margin :], 1, axis=2)
    from_right = jnp.roll(windows[..., :margin], -1, axis=2)
    pad_spec_left = ((0, 0), (0, 0), (0, 0), (0, columns - margin))
    pad_spec_right = ((0, 0), (0, 0), (0, 0), (columns - margin, 0))
    result = centre + jnp.pad(from_left, pad_spec_left) + jnp.pad(from_right, pad_spec_right)
    return result.reshape(leading + (groups * columns,))


def cut_windows(gradient, columns, margin):
    leading = gradient.shape[:2]
    groups = gradient.shape[2] // columns
    blocks = gradient.reshape(leading + (groups, columns))
    left_part = jnp.roll(blocks[..., columns - margin :], 1, axis=2)
    right_part = jnp.roll(blocks[..., :margin], -1, axis=2)
    return jnp.concatenate([left_part, blocks, right_part], -1)


def run_scans(
    trans_tile,
    illumination_field,
    measured_patterns,
    spot_list,
    active_count,
    fourier_real,
    fourier_imaginary,
):

    def one_batch(batch_idx, carry_in):
        grad_trans, grad_carried = carry_in
        leading_slot = batch_idx * scan_group_batch
        row_start = spot_list[:, 0]
        col_start = spot_list[:, 1]
        misfit_weight = (
            leading_slot + jnp.arange(scan_group_batch, dtype=jnp.int32) < active_count
        ).astype(jnp.float32)
        object_patches = jax.vmap(
            lambda r_pos, c_pos: lax.dynamic_slice(
                trans_tile, (0, r_pos, c_pos), (2, PATTERN_PIXELS, PATTERN_PIXELS)
            )
        )(row_start, col_start)
        patch_gradient = scan_gradients(
            object_patches,
            illumination_field,
            measured_patterns,
            misfit_weight,
            fourier_real,
            fourier_imaginary,
        )
        for slot_idx in range(scan_group_batch):
            anchor = (0, row_start[slot_idx], col_start[slot_idx])
            current = lax.dynamic_slice(grad_trans, anchor, (2, PATTERN_PIXELS, PATTERN_PIXELS))
            grad_trans = lax.dynamic_update_slice(
                grad_trans, current + patch_gradient[slot_idx], anchor
            )
        return (grad_trans, grad_carried)

    rounds = (active_count + scan_group_batch - 1) // scan_group_batch
    spare = jnp.zeros((1,), jnp.float32)
    return lax.fori_loop(0, rounds, one_batch, (jnp.zeros_like(trans_tile), spare))


def on_device(
    delta_obj, beta_obj, layer_shifts, illumination_field, amplitudes, positions, scan_counts
):
    tile_rows, layers, columns = delta_obj.shape
    window_len = columns + 2 * SHIFT
    fourier_real, fourier_imaginary = dft_tables()
    stacked = jnp.stack([delta_obj, beta_obj])
    padded = jnp.pad(stacked, ((0, 0), (0, 0), (0, 0), (2 * SHIFT, 2 * SHIFT)))

    def one_layer(layer_idx):
        layer_slab = padded[:, :, layer_idx, :]
        return jax.vmap(
            lambda offset: lax.dynamic_slice_in_dim(layer_slab, SHIFT + offset, window_len, 2),
            out_axes=2,
        )(layer_shifts[:, layer_idx])

    windows = one_layer(0)
    layer_idx = 1
    windows = windows + one_layer(layer_idx)
    incoming = lax.all_to_all(
        windows.astype(jnp.bfloat16), "ang", split_axis=2, concat_axis=2, tiled=True
    )
    projection = assemble(incoming.astype(jnp.float32), columns, SHIFT)
    measured_patterns = amplitudes[0]
    spot_list = positions[0]
    active_count = scan_counts[0, 0]
    below = from_behind(projection[:, :PATTERN_PIXELS, :], "rows", -1)
    extended = jnp.concatenate([projection, below], 1)
    trans_re, trans_im = transmit(extended[0], extended[1])
    grad_trans = run_scans(
        jnp.stack([trans_re, trans_im]),
        illumination_field,
        measured_patterns,
        spot_list,
        active_count,
        fourier_real,
        fourier_imaginary,
    )[0]
    grad_phase, grad_absorb = chain_back(trans_re, trans_im, grad_trans[0], grad_trans[1])
    grad_ext = jnp.stack([grad_phase, grad_absorb])
    returned = from_behind(grad_ext[:, tile_rows:, :], "rows", 1)
    grad_proj = grad_ext[:, :tile_rows].at[:, :PATTERN_PIXELS].add(returned)
    outgoing = cut_windows(grad_proj, columns, SHIFT).astype(jnp.bfloat16)
    grad_win = lax.all_to_all(outgoing, "ang", split_axis=2, concat_axis=2, tiled=True).astype(
        jnp.float32
    )

    def layer_grad(shift_col):
        parts = jax.vmap(
            lambda win_part, offset: lax.dynamic_slice_in_dim(win_part, SHIFT - offset, columns, 2),
            in_axes=(2, 0),
        )(grad_win, shift_col)
        return jnp.sum(parts, 0)

    per_layer = lax.map(layer_grad, layer_shifts.T)
    grad_obj = jnp.transpose(per_layer, (1, 2, 0, 3))
    return (grad_obj[0], grad_obj[1])


def solution(mesh):
    placed = (
        P("rows", None, "ang"),
        P("rows", None, "ang"),
        P(),
        P(),
        P("ang", "rows", None, None),
        P("ang", "rows", None),
        P("ang", "rows"),
    )
    return jax.shard_map(
        on_device,
        mesh=mesh,
        in_specs=placed,
        out_specs=(P("rows", None, "ang"), P("rows", None, "ang")),
        check_vma=False,
    )
```

profile of v0, /device:TPU:2, one launch (start us, length us, event | category | flops | bytes accessed | tf_op | source)
XLA Modules:
  0.0 136.7 jit_solution(18264381900652303163)
XLA Ops:
  3.6 1.8 %gather_fusion.1 = f32[4,2,136,144]{2,1,3,0:T(2,128)S(1)} fusion(f32[2,136,160]{1,0,2:T(2,128)S(1)} %get-tuple-element.743, s32[4]{0:T(128)S(1)} %get-tuple-element.767), kind=kCustom, calls=%fused_computation.1 | custom fusion | bytes 1253424 | tf_op jit(solution)/shard_map/vmap()/gather | solution.py:158
  5.4 1.8 %gather_fusion.2 = f32[4,2,136,144]{2,1,3,0:T(2,128)S(1)} fusion(f32[2,136,160]{1,0,2:T(2,128)S(1)} %get-tuple-element.742, s32[4]{0:T(128)S(1)} %get-tuple-element.766), kind=kCustom, calls=%fused_computation.2 | custom fusion | bytes 1253424 | tf_op jit(solution)/shard_map/vmap()/gather | solution.py:158
  9.1 4.9 %all-to-all-start = ((bf16[2,136,4,144]{3,1,0,2:T(8,128)(2,1)}), bf16[2,136,4,144]{3,1,0,2:T(8,128)(2,1)S(1)}, u32[]{:S(2)}, u32[]{:S(2)}) async-start(bf16[2,136,4,144]{3,1,0,2:T(8,128)(2,1)} %copy.199), calls=%async_computation | async-start | bytes 1114112 | tf_op jit(solution)/shard_map/all_to_all | solution.py:165
  14.7 14.5 %all-to-all-done = bf16[2,136,4,144]{3,1,0,2:T(8,128)(2,1)S(1)} async-done(((bf16[2,136,4,144]{3,1,0,2:T(8,128)(2,1)}), bf16[2,136,4,144]{3,1,0,2:T(8,128)(2,1)S(1)}, u32[]{:S(2)}, u32[]{:S(2)}) %all-to-all-start) | async-done | bytes 313376 | tf_op jit(solution)/shard_map/all_to_all | solution.py:165
  30.7 1.9 %collective-permute-start = (f32[2,128,512]{2,1,0:T(8,128)}, f32[2,128,512]{2,1,0:T(8,128)}, u32[]{:S(2)}, u32[]{:S(2)}) collective-permute-start(f32[2,128,512]{2,1,0:T(8,128)} %slice.333), channel_id=1, source_target_pairs={{4,0},{8,4},{12,8},{16,12},{20,16},{24,20},{28,24},{5,1},{9,5},{13... | collective-permute-start | bytes 1572872 | tf_op jit(solution)/shard_map/ppermute | solution.py:20
  49.5 2.0 %cosine_multiply_fusion.9 = (f32[1,264,512]{2,1,0:T(8,128)S(1)}, f32[1,264,512]{2,1,0:T(8,128)S(1)}) fusion(f32[2,264,512]{2,1,0:T(8,128)S(1)} %constant_dynamic-update-slice_fusion), kind=kLoop, calls=%fused_computation.179 | loop fusion | flops 405504 | bytes 2162688 | tf_op jit(solution)/shard_map/mul | solution.py:74
  52.6 7.7 %while.30 = (s32[]{:T(128)}, f32[2,264,512]{2,1,0:T(8,128)S(1)}, s32[4,3]{1,0:T(4,128)S(1)}, f32[4,2,128,128]{3,2,1,0:T(8,128)S(1)}, s32[]{:T(128)}) while((s32[]{:T(128)}, f32[2,264,512]{2,1,0:T(8,128)S(1)}, s32[4,3]{1,0:T(4,128)S(1)}, f32[4,2,128,128]{3,2,1,0:T(8,128)S(1)}, s32[]{:T(128)}) %tuple.121), condition=%wide.while_cond.1, body=%wide.while_body.1.sunk | while | flops 2 | bytes 262261 | solution.py:121
  62.6 1.4 %fusion.136 = f32[4,128,128]{2,1,0:T(8,128)} fusion(f32[4,128,128]{1,2,0:T(8,128)S(1)} %fusion.118), kind=kOutput, calls=%fused_computation.201 | convolution fusion | flops 100925440 | bytes 524288 | tf_op jit(solution)/shard_map/while/body/dot_general | solution.py:41
  65.6 21.6 %while.31 = (s32[]{:T(128)}, f32[2,264,512]{2,1,0:T(8,128)S(1)}, s32[]{:T(128)}, s32[]{:T(128)}, s32[]{:T(128)}, /*index=5*/f32[2,128,128]{2,1,0:T(8,128)S(1)}, ...) while((s32[]{:T(128)}, f32[2,264,512]{2,1,0:T(8,128)S(1)}, ...), condition=%wide.region_1.2_spmd.clone.clone, body=%wide.region_0.1_spmd.clone.clone.sunk | while | flops 1213333504 | bytes 16122153 | solution.py:143
  68.8 1.8 %subtract_multiply_fusion.2 = (f32[4,128,128]{2,1,0:T(8,128)S(1)}, f32[4,128,128]{2,1,0:T(8,128)S(1)}) fusion(f32[4,128,128]{2,1,0:T(8,128)} %get-tuple-element.1020, f32[4,128,128]{2,1,0:T(8,128)S(1)} %convolution_subtract_fusion.6, f32[4]{0:T(128)S(1)} %compare_convert_fusion.2, f32[4,128,128]{2,1,0:T(8,128)} %get-tuple-element.1019, ...), kind=kOutput, calls=%fused_computation.36.clone.1 | convolution fusion | flops 101433344 | bytes 1572880 | tf_op jit(solution)/shard_map/while/body/dot_general | solution.py:41
  76.7 2.5 %dynamic_update_slice.45 = f32[2,264,512]{2,1,0:T(8,128)S(1)} dynamic-update-slice(f32[2,264,512]{2,1,0:T(8,128)S(1)} %get-tuple-element.988, f32[2,128,128]{2,1,0:T(8,128)S(1)} %fusion.277, s32[]{:T(128)} %constant.143.clone.1..sunk.1, s32[]{:T(128)} %get-tuple-element.1012, s32[]{:T(128)} %get-tuple-element.1013) | dynamic-update-slice | bytes 262148 | tf_op jit(solution)/shard_map/while/body/dynamic_update_slice | solution.py:136
  79.3 2.5 %dynamic_update_slice.46 = f32[2,264,512]{2,1,0:T(8,128)S(1)} dynamic-update-slice(f32[2,264,512]{2,1,0:T(8,128)S(1)} %dynamic_update_slice.45, f32[2,128,128]{2,1,0:T(8,128)S(1)} %fusion.278, s32[]{:T(128)} %constant.143.clone.1..sunk.1, s32[]{:T(128)} %get-tuple-element.1022, s32[]{:T(128)} %get-tuple-element.1023) | dynamic-update-slice | bytes 262148 | tf_op jit(solution)/shard_map/while/body/dynamic_update_slice | solution.py:136
  81.9 2.5 %dynamic_update_slice.47 = f32[2,264,512]{2,1,0:T(8,128)S(1)} dynamic-update-slice(f32[2,264,512]{2,1,0:T(8,128)S(1)} %dynamic_update_slice.46, f32[2,128,128]{2,1,0:T(8,128)S(1)} %fusion.279, s32[]{:T(128)} %constant.143.clone.1..sunk.1, s32[]{:T(128)} %get-tuple-element.1024, s32[]{:T(128)} %get-tuple-element.1025) | dynamic-update-slice | bytes 262148 | tf_op jit(solution)/shard_map/while/body/dynamic_update_slice | solution.py:136
  84.5 2.5 %dynamic_update_slice.48 = f32[2,264,512]{2,1,0:T(8,128)S(1)} dynamic-update-slice(f32[2,264,512]{2,1,0:T(8,128)S(1)} %dynamic_update_slice.47, f32[2,128,128]{2,1,0:T(8,128)S(1)} %fusion.280, s32[]{:T(128)} %constant.143.clone.1..sunk.1, s32[]{:T(128)} %get-tuple-element.1026, s32[]{:T(128)} %get-tuple-element.1027) | dynamic-update-slice | bytes 262148 | tf_op jit(solution)/shard_map/while/body/dynamic_update_slice | solution.py:136
  87.3 1.5 %add_negate_fusion = (f32[1,264,512]{2,1,0:T(8,128)S(1)}, f32[1,264,512]{2,1,0:T(8,128)S(1)}) fusion(f32[1,264,512]{2,1,0:T(8,128)} %copy-done.1, f32[1,264,512]{2,1,0:T(8,128)} %copy-done, f32[2,264,512]{2,1,0:T(8,128)S(1)} %get-tuple-element.412), kind=kLoop, calls=%fused_computation.176 | loop fusion | flops 946176 | bytes 3244032 | tf_op jit(solution)/shard_map/neg | solution.py:78
  88.8 2.3 %collective-permute-start.1 = (f32[2,128,512]{2,1,0:T(8,128)S(1)}, f32[2,128,512]{2,1,0:T(8,128)S(1)}, u32[]{:S(2)}, u32[]{:S(2)}) collective-permute-start(f32[2,128,512]{2,1,0:T(8,128)S(1)} %pad_maximum_fusion.2), channel_id=1, source_target_pairs={{0,4},{4,8},{8,12},{12,16},{16,20},{20,24},{24,28},{1,5},{5,9},{9,... | collective-permute-start | bytes 1572872 | tf_op jit(solution)/shard_map/ppermute | solution.py:20
  91.1 8.2 %collective-permute-done.1 = f32[2,128,512]{2,1,0:T(8,128)S(1)} collective-permute-done((f32[2,128,512]{2,1,0:T(8,128)S(1)}, f32[2,128,512]{2,1,0:T(8,128)S(1)}, u32[]{:S(2)}, u32[]{:S(2)}) %collective-permute-start.1) | collective-permute-done | bytes 524320 | tf_op jit(solution)/shard_map/ppermute | solution.py:20
  102.3 3.5 %all-to-all-start.1 = ((bf16[2,136,4,144]{3,1,0,2:T(8,128)(2,1)}), bf16[2,136,4,144]{3,1,0,2:T(8,128)(2,1)S(1)}, u32[]{:S(2)}, u32[]{:S(2)}) async-start(bf16[2,136,4,144]{3,1,0,2:T(8,128)(2,1)} %copy.210), calls=%async_computation.1 | async-start | bytes 1114112 | tf_op jit(solution)/shard_map/all_to_all | solution.py:189
  105.8 14.7 %all-to-all-done.1 = bf16[2,136,4,144]{3,1,0,2:T(8,128)(2,1)S(1)} async-done(((bf16[2,136,4,144]{3,1,0,2:T(8,128)(2,1)}), bf16[2,136,4,144]{3,1,0,2:T(8,128)(2,1)S(1)}, u32[]{:S(2)}, u32[]{:S(2)}) %all-to-all-start.1) | async-done | bytes 313376 | tf_op jit(solution)/shard_map/all_to_all | solution.py:189
  121.2 14.8 %while.29 = (s32[]{:T(128)}, f32[2,2,136,128]{3,0,2,1:T(2,128)S(1)}, f32[2,136,4,144]{1,0,2,3:T(2,128)S(1)}, s32[2,4]{1,0:T(2,128)S(1)}, s32[]{:T(128)}, /*index=5*/f32[]{:T(128)}, s32[]{:T(128)}) while((s32[]{:T(128)}, f32[2,2,136,128]{3,0,2,1:T(2,128)S(1)}, f32[2,136,4,144]{1,0,2,3:T(2,128)S(1)}, s32[2,4]{1,0:T(2,128)S(1)}, s32[]{:T(128)}, ...), condition=%wide.region_4.5_spmd, body=%wide.region_2.4_spmd.sunk | while | flops 104486 | bytes 2367673 | solution.py:200
  121.2 1.8 %gather_fusion = f32[4,2,136,128]{2,1,3,0:T(2,128)S(1)} fusion(f32[4,2,136,144]{2,1,0,3:T(2,128)S(1)} %bitcast.272, s32[4]{0:T(128)S(1)} %or_bitcast_fusion.2), kind=kCustom, calls=%fused_computation.clone.1 | custom fusion | bytes 1114176 | tf_op jit(solution)/shard_map/while/body/eval_jaxpr/vmap()/gather | solution.py:195
  123.8 4.7 %dynamic_update_slice.44 = f32[2,2,136,128]{3,0,2,1:T(2,128)S(1)} dynamic-update-slice(f32[2,2,136,128]{3,0,2,1:T(2,128)S(1)} %get-tuple-element.1039, f32[1,2,136,128]{3,0,2,1:T(1,128)S(1)} %copy.260, s32[]{:T(128)} %get-tuple-element.1038, s32[]{:T(128)} %constant.143.clone.1..sunk, s32[]{:T(128)} %constant.143.clone.1..sunk, s32[]{:T(128)} %constant.143.clone.1..sunk) | dynamic-update-slice | bytes 278532 | tf_op jit(solution)/shard_map/while/body/jit(dynamic_update_index_in_dim)/dynamic_update_slice | solution.py:200
  128.6 1.8 %gather_fusion = f32[4,2,136,128]{2,1,3,0:T(2,128)S(1)} fusion(f32[4,2,136,144]{2,1,0,3:T(2,128)S(1)} %bitcast.272, s32[4]{0:T(128)S(1)} %or_bitcast_fusion.2), kind=kCustom, calls=%fused_computation.clone.1 | custom fusion | bytes 1114176 | tf_op jit(solution)/shard_map/while/body/eval_jaxpr/vmap()/gather | solution.py:195
  131.2 4.7 %dynamic_update_slice.44 = f32[2,2,136,128]{3,0,2,1:T(2,128)S(1)} dynamic-update-slice(f32[2,2,136,128]{3,0,2,1:T(2,128)S(1)} %get-tuple-element.1039, f32[1,2,136,128]{3,0,2,1:T(1,128)S(1)} %copy.260, s32[]{:T(128)} %get-tuple-element.1038, s32[]{:T(128)} %constant.143.clone.1..sunk, s32[]{:T(128)} %constant.143.clone.1..sunk, s32[]{:T(128)} %constant.143.clone.1..sunk) | dynamic-update-slice | bytes 278532 | tf_op jit(solution)/shard_map/while/body/jit(dynamic_update_index_in_dim)/dynamic_update_slice | solution.py:200
  (86 shorter events, 36.4 us)
Async XLA Ops:
  2.8 0.8 copy-start.4
  7.9 6.1 %copy-start.3 = (s32[1,4,2]{1,2,0:T(2,128)S(1)}, s32[1,4,2]{1,2,0:T(2,128)}, u32[]{:S(2)}) copy-start(s32[1,4,2]{1,2,0:T(2,128)} %param.18) | copy-start | bytes 100
  9.1 20.1 %all-to-all-start = ((bf16[2,136,4,144]{3,1,0,2:T(8,128)(2,1)}), bf16[2,136,4,144]{3,1,0,2:T(8,128)(2,1)S(1)}, u32[]{:S(2)}, u32[]{:S(2)}) async-start(bf16[2,136,4,144]{3,1,0,2:T(8,128)(2,1)} %copy.199), calls=%async_computation | async-start | bytes 1114112 | tf_op jit(solution)/shard_map/all_to_all | solution.py:165
  29.9 18.2 %copy-start.2 = (f32[2,128,128]{2,1,0:T(8,128)S(1)}, f32[2,128,128]{2,1,0:T(8,128)}, u32[]{:S(2)}) copy-start(f32[2,128,128]{2,1,0:T(8,128)} %param.16) | copy-start | bytes 393220
  30.7 17.7 %collective-permute-start = (f32[2,128,512]{2,1,0:T(8,128)}, f32[2,128,512]{2,1,0:T(8,128)}, u32[]{:S(2)}, u32[]{:S(2)}) collective-permute-start(f32[2,128,512]{2,1,0:T(8,128)} %slice.333), channel_id=1, source_target_pairs={{4,0},{8,4},{12,8},{16,12},{20,16},{24,20},{28,24},{5,1},{9,5},{13... | collective-permute-start | bytes 1572872 | tf_op jit(solution)/shard_map/ppermute | solution.py:20
  51.6 0.8 copy-start
  51.6 1.0 copy-start.1
  88.8 10.5 %collective-permute-start.1 = (f32[2,128,512]{2,1,0:T(8,128)S(1)}, f32[2,128,512]{2,1,0:T(8,128)S(1)}, u32[]{:S(2)}, u32[]{:S(2)}) collective-permute-start(f32[2,128,512]{2,1,0:T(8,128)S(1)} %pad_maximum_fusion.2), channel_id=1, source_target_pairs={{0,4},{4,8},{8,12},{12,16},{16,20},{20,24},{24,28},{1,5},{5,9},{9,... | collective-permute-start | bytes 1572872 | tf_op jit(solution)/shard_map/ppermute | solution.py:20
  102.3 18.2 %all-to-all-start.1 = ((bf16[2,136,4,144]{3,1,0,2:T(8,128)(2,1)}), bf16[2,136,4,144]{3,1,0,2:T(8,128)(2,1)S(1)}, u32[]{:S(2)}, u32[]{:S(2)}) async-start(bf16[2,136,4,144]{3,1,0,2:T(8,128)(2,1)} %copy.210), calls=%async_computation.1 | async-start | bytes 1114112 | tf_op jit(solution)/shard_map/all_to_all | solution.py:189
where the time goes:
time: 137 us
  local copies, waits for them, and re-layouts  45.1 us (33%)
  waiting for transfers between devices  37.4 us (27%)
  between operations  16.3 us (12%)
  matrix products  15.1 us (11%)
  starting transfers between devices  12.5 us (9%)
  other arithmetic  9.52 us (7%)
    all_to_all x1, waiting for transfers between devices, on_device(): lax.all_to_all(outgoing, 'ang', split_axis=2, concat_axis=2, tiled=True)  14.7 us
    all_to_all x1, waiting for transfers between devices, on_device(): lax.all_to_all(windows.astype(jnp.bfloat16), 'ang', split_axis=2, concat_...  14.5 us
    dynamic_update_slice x4, local copies, waits for them, and re-layouts, one_batch(): lax.dynamic_update_slice(grad_trans, current + patch_gradient[slot_idx],...  9.99 us
    dynamic_update_slice x4, local copies, waits for them, and re-layouts, on_device(): per_layer = lax.map(layer_grad, layer_shifts.T)  9.7 us
    ppermute x2, waiting for transfers between devices, from_behind(): lax.ppermute(value, axis, [(source, source + steps) for source in range(i...  8.19 us
    gather x12, local copies, waits for them, and re-layouts  7.56 us
    all_to_all x1, starting transfers between devices, on_device(): lax.all_to_all(windows.astype(jnp.bfloat16), 'ang', split_axis=2, concat_...  4.87 us
    ppermute x2, starting transfers between devices, from_behind(): lax.ppermute(value, axis, [(source, source + steps) for source in range(i...  4.18 us
  transfers between devices with their start and end apart: 4, of which 3 were waited for; matrix products, arithmetic and copies ran while one was open for 1% of the time, Pallas kernels for 0%

commit v1 on v0

v1 whole, which is shorter than its diff:
```python
import functools
import math

import jax
import jax.numpy as jnp
import ml_dtypes
import numpy as np
from jax import lax
from jax.experimental import pallas as pl
from jax.experimental.pallas import tpu as pltpu
from jax.sharding import PartitionSpec as P

N = 128
SHIFT = 8
AMP_FLOOR = 0.1
PACK_ROWS = 48
EDGE_ROWS = 8

f32, bf16, i32 = jnp.float32, jnp.bfloat16, jnp.int32
SMEM = pl.BlockSpec(memory_space=pltpu.SMEM)
VMEM = pl.BlockSpec(memory_space=pltpu.VMEM)


def fourier_tables():
    counter = np.arange(N)
    angle = (counter[:, None] * counter[None, :] % N) * (2.0 * math.pi / N)
    re, im = np.cos(angle) / math.sqrt(N), -np.sin(angle) / math.sqrt(N)
    right = np.block([[re, im], [-im, re]])
    tables = []
    for table in (right, right.T):
        high = table.astype(ml_dtypes.bfloat16)
        tables += [high, (table - high.astype(np.float64)).astype(ml_dtypes.bfloat16)]
    return np.stack(tables)


def lane_iota(rows):
    return lax.broadcasted_iota(i32, (rows, N), 1)


def roll_lanes(value, by):
    return pltpu.roll(value, by, 1)


def roll_left(value, by):
    return pltpu.roll(value, lax.rem(N - by, N), 1)


def groups_of(rows):
    return [(g, start, min(PACK_ROWS, rows - start)) for g, start in enumerate(range(0, rows, PACK_ROWS))]


def packed_message(main, margins, scratch):
    rows = main.shape[0]
    scratch[0:rows, :] = margins
    packed = None
    for g, start, _ in groups_of(rows):
        part = scratch[start : start + PACK_ROWS, :]
        part = roll_lanes(part, 16 * g) if g else part
        packed = part if packed is None else packed + part
    return jnp.concatenate([main, packed], 0).astype(bf16)


def margins_of(message, rows):
    packed = message[rows:, :]
    parts = []
    for g, _, size in groups_of(rows):
        part = roll_lanes(packed, N - 16 * g) if g else packed
        parts.append(part[:size])
    return jnp.concatenate(parts, 0)


def window_kernel(shifts, delta, beta, *refs):
    outs, scratch = refs[:-1], refs[-1]
    angles = len(outs)
    tile = delta.shape[0] // 2
    scratch[2 * tile :, :] = jnp.zeros((scratch.shape[0] - 2 * tile, N), f32)
    me = lax.axis_index("ang")
    lane = lane_iota(tile)
    for d, out in enumerate(outs):
        angle = lax.rem(me + d, angles)
        mains, margins = [], []
        for ref in (delta, beta):
            main = margin = None
            for z in range(2):
                s = shifts[angle, z]
                rolled = pltpu.roll(ref[pl.ds(z, tile, stride=2), :], lax.rem(N - s, N), 1)
                source = lane + s
                inside = (source >= 0) & (source < N)
                kept, out_of = jnp.where(inside, rolled, 0.0), jnp.where(inside, 0.0, rolled)
                main = kept if z == 0 else main + kept
                margin = out_of if z == 0 else margin + out_of
            mains.append(main)
            margins.append(margin)
        out[...] = packed_message(jnp.concatenate(mains, 0), jnp.concatenate(margins, 0), scratch)


def assemble_kernel(previous, *refs):
    proj, halo, margins = refs[-3:]
    received = refs[:-3]
    blocks = len(received)
    tile = proj.shape[2]
    me = lax.axis_index("ang")
    for d, ref in enumerate(received):
        block = lax.rem(me + (blocks - d), blocks)
        message = ref[...].astype(f32)
        proj[0, block] = message[:tile]
        proj[1, block] = message[tile : 2 * tile]
        margins[block] = margins_of(message, 2 * tile)
    lane = lane_iota(tile)
    for block in range(blocks):
        before, after = (block - 1) % blocks, (block + 1) % blocks
        for c in range(2):
            part = slice(c * tile, (c + 1) * tile)
            extra = jnp.where(lane < SHIFT, margins[before, part], 0.0)
            extra += jnp.where(lane >= N - SHIFT, margins[after, part], 0.0)
            proj[c, block] += extra
    column = previous[0, 1]
    first, offset = column // N, lax.rem(column, N)
    second = jnp.minimum(first + 1, blocks - 1)
    lane = lane_iota(N)
    for c in range(2):
        left = roll_left(proj[c, first, 0:N, :], offset)
        right = roll_left(proj[c, second, 0:N, :], offset)
        halo[c * N : (c + 1) * N, :] = jnp.where(lane < N - offset, left, right).astype(bf16)


def transmit(phase, absorb):
    turns = jnp.round(phase * (2.0 / math.pi))
    r = phase - turns * 1.5703125
    r = r - turns * 4.837512969970703125e-4
    r = r - turns * 7.54978995489188e-8
    z = r * r
    sine = r + r * z * (-1.6666654611e-1 + z * (8.3321608736e-3 - z * 1.9515295891e-4))
    cosine = 1.0 - 0.5 * z + z * z * (4.166664568298827e-2 + z * (-1.388731625493765e-3 + z * 2.443315711809948e-5))
    quarter = turns.astype(i32)
    odd = (quarter & 1) == 1
    damping = jnp.exp(-absorb)
    out_cos = jnp.where(odd, sine, cosine)
    out_sin = jnp.where(odd, cosine, sine)
    out_cos = jnp.where(((quarter + 1) & 2) == 2, -out_cos, out_cos)
    out_sin = jnp.where((quarter & 2) == 2, -out_sin, out_sin)
    return damping * out_cos, damping * out_sin


def split(value):
    high = value.astype(bf16)
    return high, (value - high.astype(f32)).astype(bf16)


def dot(a, b):
    return jnp.dot(a, b, preferred_element_type=f32)


def times_right(value, high, low):
    vh, vl = split(value)
    return dot(vh, high) + (dot(vl, high) + dot(vh, low))


def times_left(high, low, value):
    vh, vl = split(value)
    return dot(high, vh) + (dot(high, vl) + dot(low, vh))


def scan_gradients(patches, measured, weights, probe, tables):
    probe_re, probe_im = probe[0], probe[1]
    right_high, right_low, left_high, left_low = (tables[t] for t in range(4))
    rows = [
        jnp.concatenate([probe_re * re - probe_im * im, probe_re * im + probe_im * re], 1)
        for re, im in patches
    ]
    half = times_right(jnp.concatenate(rows, 0), right_high, right_low)
    count = len(patches)
    stacked = jnp.concatenate(
        [
            jnp.concatenate([half[j * N : (j + 1) * N, part * N : (part + 1) * N] for j in range(count)], 1)
            for part in range(2)
        ],
        0,
    )
    far = times_left(left_high, left_low, stacked)
    far_re, far_im = far[:N], far[N:]
    squared = far_re * far_re + far_im * far_im
    inverse = lax.rsqrt(jnp.maximum(squared, AMP_FLOOR * AMP_FLOOR))
    amplitude = jnp.concatenate([m for m in measured], 1)
    factor = 1.0 - amplitude * inverse
    factor = jnp.concatenate(
        [factor[:, j * N : (j + 1) * N] * weights[j] for j in range(count)], 1
    )
    residual = jnp.concatenate([far_re * factor, far_im * factor], 0)
    half = times_left(right_high, right_low, residual)
    rows = [
        jnp.concatenate([half[:N, j * N : (j + 1) * N], half[N:, j * N : (j + 1) * N]], 1)
        for j in range(count)
    ]
    back = times_right(jnp.concatenate(rows, 0), left_high, left_low)
    grads = []
    for j in range(count):
        re, im = back[j * N : (j + 1) * N, :N], back[j * N : (j + 1) * N, N:]
        grads.append((probe_re * re + probe_im * im, probe_re * im - probe_im * re))
    return grads


def column_of(spots, slot, blocks):
    column = spots[slot, 1]
    first, offset = column // N, lax.rem(column, N)
    return first, jnp.minimum(first + 1, blocks - 1), offset


def inner_kernel(spots, counts, proj, probe, measured, tables, trans, grad, frame):
    blocks, tile = proj.shape[1], proj.shape[2]
    for block in range(blocks):
        re, im = transmit(proj[0, block], proj[1, block])
        trans[0, block] = re
        trans[1, block] = im
    grad[...] = jnp.zeros(grad.shape, f32)
    frame[0:SHIFT, :] = jnp.zeros((SHIFT, N), f32)
    frame[SHIFT + N :, :] = jnp.zeros((SHIFT, N), f32)
    slots = measured.shape[0]
    lane = lane_iota(N)
    patches, weights = [], []
    for slot in range(1, slots):
        row = jnp.minimum(spots[slot, 0], EDGE_ROWS)
        first, second, offset = column_of(spots, slot, blocks)
        pair = []
        for c in range(2):
            left = roll_left(trans[c, first, pl.ds(row, N), :], offset)
            right = roll_left(trans[c, second, pl.ds(row, N), :], offset)
            pair.append(jnp.where(lane < N - offset, left, right))
        patches.append(pair)
        weights.append(jnp.where(slot < counts[0, 0], 1.0, 0.0).astype(f32))
    grads = scan_gradients(patches, [measured[slot] for slot in range(1, slots)], weights, probe, tables)
    lane = lane_iota(tile)
    for slot in range(1, slots):
        row = jnp.minimum(spots[slot, 0], EDGE_ROWS)
        first, second, offset = column_of(spots, slot, blocks)
        for c in range(2):
            frame[SHIFT : SHIFT + N, :] = grads[slot - 1][c]
            placed = roll_lanes(frame[pl.ds(SHIFT - row, tile), :], offset)
            grad[c, first] += jnp.where(lane >= offset, placed, 0.0)
            grad[c, second] += jnp.where(lane < offset, placed, 0.0)


def edge_kernel(spots, counts, halo, trans, probe, measured, tables, own, sent, patch, frame):
    blocks, tile = trans.shape[1], trans.shape[2]
    first, second, offset = column_of(spots, 0, blocks)
    row = spots[0, 0]
    last = lax.axis_index("rows") == lax.axis_size("rows") - 1
    lane = lane_iota(tile)
    for c in range(2):
        left = roll_left(trans[c, first], offset)
        right = roll_left(trans[c, second], offset)
        patch[c, 0:tile, :] = jnp.where(lane < N - offset, left, right)
    below = jnp.where(last, 0.0, halo[...].astype(f32))
    re, im = transmit(below[:N], below[N:])
    patch[0, tile:, :] = re
    patch[1, tile:, :] = im
    pair = [patch[c, pl.ds(row, N), :] for c in range(2)]
    weight = jnp.where(0 < counts[0, 0], 1.0, 0.0).astype(f32)
    grads = scan_gradients([pair], [measured[0]], [weight], probe, tables)[0]
    for c in range(2):
        frame[c, 0:tile, :] = jnp.zeros((tile, N), f32)
        frame[c, tile : tile + N, :] = grads[c]
        frame[c, tile + N :, :] = jnp.zeros((tile, N), f32)
    for c in range(2):
        own[c] = frame[c, pl.ds(tile - row, tile), :]
        sent[c * N : (c + 1) * N, :] = frame[c, pl.ds(2 * tile - row, N), :].astype(bf16)


def cut_kernel(spots, previous, trans, inner, own, above, *refs):
    outs, total, scratch = refs[:-2], refs[-2], refs[-1]
    blocks, tile = trans.shape[1], trans.shape[2]
    scratch[2 * tile :, :] = jnp.zeros((scratch.shape[0] - 2 * tile, N), f32)
    total[...] = inner[...]
    first, second, offset = column_of(spots, 0, blocks)
    lane = lane_iota(tile)
    for c in range(2):
        placed = roll_lanes(own[c], offset)
        total[c, first] += jnp.where(lane >= offset, placed, 0.0)
        total[c, second] += jnp.where(lane < offset, placed, 0.0)
    first, second, offset = column_of(previous, 0, blocks)
    top = lax.axis_index("rows") == 0
    received = jnp.where(top, 0.0, above[...].astype(f32))
    lane = lane_iota(N)
    for c in range(2):
        placed = roll_lanes(received[c * N : (c + 1) * N], offset)
        total[c, first, 0:N, :] += jnp.where(lane >= offset, placed, 0.0)
        total[c, second, 0:N, :] += jnp.where(lane < offset, placed, 0.0)
    for block in range(blocks):
        tr, ti = trans[0, block], trans[1, block]
        gr, gi = total[0, block], total[1, block]
        total[0, block] = tr * gi - ti * gr
        total[1, block] = -(tr * gr + ti * gi)
    me = lax.axis_index("ang")
    lane = lane_iota(tile)
    for d, out in enumerate(outs):
        block = lax.rem(me + d, blocks)
        before, after = lax.rem(block + (blocks - 1), blocks), lax.rem(block + 1, blocks)
        mains, margins = [], []
        for c in range(2):
            mains.append(total[c, block])
            margin = jnp.where(lane < SHIFT, total[c, after], 0.0)
            margins.append(jnp.where(lane >= N - SHIFT, total[c, before], margin))
        out[...] = packed_message(jnp.concatenate(mains, 0), jnp.concatenate(margins, 0), scratch)


def slab_kernel(shifts, *refs):
    outs, received = refs[-2:], refs[:-2]
    angles = len(received)
    tile = outs[0].shape[0] // 2
    me = lax.axis_index("ang")
    lane = lane_iota(tile)
    sums = [[None, None], [None, None]]
    for d, ref in enumerate(received):
        angle = lax.rem(me + (angles - d), angles)
        message = ref[...].astype(f32)
        margins = margins_of(message, 2 * tile)
        for z in range(2):
            s = shifts[angle, z]
            target = lane + s
            inside = (target >= 0) & (target < N)
            for c in range(2):
                part = slice(c * tile, (c + 1) * tile)
                value = jnp.where(inside, message[part], margins[part])
                value = pltpu.roll(value, lax.rem(s + N, N), 1)
                sums[c][z] = value if sums[c][z] is None else sums[c][z] + value
    for c in range(2):
        for z in range(2):
            outs[c][pl.ds(z, tile, stride=2), :] = sums[c][z]


def call(kernel, ins, outs, scratch=(), flops=0, bytes_accessed=0):
    return pl.pallas_call(
        kernel,
        in_specs=ins,
        out_specs=[VMEM] * len(outs),
        out_shape=[jax.ShapeDtypeStruct(shape, dtype) for shape, dtype in outs],
        scratch_shapes=[pltpu.VMEM(shape, f32) for shape in scratch],
        compiler_params=pltpu.CompilerParams(vmem_limit_bytes=32 * 1024 * 1024),
        cost_estimate=pl.CostEstimate(flops=flops, bytes_accessed=bytes_accessed, transcendentals=0),
    )


def exchange(messages):
    count = lax.axis_size("ang")
    received = [messages[0]]
    for d in range(1, count):
        received.append(lax.ppermute(messages[d], "ang", [(i, (i + d) % count) for i in range(count)]))
    return received


def shift_rows(value, steps):
    count = lax.axis_size("rows")
    return lax.ppermute(value, "rows", [(i, (i + steps) % count) for i in range(count)])


def on_device(delta_obj, beta_obj, layer_shifts, illumination_field, amplitudes, positions, scan_counts):
    tile = delta_obj.shape[0]
    angles = lax.axis_size("ang")
    message = ((2 * tile + PACK_ROWS, N), bf16)
    padded = len(groups_of(2 * tile)) * PACK_ROWS
    field = ((2, angles, tile, N), f32)
    measured, spots = amplitudes[0], positions[0]
    tables = jnp.asarray(fourier_tables())
    previous = shift_rows(spots, 1)

    windows = call(window_kernel, [SMEM] + [VMEM] * 2, [message] * angles, [(padded, N)])(
        layer_shifts, delta_obj.reshape(2 * tile, N), beta_obj.reshape(2 * tile, N)
    )
    received = exchange(windows)
    proj, halo = call(
        assemble_kernel,
        [SMEM] + [VMEM] * angles,
        [field, ((2 * N, N), bf16)],
        [(angles, 2 * tile, N)],
    )(previous, *received)
    below = shift_rows(halo, -1)
    trans, inner = call(
        inner_kernel,
        [SMEM] * 2 + [VMEM] * 4,
        [field, field],
        [(N + 2 * SHIFT, N)],
        flops=3 * 10**9,
        bytes_accessed=3 * 10**6,
    )(spots, scan_counts, proj, illumination_field, measured, tables)
    own, sent = call(
        edge_kernel,
        [SMEM] * 2 + [VMEM] * 5,
        [((2, tile, N), f32), ((2 * N, N), bf16)],
        [(2, tile + N, N), (2, 2 * tile + N, N)],
    )(spots, scan_counts, below, trans, illumination_field, measured, tables)
    above = shift_rows(sent, 1)
    outgoing = call(
        cut_kernel,
        [SMEM] * 2 + [VMEM] * 4,
        [message] * angles,
        [field[0], (padded, N)],
    )(spots, previous, trans, inner, own, above)
    grad_delta, grad_beta = call(slab_kernel, [SMEM] + [VMEM] * angles, [((2 * tile, N), f32)] * 2)(
        layer_shifts, *exchange(outgoing)
    )
    return grad_delta.reshape(tile, 2, N), grad_beta.reshape(tile, 2, N)


def solution(mesh):
    placed = (
        P("rows", None, "ang"),
        P("rows", None, "ang"),
        P(),
        P(),
        P("ang", "rows", None, None),
        P("ang", "rows", None),
        P("ang", "rows"),
    )
    return jax.shard_map(
        on_device,
        mesh=mesh,
        in_specs=placed,
        out_specs=(P("rows", None, "ang"), P("rows", None, "ang")),
        check_vma=False,
    )
```

time: 137 us -> 41.2 us (0.30)
  the two profiles are of different devices: /device:TPU:2 before, /device:TPU:0 now
where the time goes in v1:
time: 41.2 us; the launch traced here: 40.9 us
  starting transfers between devices  13.2 us (32%)
  waiting for transfers between devices  11.5 us (28%)
  Pallas kernels  9.53 us (23%)
  local copies, waits for them, and re-layouts  5.26 us (13%)
  between operations  1.35 us (3%)
    ppermute x6, starting transfers between devices, exchange(): lax.ppermute(messages[d], 'ang', [(i, (i + d) % count) for i in range(cou...  11.8 us
    ppermute x3, waiting for transfers between devices, shift_rows(): lax.ppermute(value, 'rows', [(i, (i + steps) % count) for i in range(coun...  7.83 us
    unnamed x11, local copies, waits for them, and re-layouts  4.5 us
    ppermute x6, waiting for transfers between devices, exchange(): lax.ppermute(messages[d], 'ang', [(i, (i + d) % count) for i in range(cou...  3.71 us
    pallas_call x1, Pallas kernels, on_device(): call(inner_kernel, [SMEM] * 2 + [VMEM] * 4, [field, field], [(N + 2 * SHI...  2.84 us
    pallas_call x1, Pallas kernels, on_device(): call(edge_kernel, [SMEM] * 2 + [VMEM] * 5, [((2, tile, N), f32), ((2 * N,...  1.78 us
    pallas_call x1, Pallas kernels, on_device(): call(slab_kernel, [SMEM] + [VMEM] * angles, [((2 * tile, N), f32)] * 2)  1.68 us
    ppermute x3, starting transfers between devices, shift_rows(): lax.ppermute(value, 'rows', [(i, (i + steps) % count) for i in range(coun...  1.44 us
  transfers between devices with their start and end apart: 9, of which 5 were waited for; matrix products, arithmetic and copies ran while one was open for 2% of the time, Pallas kernels for 7%

profile of v1, /device:TPU:0, one launch (start us, length us, event | category | flops | bytes accessed | tf_op | source)
XLA Modules:
  0.0 40.9 jit_solution(17503178123771779113)
XLA Ops:
  0.6 0.8 %copy.15.shifts = s32[4,2]{1,0:T(4,128)S(1)} copy(s32[4,2]{0,1:T(2,128)} %param.10) | data formatting | bytes 64 | tf_op args[2]
  1.5 0.9 %copy-done.2 = f32[136,2,128]{2,1,0:T(2,128)S(1)} copy-done((f32[136,2,128]{2,1,0:T(2,128)S(1)}, f32[136,2,128]{2,1,0:T(2,128)}, u32[]{:S(2)}) %copy-start.2) | copy-done | bytes 139288
  2.4 0.9 %copy-done.3 = f32[136,2,128]{2,1,0:T(2,128)S(1)} copy-done((f32[136,2,128]{2,1,0:T(2,128)S(1)}, f32[136,2,128]{2,1,0:T(2,128)}, u32[]{:S(2)}) %copy-start.3) | copy-done | bytes 139288
  3.3 1.2 %shard_map.95 = (bf16[320,128]{1,0:T(8,128)(2,1)S(1)}, bf16[320,128]{1,0:T(8,128)(2,1)S(1)}, bf16[320,128]{1,0:T(8,128)(2,1)S(1)}, bf16[320,128]{1,0:T(8,128)(2,1)S(1)}) custom-call(s32[4,2]{1,0:T(4,128)S(1)} %copy.15.shifts, f32[272,128]{1,0:T(8,128)S(1)} %bitcast.8, f32[272,128]{1,0:T(8,128)S(1)} %bitcast.9), custom_call_target="tpu_custom_call" | custom-call | tf_op jit(solution)/shard_map/pallas_call | solution.py:366
  4.5 3.1 %collective-permute-start.1 = (bf16[320,128]{1,0:T(8,128)(2,1)S(1)}, bf16[320,128]{1,0:T(8,128)(2,1)S(1)}, u32[]{:S(2)}, u32[]{:S(2)}) collective-permute-start(bf16[320,128]{1,0:T(8,128)(2,1)S(1)} %get-tuple-element.19), channel_id=1, source_target_pairs={{0,1},{1,2},{2,3},{3,0},{4,5},{5,6},{6,7},{7,4},{8,9},{9,10},{10,1... | collective-permute-start | bytes 245768 | tf_op jit(solution)/shard_map/ppermute | solution.py:347
  7.6 2.6 %collective-permute-start.2 = (bf16[320,128]{1,0:T(8,128)(2,1)S(1)}, bf16[320,128]{1,0:T(8,128)(2,1)S(1)}, u32[]{:S(2)}, u32[]{:S(2)}) collective-permute-start(bf16[320,128]{1,0:T(8,128)(2,1)S(1)} %get-tuple-element.20), channel_id=1, source_target_pairs={{0,2},{1,3},{2,0},{3,1},{4,6},{5,7},{6,4},{7,5},{8,10},{9,11},{10,... | collective-permute-start | bytes 245768 | tf_op jit(solution)/shard_map/ppermute | solution.py:347
  10.2 1.3 %collective-permute-start.3 = (bf16[320,128]{1,0:T(8,128)(2,1)S(1)}, bf16[320,128]{1,0:T(8,128)(2,1)S(1)}, u32[]{:S(2)}, u32[]{:S(2)}) collective-permute-start(bf16[320,128]{1,0:T(8,128)(2,1)S(1)} %get-tuple-element.21), channel_id=1, source_target_pairs={{0,3},{1,0},{2,1},{3,2},{4,7},{5,4},{6,5},{7,6},{8,11},{9,8},{10,9... | collective-permute-start | bytes 245768 | tf_op jit(solution)/shard_map/ppermute | solution.py:347
  11.5 0.8 %copy.14.spots = s32[4,2]{1,0:T(4,128)S(1)} copy(s32[4,2]{0,1:T(2,128)} %bitcast.10) | data formatting | bytes 64 | tf_op jit(solution)/shard_map/squeeze | solution.py:362
  12.9 3.3 %collective-permute-done.previous = s32[4,2]{1,0:T(4,128)S(1)} collective-permute-done((s32[4,2]{1,0:T(4,128)S(1)}, s32[4,2]{1,0:T(4,128)S(1)}, u32[]{:S(2)}, u32[]{:S(2)}) %collective-permute-start) | collective-permute-done | bytes 64 | tf_op jit(solution)/shard_map/ppermute | solution.py:353
  16.2 0.9 %shard_map.96 = (f32[2,4,136,128]{3,2,1,0:T(8,128)S(1)}, bf16[256,128]{1,0:T(8,128)(2,1)S(1)}) custom-call(s32[4,2]{1,0:T(4,128)S(1)} %collective-permute-done.previous, bf16[320,128]{1,0:T(8,128)(2,1)S(1)} %get-tuple-element.18.refs_0_, bf16[320,128]{1,0:T(8,128)(2,1)S(1)} %collective-permute-done.1.refs_1_, ...), custom_call_target="tpu_custom_call" | custom-call | tf_op jit(solution)/shard_map/pallas_call | solution.py:370
  17.1 1.4 %collective-permute-start.4 = (bf16[256,128]{1,0:T(8,128)(2,1)S(1)}, bf16[256,128]{1,0:T(8,128)(2,1)S(1)}, u32[]{:S(2)}, u32[]{:S(2)}) collective-permute-start(bf16[256,128]{1,0:T(8,128)(2,1)S(1)} %get-tuple-element.25), channel_id=1, source_target_pairs={{0,28},{4,0},{8,4},{12,8},{16,12},{20,16},{24,20},{28,24},{1,29},{... | collective-permute-start | bytes 196616 | tf_op jit(solution)/shard_map/ppermute | solution.py:353
  18.5 0.9 %copy-done.1 = f32[1,4,128,128]{3,2,1,0:T(8,128)S(1)} copy-done((f32[1,4,128,128]{3,2,1,0:T(8,128)S(1)}, f32[1,4,128,128]{3,2,1,0:T(8,128)}, u32[]{:S(2)}) %copy-start.1) | copy-done | bytes 262168
  19.4 0.9 %copy-done.4 = f32[2,128,128]{2,1,0:T(8,128)S(1)} copy-done((f32[2,128,128]{2,1,0:T(8,128)S(1)}, f32[2,128,128]{2,1,0:T(8,128)}, u32[]{:S(2)}) %copy-start.4) | copy-done | bytes 131096
  20.3 2.8 %shard_map.97 = (f32[2,4,136,128]{3,2,1,0:T(8,128)S(1)}, f32[2,4,136,128]{3,2,1,0:T(8,128)S(1)}) custom-call(s32[4,2]{1,0:T(4,128)S(1)} %copy.14.spots, s32[1,1]{1,0:T(1,128)S(6)} %copy.16.counts, f32[2,4,136,128]{3,2,1,0:T(8,128)S(1)} %get-tuple-element.22.proj, f32[2,128,128]{2,1,0:T(8,128)S(1)} %copy-done.4, f32[4,128,128]{2,1,0:T(8,128)S(1)} %bitcast.6, ...), custom_call_target="tpu_custom_call" | custom-call | flops 3000000000 | bytes 3000000 | tf_op jit(solution)/shard_map/pallas_call | solution.py:377
  23.2 1.8 %shard_map.98 = (f32[2,136,128]{2,1,0:T(8,128)S(1)}, bf16[256,128]{1,0:T(8,128)(2,1)S(1)}) custom-call(s32[4,2]{1,0:T(4,128)S(1)} %copy.14.spots, s32[1,1]{1,0:T(1,128)S(6)} %copy.16.counts, bf16[256,128]{1,0:T(8,128)(2,1)S(1)} %collective-permute-done.4.halo, f32[2,4,136,128]{3,2,1,0:T(8,128)S(1)} %get-tuple-element.23.trans, f32[2,128,128]{2,1,0:T(8,128)S(1)} %copy-done.4, ...), custom_call_target="tpu_custom_call" | custom-call | tf_op jit(solution)/shard_map/pallas_call | solution.py:385
  25.0 4.6 %collective-permute-done.5.above = bf16[256,128]{1,0:T(8,128)(2,1)S(1)} collective-permute-done((bf16[256,128]{1,0:T(8,128)(2,1)S(1)}, bf16[256,128]{1,0:T(8,128)(2,1)S(1)}, u32[]{:S(2)}, u32[]{:S(2)}) %collective-permute-start.5) | collective-permute-done | bytes 65568 | tf_op jit(solution)/shard_map/ppermute | solution.py:353
  29.6 1.1 %shard_map.99 = (bf16[320,128]{1,0:T(8,128)(2,1)S(1)}, bf16[320,128]{1,0:T(8,128)(2,1)S(1)}, bf16[320,128]{1,0:T(8,128)(2,1)S(1)}, bf16[320,128]{1,0:T(8,128)(2,1)S(1)}) custom-call(s32[4,2]{1,0:T(4,128)S(1)} %copy.14.spots, s32[4,2]{1,0:T(4,128)S(1)} %collective-permute-done.previous, f32[2,4,136,128]{3,2,1,0:T(8,128)S(1)} %get-tuple-element.23.trans, ...), custom_call_target="tpu_custom_call" | custom-call | tf_op jit(solution)/shard_map/pallas_call | solution.py:392
  30.7 2.4 %collective-permute-start.6 = (bf16[320,128]{1,0:T(8,128)(2,1)S(1)}, bf16[320,128]{1,0:T(8,128)(2,1)S(1)}, u32[]{:S(2)}, u32[]{:S(2)}) collective-permute-start(bf16[320,128]{1,0:T(8,128)(2,1)S(1)} %get-tuple-element.29), channel_id=1, source_target_pairs={{0,1},{1,2},{2,3},{3,0},{4,5},{5,6},{6,7},{7,4},{8,9},{9,10},{10,1... | collective-permute-start | bytes 245768 | tf_op jit(solution)/shard_map/ppermute | solution.py:347
  33.1 0.8 %collective-permute-start.7 = (bf16[320,128]{1,0:T(8,128)(2,1)S(1)}, bf16[320,128]{1,0:T(8,128)(2,1)S(1)}, u32[]{:S(2)}, u32[]{:S(2)}) collective-permute-start(bf16[320,128]{1,0:T(8,128)(2,1)S(1)} %get-tuple-element.30), channel_id=1, source_target_pairs={{0,2},{1,3},{2,0},{3,1},{4,6},{5,7},{6,4},{7,5},{8,10},{9,11},{10,... | collective-permute-start | bytes 245768 | tf_op jit(solution)/shard_map/ppermute | solution.py:347
  33.9 1.6 %collective-permute-start.8 = (bf16[320,128]{1,0:T(8,128)(2,1)S(1)}, bf16[320,128]{1,0:T(8,128)(2,1)S(1)}, u32[]{:S(2)}, u32[]{:S(2)}) collective-permute-start(bf16[320,128]{1,0:T(8,128)(2,1)S(1)} %get-tuple-element.31), channel_id=1, source_target_pairs={{0,3},{1,0},{2,1},{3,2},{4,7},{5,4},{6,5},{7,6},{8,11},{9,8},{10,9... | collective-permute-start | bytes 245768 | tf_op jit(solution)/shard_map/ppermute | solution.py:347
  35.6 1.5 %collective-permute-done.6.refs_1_ = bf16[320,128]{1,0:T(8,128)(2,1)S(1)} collective-permute-done((bf16[320,128]{1,0:T(8,128)(2,1)S(1)}, bf16[320,128]{1,0:T(8,128)(2,1)S(1)}, u32[]{:S(2)}, u32[]{:S(2)}) %collective-permute-start.6) | collective-permute-done | bytes 81952 | tf_op jit(solution)/shard_map/ppermute | solution.py:347
  37.0 1.9 %collective-permute-done.7.refs_2_ = bf16[320,128]{1,0:T(8,128)(2,1)S(1)} collective-permute-done((bf16[320,128]{1,0:T(8,128)(2,1)S(1)}, bf16[320,128]{1,0:T(8,128)(2,1)S(1)}, u32[]{:S(2)}, u32[]{:S(2)}) %collective-permute-start.7) | collective-permute-done | bytes 81952 | tf_op jit(solution)/shard_map/ppermute | solution.py:347
  39.0 0.3 collective-permute-done.8.refs_3_
  39.3 1.7 %shard_map.100 = (f32[272,128]{1,0:T(8,128)}, f32[272,128]{1,0:T(8,128)}) custom-call(s32[4,2]{1,0:T(4,128)S(1)} %copy.15.shifts, bf16[320,128]{1,0:T(8,128)(2,1)S(1)} %get-tuple-element.28.refs_0_, bf16[320,128]{1,0:T(8,128)(2,1)S(1)} %collective-permute-done.6.refs_1_, bf16[320,128]{1,0:T(8,128)(2,1)S(1)} %collective-permute-done.7.refs_2_, ...), custom_call_target="tpu_custom_call" | custom-call | tf_op jit(solution)/shard_map/pallas_call | solution.py:398
  (12 shorter events, 0.1 us)
Async XLA Ops:
  0.6 17.9 %copy-start = (bf16[4,256,256]{2,1,0:T(8,128)(2,1)S(1)}, bf16[4,256,256]{2,1,0:T(8,128)(2,1)}, u32[]{:S(2)}) copy-start(bf16[4,256,256]{2,1,0:T(8,128)(2,1)} %constant.2.clone.tables) | copy-start | bytes 1572868
  1.5 0.9 %copy-start.2 = (f32[136,2,128]{2,1,0:T(2,128)S(1)}, f32[136,2,128]{2,1,0:T(2,128)}, u32[]{:S(2)}) copy-start(f32[136,2,128]{2,1,0:T(2,128)} %param.8) | copy-start | bytes 417796
  2.4 0.9 %copy-start.3 = (f32[136,2,128]{2,1,0:T(2,128)S(1)}, f32[136,2,128]{2,1,0:T(2,128)}, u32[]{:S(2)}) copy-start(f32[136,2,128]{2,1,0:T(2,128)} %param.9) | copy-start | bytes 417796
  4.5 11.7 %collective-permute-start.1 = (bf16[320,128]{1,0:T(8,128)(2,1)S(1)}, bf16[320,128]{1,0:T(8,128)(2,1)S(1)}, u32[]{:S(2)}, u32[]{:S(2)}) collective-permute-start(bf16[320,128]{1,0:T(8,128)(2,1)S(1)} %get-tuple-element.19), channel_id=1, source_target_pairs={{0,1},{1,2},{2,3},{3,0},{4,5},{5,6},{6,7},{7,4},{8,9},{9,10},{10,1... | collective-permute-start | bytes 245768 | tf_op jit(solution)/shard_map/ppermute | solution.py:347
  7.6 8.6 %collective-permute-start.2 = (bf16[320,128]{1,0:T(8,128)(2,1)S(1)}, bf16[320,128]{1,0:T(8,128)(2,1)S(1)}, u32[]{:S(2)}, u32[]{:S(2)}) collective-permute-start(bf16[320,128]{1,0:T(8,128)(2,1)S(1)} %get-tuple-element.20), channel_id=1, source_target_pairs={{0,2},{1,3},{2,0},{3,1},{4,6},{5,7},{6,4},{7,5},{8,10},{9,11},{10,... | collective-permute-start | bytes 245768 | tf_op jit(solution)/shard_map/ppermute | solution.py:347
  10.2 6.0 %collective-permute-start.3 = (bf16[320,128]{1,0:T(8,128)(2,1)S(1)}, bf16[320,128]{1,0:T(8,128)(2,1)S(1)}, u32[]{:S(2)}, u32[]{:S(2)}) collective-permute-start(bf16[320,128]{1,0:T(8,128)(2,1)S(1)} %get-tuple-element.21), channel_id=1, source_target_pairs={{0,3},{1,0},{2,1},{3,2},{4,7},{5,4},{6,5},{7,6},{8,11},{9,8},{10,9... | collective-permute-start | bytes 245768 | tf_op jit(solution)/shard_map/ppermute | solution.py:347
  12.3 3.9 %collective-permute-start = (s32[4,2]{1,0:T(4,128)S(1)}, s32[4,2]{1,0:T(4,128)S(1)}, u32[]{:S(2)}, u32[]{:S(2)}) collective-permute-start(s32[4,2]{1,0:T(4,128)S(1)} %copy.14.spots), channel_id=1, source_target_pairs={{0,4},{4,8},{8,12},{12,16},{16,20},{20,24},{24,28},{28,0},{1,5},{5... | collective-permute-start | bytes 104 | tf_op jit(solution)/shard_map/ppermute | solution.py:353
  17.1 6.1 %collective-permute-start.4 = (bf16[256,128]{1,0:T(8,128)(2,1)S(1)}, bf16[256,128]{1,0:T(8,128)(2,1)S(1)}, u32[]{:S(2)}, u32[]{:S(2)}) collective-permute-start(bf16[256,128]{1,0:T(8,128)(2,1)S(1)} %get-tuple-element.25), channel_id=1, source_target_pairs={{0,28},{4,0},{8,4},{12,8},{16,12},{20,16},{24,20},{28,24},{1,29},{... | collective-permute-start | bytes 196616 | tf_op jit(solution)/shard_map/ppermute | solution.py:353
  18.5 1.0 %copy-start.1 = (f32[1,4,128,128]{3,2,1,0:T(8,128)S(1)}, f32[1,4,128,128]{3,2,1,0:T(8,128)}, u32[]{:S(2)}) copy-start(f32[1,4,128,128]{3,2,1,0:T(8,128)} %param.12) | copy-start | bytes 786436
  19.4 0.9 %copy-start.4 = (f32[2,128,128]{2,1,0:T(8,128)S(1)}, f32[2,128,128]{2,1,0:T(8,128)}, u32[]{:S(2)}) copy-start(f32[2,128,128]{2,1,0:T(8,128)} %probe.3) | copy-start | bytes 393220
  25.0 4.6 %collective-permute-start.5 = (bf16[256,128]{1,0:T(8,128)(2,1)S(1)}, bf16[256,128]{1,0:T(8,128)(2,1)S(1)}, u32[]{:S(2)}, u32[]{:S(2)}) collective-permute-start(bf16[256,128]{1,0:T(8,128)(2,1)S(1)} %get-tuple-element.27), channel_id=1, source_target_pairs={{0,4},{4,8},{8,12},{12,16},{16,20},{20,24},{24,28},{28,0},{1,5},{5... | collective-permute-start | bytes 196616 | tf_op jit(solution)/shard_map/ppermute | solution.py:353
  30.7 6.3 %collective-permute-start.6 = (bf16[320,128]{1,0:T(8,128)(2,1)S(1)}, bf16[320,128]{1,0:T(8,128)(2,1)S(1)}, u32[]{:S(2)}, u32[]{:S(2)}) collective-permute-start(bf16[320,128]{1,0:T(8,128)(2,1)S(1)} %get-tuple-element.29), channel_id=1, source_target_pairs={{0,1},{1,2},{2,3},{3,0},{4,5},{5,6},{6,7},{7,4},{8,9},{9,10},{10,1... | collective-permute-start | bytes 245768 | tf_op jit(solution)/shard_map/ppermute | solution.py:347
  33.1 5.8 %collective-permute-start.7 = (bf16[320,128]{1,0:T(8,128)(2,1)S(1)}, bf16[320,128]{1,0:T(8,128)(2,1)S(1)}, u32[]{:S(2)}, u32[]{:S(2)}) collective-permute-start(bf16[320,128]{1,0:T(8,128)(2,1)S(1)} %get-tuple-element.30), channel_id=1, source_target_pairs={{0,2},{1,3},{2,0},{3,1},{4,6},{5,7},{6,4},{7,5},{8,10},{9,11},{10,... | collective-permute-start | bytes 245768 | tf_op jit(solution)/shard_map/ppermute | solution.py:347
  33.9 5.3 %collective-permute-start.8 = (bf16[320,128]{1,0:T(8,128)(2,1)S(1)}, bf16[320,128]{1,0:T(8,128)(2,1)S(1)}, u32[]{:S(2)}, u32[]{:S(2)}) collective-permute-start(bf16[320,128]{1,0:T(8,128)(2,1)S(1)} %get-tuple-element.31), channel_id=1, source_target_pairs={{0,3},{1,0},{2,1},{3,2},{4,7},{5,4},{6,5},{7,6},{8,11},{9,8},{10,9... | collective-permute-start | bytes 245768 | tf_op jit(solution)/shard_map/ppermute | solution.py:347

commit v2 on v1

--- a/solution.py
+++ b/solution.py
@@ -19,6 +19,7 @@
 f32, bf16, i32 = jnp.float32, jnp.bfloat16, jnp.int32
 SMEM = pl.BlockSpec(memory_space=pltpu.SMEM)
 VMEM = pl.BlockSpec(memory_space=pltpu.VMEM)
+HBM = pl.BlockSpec(memory_space=pltpu.HBM)
 
 
 def fourier_tables():
@@ -69,20 +70,33 @@
     return jnp.concatenate(parts, 0)
 
 
-def window_kernel(shifts, delta, beta, *refs):
-    outs, scratch = refs[:-1], refs[-1]
+def window_kernel(shifts, spots, counts, delta, beta, probe_in, measured_in, *refs):
+    outs = refs[:-8]
+    slot, probe, measured, slab_delta, slab_beta, scratch, near, far = refs[-8:]
+    copies = [
+        pltpu.make_async_copy(source, target, near.at[k])
+        for k, (source, target) in enumerate([(delta, slab_delta), (beta, slab_beta)])
+    ]
+    others = [
+        pltpu.make_async_copy(source, target, far.at[k])
+        for k, (source, target) in enumerate([(measured_in, measured), (probe_in, probe)])
+    ]
+    for copy in copies + others:
+        copy.start()
     angles = len(outs)
     tile = delta.shape[0] // 2
     scratch[2 * tile :, :] = jnp.zeros((scratch.shape[0] - 2 * tile, N), f32)
     me = lax.axis_index("ang")
     lane = lane_iota(tile)
-    for d, out in enumerate(outs):
+    for copy in copies:
+        copy.wait()
+    for d in [*range(1, angles), 0]:
         angle = lax.rem(me + d, angles)
         mains, margins = [], []
-        for ref in (delta, beta):
+        for ref in (slab_delta, slab_beta):
             main = margin = None
             for z in range(2):
-                s = shifts[angle, z]
+                s = shifts[z, angle]
                 rolled = pltpu.roll(ref[pl.ds(z, tile, stride=2), :], lax.rem(N - s, N), 1)
                 source = lane + s
                 inside = (source >= 0) & (source < N)
@@ -91,12 +105,31 @@
                 margin = out_of if z == 0 else margin + out_of
             mains.append(main)
             margins.append(margin)
-        out[...] = packed_message(jnp.concatenate(mains, 0), jnp.concatenate(margins, 0), scratch)
-
-
-def assemble_kernel(previous, *refs):
-    proj, halo, margins = refs[-3:]
-    received = refs[:-3]
+        outs[d][...] = packed_message(jnp.concatenate(mains, 0), jnp.concatenate(margins, 0), scratch)
+    for copy in others:
+        copy.wait()
+    slot[0:N, :] = measured[0]
+    row = jnp.where(counts[0, 0] > 0, spots[0, 0], 0)
+    slot[N : N + 8, :] = jnp.full((8, N), row, i32).astype(f32)
+    slot[N + 8 :, :] = jnp.full((8, N), spots[1, 0], i32).astype(f32)
+
+
+def slot_position(slot):
+    return slot[N, 0].astype(i32), slot[N + 8, 0].astype(i32)
+
+
+def block_of(column, blocks):
+    first, offset = column // N, lax.rem(column, N)
+    return first, jnp.minimum(first + 1, blocks - 1), offset
+
+
+def is_even():
+    return lax.rem(lax.axis_index("rows"), 2) == 0
+
+
+def assemble_kernel(spots, slot, *refs):
+    proj, core, cross, margins = refs[-4:]
+    received = refs[:-4]
     blocks = len(received)
     tile = proj.shape[2]
     me = lax.axis_index("ang")
@@ -114,14 +147,25 @@
             extra = jnp.where(lane < SHIFT, margins[before, part], 0.0)
             extra += jnp.where(lane >= N - SHIFT, margins[after, part], 0.0)
             proj[c, block] += extra
-    column = previous[0, 1]
-    first, offset = column // N, lax.rem(column, N)
-    second = jnp.minimum(first + 1, blocks - 1)
+    _, previous = slot_position(slot)
     lane = lane_iota(N)
-    for c in range(2):
-        left = roll_left(proj[c, first, 0:N, :], offset)
-        right = roll_left(proj[c, second, 0:N, :], offset)
-        halo[c * N : (c + 1) * N, :] = jnp.where(lane < N - offset, left, right).astype(bf16)
+    even = is_even()
+    for upper in (True, False):
+        first, second, offset = block_of(spots[1, 0] if upper else previous, blocks)
+        start = EDGE_ROWS if upper else 0
+        for c in range(2):
+            left = roll_left(proj[c, first, start : start + N, :], offset)
+            right = roll_left(proj[c, second, start : start + N, :], offset)
+            value = jnp.where(lane < N - offset, left, right).astype(bf16)
+            part = slice(c * N, (c + 1) * N)
+
+            @pl.when(even == upper)
+            def _():
+                core[part, :] = value
+
+            @pl.when(even != upper)
+            def _():
+                cross[part, :] = value
 
 
 def transmit(phase, absorb):
@@ -200,10 +244,19 @@
     return grads
 
 
-def column_of(spots, slot, blocks):
-    column = spots[slot, 1]
-    first, offset = column // N, lax.rem(column, N)
-    return first, jnp.minimum(first + 1, blocks - 1), offset
+def patch_of(values, lane, offset, first, second, rows):
+    pair = []
+    for c in range(2):
+        left = roll_left(values[c, first, rows, :], offset)
+        right = roll_left(values[c, second, rows, :], offset)
+        pair.append(jnp.where(lane < N - offset, left, right))
+    return pair
+
+
+def add_patch(total, c, rows, value, lane, offset, first, second):
+    placed = roll_lanes(value, offset)
+    total[c, first, rows, :] += jnp.where(lane >= offset, placed, 0.0)
+    total[c, second, rows, :] += jnp.where(lane < offset, placed, 0.0)
 
 
 def inner_kernel(spots, counts, proj, probe, measured, tables, trans, grad, frame):
@@ -219,72 +272,66 @@
     lane = lane_iota(N)
     patches, weights = [], []
     for slot in range(1, slots):
-        row = jnp.minimum(spots[slot, 0], EDGE_ROWS)
-        first, second, offset = column_of(spots, slot, blocks)
-        pair = []
-        for c in range(2):
-            left = roll_left(trans[c, first, pl.ds(row, N), :], offset)
-            right = roll_left(trans[c, second, pl.ds(row, N), :], offset)
-            pair.append(jnp.where(lane < N - offset, left, right))
-        patches.append(pair)
+        row = jnp.minimum(spots[0, slot], EDGE_ROWS)
+        first, second, offset = block_of(spots[1, slot], blocks)
+        patches.append(patch_of(trans, lane, offset, first, second, pl.ds(row, N)))
         weights.append(jnp.where(slot < counts[0, 0], 1.0, 0.0).astype(f32))
     grads = scan_gradients(patches, [measured[slot] for slot in range(1, slots)], weights, probe, tables)
     lane = lane_iota(tile)
     for slot in range(1, slots):
-        row = jnp.minimum(spots[slot, 0], EDGE_ROWS)
-        first, second, offset = column_of(spots, slot, blocks)
+        row = jnp.minimum(spots[0, slot], EDGE_ROWS)
+        first, second, offset = block_of(spots[1, slot], blocks)
         for c in range(2):
             frame[SHIFT : SHIFT + N, :] = grads[slot - 1][c]
-            placed = roll_lanes(frame[pl.ds(SHIFT - row, tile), :], offset)
-            grad[c, first] += jnp.where(lane >= offset, placed, 0.0)
-            grad[c, second] += jnp.where(lane < offset, placed, 0.0)
-
-
-def edge_kernel(spots, counts, halo, trans, probe, measured, tables, own, sent, patch, frame):
-    blocks, tile = trans.shape[1], trans.shape[2]
-    first, second, offset = column_of(spots, 0, blocks)
-    row = spots[0, 0]
-    last = lax.axis_index("rows") == lax.axis_size("rows") - 1
-    lane = lane_iota(tile)
-    for c in range(2):
-        left = roll_left(trans[c, first], offset)
-        right = roll_left(trans[c, second], offset)
-        patch[c, 0:tile, :] = jnp.where(lane < N - offset, left, right)
-    below = jnp.where(last, 0.0, halo[...].astype(f32))
-    re, im = transmit(below[:N], below[N:])
-    patch[0, tile:, :] = re
-    patch[1, tile:, :] = im
-    pair = [patch[c, pl.ds(row, N), :] for c in range(2)]
-    weight = jnp.where(0 < counts[0, 0], 1.0, 0.0).astype(f32)
-    grads = scan_gradients([pair], [measured[0]], [weight], probe, tables)[0]
-    for c in range(2):
-        frame[c, 0:tile, :] = jnp.zeros((tile, N), f32)
-        frame[c, tile : tile + N, :] = grads[c]
-        frame[c, tile + N :, :] = jnp.zeros((tile, N), f32)
-    for c in range(2):
-        own[c] = frame[c, pl.ds(tile - row, tile), :]
-        sent[c * N : (c + 1) * N, :] = frame[c, pl.ds(2 * tile - row, N), :].astype(bf16)
-
-
-def cut_kernel(spots, previous, trans, inner, own, above, *refs):
-    outs, total, scratch = refs[:-2], refs[-2], refs[-1]
+            add_patch(grad, c, slice(None), frame[pl.ds(SHIFT - row, tile), :], lane, offset, first, second)
+
+
+def edge_kernel(spots, counts, slot, core, cross, trans, inner, probe, measured, tables, *refs):
+    outs, (total, patch, frame, scratch) = refs[:-4], refs[-4:]
     blocks, tile = trans.shape[1], trans.shape[2]
     scratch[2 * tile :, :] = jnp.zeros((scratch.shape[0] - 2 * tile, N), f32)
+    even = is_even()
+    own_row, own_column = spots[0, 0], spots[1, 0]
+    prev_row, prev_column = slot_position(slot)
+    own_block, prev_block = block_of(own_column, blocks), block_of(prev_column, blocks)
+    last = lax.axis_index("rows") == lax.axis_size("rows") - 1
+    near, away = core[...].astype(f32), cross[...].astype(f32)
+    below = jnp.where(last, 0.0, jnp.where(even, near, away))
+    above = jnp.where(even, away, near)
+    re, im = transmit(below[:N], below[N:])
+    patch[0, 0, tile:, :] = re
+    patch[0, 1, tile:, :] = im
+    re, im = transmit(above[:N], above[N:])
+    patch[1, 0, EDGE_ROWS:tile, :] = re
+    patch[1, 1, EDGE_ROWS:tile, :] = im
+    first, second, offset = own_block
+    pair = patch_of(trans, lane_iota(tile), offset, first, second, slice(None))
+    for c in range(2):
+        patch[0, c, 0:tile, :] = pair[c]
+    first, second, offset = prev_block
+    pair = patch_of(trans, lane_iota(N), offset, first, second, slice(0, N))
+    for c in range(2):
+        patch[1, c, tile:, :] = pair[c]
+    reaches = (prev_row > EDGE_ROWS) & (lax.axis_index("rows") > 0)
+    start = jnp.maximum(prev_row, EDGE_ROWS)
+    patches = [
+        [patch[0, c, pl.ds(own_row, N), :] for c in range(2)],
+        [patch[1, c, pl.ds(start, N), :] for c in range(2)],
+    ]
+    weights = [jnp.where(flag, 1.0, 0.0).astype(f32) for flag in (counts[0, 0] > 0, reaches)]
+    grads = scan_gradients(patches, [measured[0], slot[0:N, :]], weights, probe, tables)
     total[...] = inner[...]
-    first, second, offset = column_of(spots, 0, blocks)
-    lane = lane_iota(tile)
-    for c in range(2):
-        placed = roll_lanes(own[c], offset)
-        total[c, first] += jnp.where(lane >= offset, placed, 0.0)
-        total[c, second] += jnp.where(lane < offset, placed, 0.0)
-    first, second, offset = column_of(previous, 0, blocks)
-    top = lax.axis_index("rows") == 0
-    received = jnp.where(top, 0.0, above[...].astype(f32))
-    lane = lane_iota(N)
-    for c in range(2):
-        placed = roll_lanes(received[c * N : (c + 1) * N], offset)
-        total[c, first, 0:N, :] += jnp.where(lane >= offset, placed, 0.0)
-        total[c, second, 0:N, :] += jnp.where(lane < offset, placed, 0.0)
+    for c in range(2):
+        frame[c, 0:tile, :] = jnp.zeros((tile, N), f32)
+        frame[c, tile : tile + N, :] = grads[0][c]
+        frame[c, tile + N :, :] = jnp.zeros((frame.shape[1] - tile - N, N), f32)
+    for c in range(2):
+        add_patch(total, c, slice(None), frame[c, pl.ds(tile - own_row, tile), :], lane_iota(tile), offset=own_block[2], first=own_block[0], second=own_block[1])
+    for c in range(2):
+        frame[c, 0:N, :] = grads[1][c]
+        frame[c, N : 2 * N, :] = jnp.zeros((N, N), f32)
+    for c in range(2):
+        add_patch(total, c, slice(0, N), frame[c, pl.ds(tile - start, N), :], lane_iota(N), offset=prev_block[2], first=prev_block[0], second=prev_block[1])
     for block in range(blocks):
         tr, ti = trans[0, block], trans[1, block]
         gr, gi = total[0, block], total[1, block]
@@ -315,7 +362,7 @@
         message = ref[...].astype(f32)
         margins = margins_of(message, 2 * tile)
         for z in range(2):
-            s = shifts[angle, z]
+            s = shifts[z, angle]
             target = lane + s
             inside = (target >= 0) & (target < N)
             for c in range(2):
@@ -329,12 +376,13 @@
 
 
 def call(kernel, ins, outs, scratch=(), flops=0, bytes_accessed=0):
+    scratch = [pltpu.VMEM(item, f32) if isinstance(item, tuple) else item for item in scratch]
     return pl.pallas_call(
         kernel,
         in_specs=ins,
         out_specs=[VMEM] * len(outs),
         out_shape=[jax.ShapeDtypeStruct(shape, dtype) for shape, dtype in outs],
-        scratch_shapes=[pltpu.VMEM(shape, f32) for shape in scratch],
+        scratch_shapes=scratch,
         compiler_params=pltpu.CompilerParams(vmem_limit_bytes=32 * 1024 * 1024),
         cost_estimate=pl.CostEstimate(flops=flops, bytes_accessed=bytes_accessed, transcendentals=0),
     )
@@ -348,32 +396,46 @@
     return received
 
 
-def shift_rows(value, steps):
+def on_rows(value, target):
     count = lax.axis_size("rows")
-    return lax.ppermute(value, "rows", [(i, (i + steps) % count) for i in range(count)])
+    return lax.ppermute(value, "rows", [(i, target(i) % count) for i in range(count)])
 
 
 def on_device(delta_obj, beta_obj, layer_shifts, illumination_field, amplitudes, positions, scan_counts):
     tile = delta_obj.shape[0]
     angles = lax.axis_size("ang")
     message = ((2 * tile + PACK_ROWS, N), bf16)
-    padded = len(groups_of(2 * tile)) * PACK_ROWS
+    padded = (len(groups_of(2 * tile)) * PACK_ROWS, N)
     field = ((2, angles, tile, N), f32)
-    measured, spots = amplitudes[0], positions[0]
+    slab = (2 * tile, N)
+    halo = ((2 * N, N), bf16)
+    shifts, spots = layer_shifts.T, positions[0].T
     tables = jnp.asarray(fourier_tables())
-    previous = shift_rows(spots, 1)
-
-    windows = call(window_kernel, [SMEM] + [VMEM] * 2, [message] * angles, [(padded, N)])(
-        layer_shifts, delta_obj.reshape(2 * tile, N), beta_obj.reshape(2 * tile, N)
+
+    *windows, slot, probe, measured = call(
+        window_kernel,
+        [SMEM] * 3 + [HBM] * 4,
+        [message] * angles + [((N + 16, N), f32), (illumination_field.shape, f32), (amplitudes.shape[1:], f32)],
+        [slab, slab, padded, pltpu.SemaphoreType.DMA((2,)), pltpu.SemaphoreType.DMA((2,))],
+    )(
+        shifts,
+        spots,
+        scan_counts,
+        *(
+            pltpu.with_memory_space_constraint(value, pltpu.HBM)
+            for value in (delta_obj.reshape(slab), beta_obj.reshape(slab), illumination_field, amplitudes[0])
+        ),
     )
     received = exchange(windows)
-    proj, halo = call(
+    previous = on_rows(slot, lambda i: i + 1)
+    proj, core, cross = call(
         assemble_kernel,
-        [SMEM] + [VMEM] * angles,
-        [field, ((2 * N, N), bf16)],
+        [SMEM] + [VMEM] * (angles + 1),
+        [field, halo, halo],
         [(angles, 2 * tile, N)],
-    )(previous, *received)
-    below = shift_rows(halo, -1)
+    )(spots, previous, *received)
+    core = on_rows(core, lambda i: i ^ 1)
+    cross = on_rows(cross, lambda i: i + 1 if i % 2 else i - 1)
     trans, inner = call(
         inner_kernel,
         [SMEM] * 2 + [VMEM] * 4,
@@ -381,22 +443,15 @@
         [(N + 2 * SHIFT, N)],
         flops=3 * 10**9,
         bytes_accessed=3 * 10**6,
-    )(spots, scan_counts, proj, illumination_field, measured, tables)
-    own, sent = call(
+    )(spots, scan_counts, proj, probe, measured, tables)
+    outgoing = call(
         edge_kernel,
-        [SMEM] * 2 + [VMEM] * 5,
-        [((2, tile, N), f32), ((2 * N, N), bf16)],
-        [(2, tile + N, N), (2, 2 * tile + N, N)],
-    )(spots, scan_counts, below, trans, illumination_field, measured, tables)
-    above = shift_rows(sent, 1)
-    outgoing = call(
-        cut_kernel,
-        [SMEM] * 2 + [VMEM] * 4,
+        [SMEM] * 2 + [VMEM] * 8,
         [message] * angles,
-        [field[0], (padded, N)],
-    )(spots, previous, trans, inner, own, above)
-    grad_delta, grad_beta = call(slab_kernel, [SMEM] + [VMEM] * angles, [((2 * tile, N), f32)] * 2)(
-        layer_shifts, *exchange(outgoing)
+        [field[0], (2, 2, tile + N, N), (2, 2 * tile + 8, N), padded],
+    )(spots, scan_counts, previous, core, cross, trans, inner, probe, measured, tables)
+    grad_delta, grad_beta = call(slab_kernel, [SMEM] + [VMEM] * angles, [(slab, f32)] * 2)(
+        shifts, *exchange(outgoing)
     )
     return grad_delta.reshape(tile, 2, N), grad_beta.reshape(tile, 2, N)
 

time: 41.2 us -> 36.6 us (0.89)
  local copies, waits for them, and re-layouts: 5.26 us -> 0.68 us
  waiting for transfers between devices: 11.5 us -> 9.85 us
  Pallas kernels: 9.53 us -> 10.8 us
  starting transfers between devices: 13.2 us -> 13.8 us
    unnamed x11 -> x6, local copies, waits for them, and re-layouts: 4.5 us -> 0.68 us
    ppermute x3, waiting for transfers between devices: 7.83 us -> 4.68 us  [on_rows(): lax.ppermute(value, 'rows', [(i, target(i) % count) for i in range(count)])]
    ppermute x6, waiting for transfers between devices: 3.71 us -> 5.17 us  [exchange(): lax.ppermute(messages[d], 'ang', [(i, (i + d) % count) for i in range(cou...]
    pallas_call x5 -> x4, Pallas kernels: 6.69 us -> 7.9 us  [the longest x1 2.78 us: on_device(): call(edge_kernel, [SMEM] * 2 + [VMEM] * 8, [message] * angles, [field[0],...]
    ppermute x3, starting transfers between devices: 1.44 us -> 2.28 us  [on_rows(): lax.ppermute(value, 'rows', [(i, target(i) % count) for i in range(count)])]
    squeeze x1 -> x0, local copies, waits for them, and re-layouts: 0.76 us -> none  [on_device(): measured, spots = (amplitudes[0], positions[0])]
  transfers between devices with their start and end apart: 9 -> 9, of which waited for: 5 -> 4; matrix products, arithmetic and copies ran while one was open for 2% -> 0% of each run, Pallas kernels for 7% -> 8%
where the time goes in v2:
time: 36.6 us; the launch traced here: 36.4 us
  starting transfers between devices  13.8 us (38%)
  Pallas kernels  10.8 us (30%)
  waiting for transfers between devices  9.85 us (27%)
  between operations  1.36 us (4%)
  local copies, waits for them, and re-layouts  0.68 us (2%)
    ppermute x6, starting transfers between devices, exchange(): lax.ppermute(messages[d], 'ang', [(i, (i + d) % count) for i in range(cou...  11.5 us
    ppermute x6, waiting for transfers between devices, exchange(): lax.ppermute(messages[d], 'ang', [(i, (i + d) % count) for i in range(cou...  5.17 us
    ppermute x3, waiting for transfers between devices, on_rows(): lax.ppermute(value, 'rows', [(i, target(i) % count) for i in range(count)])  4.68 us
    pallas_call x1, Pallas kernels, on_device(): call(inner_kernel, [SMEM] * 2 + [VMEM] * 4, [field, field], [(N + 2 * SHI...  2.85 us
    pallas_call x1, Pallas kernels, on_device(): call(edge_kernel, [SMEM] * 2 + [VMEM] * 8, [message] * angles, [field[0],...  2.78 us
    pallas_call x1, Pallas kernels, on_device(): call(window_kernel, [SMEM] * 3 + [HBM] * 4, [message] * angles + [((N + 1...  2.3 us
    ppermute x3, starting transfers between devices, on_rows(): lax.ppermute(value, 'rows', [(i, target(i) % count) for i in range(count)])  2.28 us
    pallas_call x1, Pallas kernels, on_device(): call(slab_kernel, [SMEM] + [VMEM] * angles, [(slab, f32)] * 2)  1.66 us
  transfers between devices with their start and end apart: 9, of which 4 were waited for; matrix products, arithmetic and copies ran while one was open for 0% of the time, Pallas kernels for 8%

profile of v2, /device:TPU:0, one launch (start us, length us, event | category | flops | bytes accessed | tf_op | source)
XLA Modules:
  0.0 36.4 jit_solution(14352168445611300297)
XLA Ops:
  1.3 0.7 %copy-done.2 = s32[4,2]{0,1:T(2,128)S(1)} copy-done((s32[4,2]{0,1:T(2,128)S(1)}, s32[4,2]{0,1:T(2,128)}, u32[]{:S(2)}) %copy-start.2) | copy-done | bytes 56
  2.0 0.0 copy-done.1
  2.0 2.3 %shard_map.95 = (bf16[320,128]{1,0:T(8,128)(2,1)S(1)}, bf16[320,128]{1,0:T(8,128)(2,1)S(1)}, bf16[320,128]{1,0:T(8,128)(2,1)S(1)}, bf16[320,128]{1,0:T(8,128)(2,...) custom-call(s32[2,4]{1,0:T(2,128)S(1)} %bitcast.13, s32[2,4]{1,0:T(2,128)S(1)} %bitcast.9, ...), custom_call_target="tpu_custom_call" | custom-call | tf_op jit(solution)/shard_map/pallas_call | solution.py:415
  4.3 3.1 %collective-permute-start.1 = (bf16[320,128]{1,0:T(8,128)(2,1)S(1)}, bf16[320,128]{1,0:T(8,128)(2,1)S(1)}, u32[]{:S(2)}, u32[]{:S(2)}) collective-permute-start(bf16[320,128]{1,0:T(8,128)(2,1)S(1)} %get-tuple-element.22), channel_id=1, source_target_pairs={{0,1},{1,2},{2,3},{3,0},{4,5},{5,6},{6,7},{7,4},{8,9},{9,10},{10,1... | collective-permute-start | bytes 245768 | tf_op jit(solution)/shard_map/ppermute | solution.py:395
  7.4 2.6 %collective-permute-start.2 = (bf16[320,128]{1,0:T(8,128)(2,1)S(1)}, bf16[320,128]{1,0:T(8,128)(2,1)S(1)}, u32[]{:S(2)}, u32[]{:S(2)}) collective-permute-start(bf16[320,128]{1,0:T(8,128)(2,1)S(1)} %get-tuple-element.23), channel_id=1, source_target_pairs={{0,2},{1,3},{2,0},{3,1},{4,6},{5,7},{6,4},{7,5},{8,10},{9,11},{10,... | collective-permute-start | bytes 245768 | tf_op jit(solution)/shard_map/ppermute | solution.py:395
  9.9 1.3 %collective-permute-start.3 = (bf16[320,128]{1,0:T(8,128)(2,1)S(1)}, bf16[320,128]{1,0:T(8,128)(2,1)S(1)}, u32[]{:S(2)}, u32[]{:S(2)}) collective-permute-start(bf16[320,128]{1,0:T(8,128)(2,1)S(1)} %get-tuple-element.24), channel_id=1, source_target_pairs={{0,3},{1,0},{2,1},{3,2},{4,7},{5,4},{6,5},{7,6},{8,11},{9,8},{10,9... | collective-permute-start | bytes 245768 | tf_op jit(solution)/shard_map/ppermute | solution.py:395
  11.3 0.0 collective-permute-start
  11.3 4.7 %collective-permute-done.slot = f32[144,128]{1,0:T(8,128)S(1)} collective-permute-done((f32[144,128]{1,0:T(8,128)S(1)}, f32[144,128]{1,0:T(8,128)S(1)}, u32[]{:S(2)}, u32[]{:S(2)}) %collective-permute-start) | collective-permute-done | bytes 73760 | tf_op jit(solution)/shard_map/ppermute | solution.py:401
  16.0 0.0 collective-permute-done.1.refs_1_
  16.0 0.0 collective-permute-done.2.refs_2_
  16.0 0.0 collective-permute-done.3.refs_3_
  16.0 1.2 %shard_map.96 = (f32[2,4,136,128]{3,2,1,0:T(8,128)S(1)}, bf16[256,128]{1,0:T(8,128)(2,1)S(1)}, bf16[256,128]{1,0:T(8,128)(2,1)S(1)}) custom-call(s32[2,4]{1,0:T(2,128)S(1)} %bitcast.10, f32[144,128]{1,0:T(8,128)S(1)} %collective-permute-done.slot, bf16[320,128]{1,0:T(8,128)(2,1)S(1)} %get-tuple-element.21.refs_0_, ...), custom_call_target="tpu_custom_call" | custom-call | tf_op jit(solution)/shard_map/pallas_call | solution.py:431
  17.2 0.1 collective-permute-start.4
  17.2 2.2 %collective-permute-start.5 = (bf16[256,128]{1,0:T(8,128)(2,1)S(1)}, bf16[256,128]{1,0:T(8,128)(2,1)S(1)}, u32[]{:S(2)}, u32[]{:S(2)}) collective-permute-start(bf16[256,128]{1,0:T(8,128)(2,1)S(1)} %get-tuple-element.26), channel_id=1, source_target_pairs={{0,28},{4,8},{8,4},{12,16},{16,12},{20,24},{24,20},{28,0},{1,29},{... | collective-permute-start | bytes 196616 | tf_op jit(solution)/shard_map/ppermute | solution.py:401
  19.4 2.9 %shard_map.97 = (f32[2,4,136,128]{3,2,1,0:T(8,128)S(1)}, f32[2,4,136,128]{3,2,1,0:T(8,128)S(1)}) custom-call(s32[2,4]{1,0:T(2,128)S(1)} %bitcast.11, s32[1,1]{1,0:T(1,128)S(6)} %copy.10.counts, f32[2,4,136,128]{3,2,1,0:T(8,128)S(1)} %get-tuple-element.27.proj, f32[2,128,128]{2,1,0:T(8,128)S(1)} %get-tuple-element.28.probe, ...), custom_call_target="tpu_custom_call" | custom-call | flops 3000000000 | bytes 3000000 | tf_op jit(solution)/shard_map/pallas_call | solution.py:439
  22.3 0.0 collective-permute-done.5.cross
  22.3 2.8 %shard_map.98 = (bf16[320,128]{1,0:T(8,128)(2,1)S(1)}, bf16[320,128]{1,0:T(8,128)(2,1)S(1)}, bf16[320,128]{1,0:T(8,128)(2,1)S(1)}, bf16[320,128]{1,0:T(8,128)(2,1)S(1)}) custom-call(s32[2,4]{1,0:T(2,128)S(1)} %bitcast.12, s32[1,1]{1,0:T(1,128)S(6)} %copy.10.counts, f32[144,128]{1,0:T(8,128)S(1)} %collective-permute-done.slot, ...), custom_call_target="tpu_custom_call" | custom-call | tf_op jit(solution)/shard_map/pallas_call | solution.py:447
  25.1 2.1 %collective-permute-start.6 = (bf16[320,128]{1,0:T(8,128)(2,1)S(1)}, bf16[320,128]{1,0:T(8,128)(2,1)S(1)}, u32[]{:S(2)}, u32[]{:S(2)}) collective-permute-start(bf16[320,128]{1,0:T(8,128)(2,1)S(1)} %get-tuple-element.33), channel_id=1, source_target_pairs={{0,1},{1,2},{2,3},{3,0},{4,5},{5,6},{6,7},{7,4},{8,9},{9,10},{10,1... | collective-permute-start | bytes 245768 | tf_op jit(solution)/shard_map/ppermute | solution.py:395
  27.2 1.8 %collective-permute-start.7 = (bf16[320,128]{1,0:T(8,128)(2,1)S(1)}, bf16[320,128]{1,0:T(8,128)(2,1)S(1)}, u32[]{:S(2)}, u32[]{:S(2)}) collective-permute-start(bf16[320,128]{1,0:T(8,128)(2,1)S(1)} %get-tuple-element.34), channel_id=1, source_target_pairs={{0,2},{1,3},{2,0},{3,1},{4,6},{5,7},{6,4},{7,5},{8,10},{9,11},{10,... | collective-permute-start | bytes 245768 | tf_op jit(solution)/shard_map/ppermute | solution.py:395
  29.0 0.6 %collective-permute-start.8 = (bf16[320,128]{1,0:T(8,128)(2,1)S(1)}, bf16[320,128]{1,0:T(8,128)(2,1)S(1)}, u32[]{:S(2)}, u32[]{:S(2)}) collective-permute-start(bf16[320,128]{1,0:T(8,128)(2,1)S(1)} %get-tuple-element.35), channel_id=1, source_target_pairs={{0,3},{1,0},{2,1},{3,2},{4,7},{5,4},{6,5},{7,6},{8,11},{9,8},{10,9... | collective-permute-start | bytes 245768 | tf_op jit(solution)/shard_map/ppermute | solution.py:395
  29.6 2.8 %collective-permute-done.6.refs_1_ = bf16[320,128]{1,0:T(8,128)(2,1)S(1)} collective-permute-done((bf16[320,128]{1,0:T(8,128)(2,1)S(1)}, bf16[320,128]{1,0:T(8,128)(2,1)S(1)}, u32[]{:S(2)}, u32[]{:S(2)}) %collective-permute-start.6) | collective-permute-done | bytes 81952 | tf_op jit(solution)/shard_map/ppermute | solution.py:395
  32.4 2.3 %collective-permute-done.7.refs_2_ = bf16[320,128]{1,0:T(8,128)(2,1)S(1)} collective-permute-done((bf16[320,128]{1,0:T(8,128)(2,1)S(1)}, bf16[320,128]{1,0:T(8,128)(2,1)S(1)}, u32[]{:S(2)}, u32[]{:S(2)}) %collective-permute-start.7) | collective-permute-done | bytes 81952 | tf_op jit(solution)/shard_map/ppermute | solution.py:395
  34.7 0.1 collective-permute-done.8.refs_3_
  34.8 1.7 %shard_map.99 = (f32[272,128]{1,0:T(8,128)}, f32[272,128]{1,0:T(8,128)}) custom-call(s32[2,4]{1,0:T(2,128)S(1)} %bitcast.14, bf16[320,128]{1,0:T(8,128)(2,1)S(1)} %get-tuple-element.32.refs_0_, bf16[320,128]{1,0:T(8,128)(2,1)S(1)} %collective-permute-done.6.refs_1_, bf16[320,128]{1,0:T(8,128)(2,1)S(1)} %collective-permute-done.7.refs_2_, ...), custom_call_target="tpu_custom_call" | custom-call | tf_op jit(solution)/shard_map/pallas_call | solution.py:453
  (5 shorter events, 0.0 us)
Async XLA Ops:
  1.3 0.7 %copy-start.2 = (s32[4,2]{0,1:T(2,128)S(1)}, s32[4,2]{0,1:T(2,128)}, u32[]{:S(2)}) copy-start(s32[4,2]{0,1:T(2,128)} %param.10) | copy-start | bytes 100
  1.3 0.7 %copy-start.1 = (s32[1,4,2]{1,2,0:T(2,128)S(1)}, s32[1,4,2]{1,2,0:T(2,128)}, u32[]{:S(2)}) copy-start(s32[1,4,2]{1,2,0:T(2,128)} %param.13) | copy-start | bytes 100
  2.0 17.5 %copy-start = (bf16[4,256,256]{2,1,0:T(8,128)(2,1)S(1)}, bf16[4,256,256]{2,1,0:T(8,128)(2,1)}, u32[]{:S(2)}) copy-start(bf16[4,256,256]{2,1,0:T(8,128)(2,1)} %constant.2.clone.tables) | copy-start | bytes 1572868
  4.3 11.7 %collective-permute-start.1 = (bf16[320,128]{1,0:T(8,128)(2,1)S(1)}, bf16[320,128]{1,0:T(8,128)(2,1)S(1)}, u32[]{:S(2)}, u32[]{:S(2)}) collective-permute-start(bf16[320,128]{1,0:T(8,128)(2,1)S(1)} %get-tuple-element.22), channel_id=1, source_target_pairs={{0,1},{1,2},{2,3},{3,0},{4,5},{5,6},{6,7},{7,4},{8,9},{9,10},{10,1... | collective-permute-start | bytes 245768 | tf_op jit(solution)/shard_map/ppermute | solution.py:395
  7.4 8.6 %collective-permute-start.2 = (bf16[320,128]{1,0:T(8,128)(2,1)S(1)}, bf16[320,128]{1,0:T(8,128)(2,1)S(1)}, u32[]{:S(2)}, u32[]{:S(2)}) collective-permute-start(bf16[320,128]{1,0:T(8,128)(2,1)S(1)} %get-tuple-element.23), channel_id=1, source_target_pairs={{0,2},{1,3},{2,0},{3,1},{4,6},{5,7},{6,4},{7,5},{8,10},{9,11},{10,... | collective-permute-start | bytes 245768 | tf_op jit(solution)/shard_map/ppermute | solution.py:395
  9.9 6.0 %collective-permute-start.3 = (bf16[320,128]{1,0:T(8,128)(2,1)S(1)}, bf16[320,128]{1,0:T(8,128)(2,1)S(1)}, u32[]{:S(2)}, u32[]{:S(2)}) collective-permute-start(bf16[320,128]{1,0:T(8,128)(2,1)S(1)} %get-tuple-element.24), channel_id=1, source_target_pairs={{0,3},{1,0},{2,1},{3,2},{4,7},{5,4},{6,5},{7,6},{8,11},{9,8},{10,9... | collective-permute-start | bytes 245768 | tf_op jit(solution)/shard_map/ppermute | solution.py:395
  11.3 4.7 %collective-permute-start = (f32[144,128]{1,0:T(8,128)S(1)}, f32[144,128]{1,0:T(8,128)S(1)}, u32[]{:S(2)}, u32[]{:S(2)}) collective-permute-start(f32[144,128]{1,0:T(8,128)S(1)} %get-tuple-element.20), channel_id=1, source_target_pairs={{0,4},{4,8},{8,12},{12,16},{16,20},{20,24},{24,28},{28,0},{1,5},{5... | collective-permute-start | bytes 221192 | tf_op jit(solution)/shard_map/ppermute | solution.py:401
  17.2 5.1 %collective-permute-start.4 = (bf16[256,128]{1,0:T(8,128)(2,1)S(1)}, bf16[256,128]{1,0:T(8,128)(2,1)S(1)}, u32[]{:S(2)}, u32[]{:S(2)}) collective-permute-start(bf16[256,128]{1,0:T(8,128)(2,1)S(1)} %get-tuple-element.25), channel_id=1, source_target_pairs={{0,4},{4,0},{8,12},{12,8},{16,20},{20,16},{24,28},{28,24},{1,5},{5... | collective-permute-start | bytes 196616 | tf_op jit(solution)/shard_map/ppermute | solution.py:401
  17.2 5.1 %collective-permute-start.5 = (bf16[256,128]{1,0:T(8,128)(2,1)S(1)}, bf16[256,128]{1,0:T(8,128)(2,1)S(1)}, u32[]{:S(2)}, u32[]{:S(2)}) collective-permute-start(bf16[256,128]{1,0:T(8,128)(2,1)S(1)} %get-tuple-element.26), channel_id=1, source_target_pairs={{0,28},{4,8},{8,4},{12,16},{16,12},{20,24},{24,20},{28,0},{1,29},{... | collective-permute-start | bytes 196616 | tf_op jit(solution)/shard_map/ppermute | solution.py:401
  25.1 7.3 %collective-permute-start.6 = (bf16[320,128]{1,0:T(8,128)(2,1)S(1)}, bf16[320,128]{1,0:T(8,128)(2,1)S(1)}, u32[]{:S(2)}, u32[]{:S(2)}) collective-permute-start(bf16[320,128]{1,0:T(8,128)(2,1)S(1)} %get-tuple-element.33), channel_id=1, source_target_pairs={{0,1},{1,2},{2,3},{3,0},{4,5},{5,6},{6,7},{7,4},{8,9},{9,10},{10,1... | collective-permute-start | bytes 245768 | tf_op jit(solution)/shard_map/ppermute | solution.py:395
  27.2 7.5 %collective-permute-start.7 = (bf16[320,128]{1,0:T(8,128)(2,1)S(1)}, bf16[320,128]{1,0:T(8,128)(2,1)S(1)}, u32[]{:S(2)}, u32[]{:S(2)}) collective-permute-start(bf16[320,128]{1,0:T(8,128)(2,1)S(1)} %get-tuple-element.34), channel_id=1, source_target_pairs={{0,2},{1,3},{2,0},{3,1},{4,6},{5,7},{6,4},{7,5},{8,10},{9,11},{10,... | collective-permute-start | bytes 245768 | tf_op jit(solution)/shard_map/ppermute | solution.py:395
  29.0 5.8 %collective-permute-start.8 = (bf16[320,128]{1,0:T(8,128)(2,1)S(1)}, bf16[320,128]{1,0:T(8,128)(2,1)S(1)}, u32[]{:S(2)}, u32[]{:S(2)}) collective-permute-start(bf16[320,128]{1,0:T(8,128)(2,1)S(1)} %get-tuple-element.35), channel_id=1, source_target_pairs={{0,3},{1,0},{2,1},{3,2},{4,7},{5,4},{6,5},{7,6},{8,11},{9,8},{10,9... | collective-permute-start | bytes 245768 | tf_op jit(solution)/shard_map/ppermute | solution.py:395

commit v3 on v2

--- a/solution.py
+++ b/solution.py
@@ -17,8 +17,8 @@
 EDGE_ROWS = 8
 
 f32, bf16, i32 = jnp.float32, jnp.bfloat16, jnp.int32
+VMEM = pl.BlockSpec(memory_space=pltpu.VMEM)
 SMEM = pl.BlockSpec(memory_space=pltpu.SMEM)
-VMEM = pl.BlockSpec(memory_space=pltpu.VMEM)
 HBM = pl.BlockSpec(memory_space=pltpu.HBM)
 
 
@@ -70,48 +70,63 @@
     return jnp.concatenate(parts, 0)
 
 
-def window_kernel(shifts, spots, counts, delta, beta, probe_in, measured_in, *refs):
-    outs = refs[:-8]
-    slot, probe, measured, slab_delta, slab_beta, scratch, near, far = refs[-8:]
-    copies = [
-        pltpu.make_async_copy(source, target, near.at[k])
-        for k, (source, target) in enumerate([(delta, slab_delta), (beta, slab_beta)])
+def window_message(d, shifts, slab_delta, slab_beta, scratch):
+    tile = slab_delta.shape[0] // 2
+    lane = lane_iota(tile)
+    mains, margins = [], []
+    for ref in (slab_delta, slab_beta):
+        main = margin = None
+        for z in range(2):
+            s = shifts[2 * d + z, 0]
+            rolled = pltpu.roll(ref[pl.ds(z, tile, stride=2), :], lax.rem(N - s, N), 1)
+            source = lane + s
+            inside = (source >= 0) & (source < N)
+            kept, out_of = jnp.where(inside, rolled, 0.0), jnp.where(inside, 0.0, rolled)
+            main = kept if z == 0 else main + kept
+            margin = out_of if z == 0 else margin + out_of
+        mains.append(main)
+        margins.append(margin)
+    scratch[2 * tile :, :] = jnp.zeros((scratch.shape[0] - 2 * tile, N), f32)
+    return packed_message(jnp.concatenate(mains, 0), jnp.concatenate(margins, 0), scratch)
+
+
+def first_kernel(angles, counts, *refs):
+    sources, targets = refs[:6], refs[6:11]
+    shifts, out, slot, scalar_shifts, scalar_spots, scratch, first_sems, second_sems = refs[11:]
+    spots, slab_delta, slab_beta, _, measured = targets
+    first = [
+        pltpu.make_async_copy(source, target, first_sems.at[k])
+        for k, (source, target) in enumerate(
+            [*zip(sources[:4], (scalar_shifts, scalar_spots, slab_delta, slab_beta))]
+        )
     ]
-    others = [
-        pltpu.make_async_copy(source, target, far.at[k])
-        for k, (source, target) in enumerate([(measured_in, measured), (probe_in, probe)])
+    second = [
+        pltpu.make_async_copy(source, target, second_sems.at[k])
+        for k, (source, target) in enumerate([(sources[1], spots), *zip(sources[4:], targets[3:])])
     ]
-    for copy in copies + others:
+    for copy in first + second:
         copy.start()
-    angles = len(outs)
-    tile = delta.shape[0] // 2
-    scratch[2 * tile :, :] = jnp.zeros((scratch.shape[0] - 2 * tile, N), f32)
+    for copy in first:
+        copy.wait()
     me = lax.axis_index("ang")
-    lane = lane_iota(tile)
-    for copy in copies:
-        copy.wait()
-    for d in [*range(1, angles), 0]:
+    for d in range(angles):
         angle = lax.rem(me + d, angles)
-        mains, margins = [], []
-        for ref in (slab_delta, slab_beta):
-            main = margin = None
-            for z in range(2):
-                s = shifts[z, angle]
-                rolled = pltpu.roll(ref[pl.ds(z, tile, stride=2), :], lax.rem(N - s, N), 1)
-                source = lane + s
-                inside = (source >= 0) & (source < N)
-                kept, out_of = jnp.where(inside, rolled, 0.0), jnp.where(inside, 0.0, rolled)
-                main = kept if z == 0 else main + kept
-                margin = out_of if z == 0 else margin + out_of
-            mains.append(main)
-            margins.append(margin)
-        outs[d][...] = packed_message(jnp.concatenate(mains, 0), jnp.concatenate(margins, 0), scratch)
-    for copy in others:
+        for z in range(2):
+            shifts[2 * d + z : 2 * d + z + 1, :] = jnp.full((1, N), scalar_shifts[z, angle], i32)
+    out[...] = window_message(1, shifts, slab_delta, slab_beta, scratch)
+    for copy in second:
         copy.wait()
     slot[0:N, :] = measured[0]
-    row = jnp.where(counts[0, 0] > 0, spots[0, 0], 0)
+    row = jnp.where(counts[0, 0] > 0, scalar_spots[0, 0], 0)
     slot[N : N + 8, :] = jnp.full((8, N), row, i32).astype(f32)
-    slot[N + 8 :, :] = jnp.full((8, N), spots[1, 0], i32).astype(f32)
+    slot[N + 8 :, :] = jnp.full((8, N), scalar_spots[1, 0], i32).astype(f32)
+
+
+def window_kernel(shifts, slab_delta, slab_beta, *refs):
+    outs, scratch = refs[:-1], refs[-1]
+    angles = len(outs) + 1
+    for out, d in zip(outs, [*range(2, angles), 0]):
+        out[...] = window_message(d, shifts, slab_delta, slab_beta, scratch)
 
 
 def slot_position(slot):
@@ -350,19 +365,17 @@
         out[...] = packed_message(jnp.concatenate(mains, 0), jnp.concatenate(margins, 0), scratch)
 
 
-def slab_kernel(shifts, *refs):
-    outs, received = refs[-2:], refs[:-2]
-    angles = len(received)
-    tile = outs[0].shape[0] // 2
-    me = lax.axis_index("ang")
+def slab_kernel(angles, steps, last, shifts, *refs):
+    refs, outs = (refs[:-2], refs[-2:]) if last else (refs[:-1], refs[-1:])
+    received, before = refs[: len(steps)], refs[len(steps) :]
+    tile = (received[0].shape[0] - PACK_ROWS) // 2
     lane = lane_iota(tile)
-    sums = [[None, None], [None, None]]
-    for d, ref in enumerate(received):
-        angle = lax.rem(me + (angles - d), angles)
+    sums = [[before[0][c, z] if before else None for z in range(2)] for c in range(2)]
+    for d, ref in zip(steps, received):
         message = ref[...].astype(f32)
         margins = margins_of(message, 2 * tile)
         for z in range(2):
-            s = shifts[z, angle]
+            s = shifts[2 * ((angles - d) % angles) + z, 0]
             target = lane + s
             inside = (target >= 0) & (target < N)
             for c in range(2):
@@ -372,7 +385,10 @@
                 sums[c][z] = value if sums[c][z] is None else sums[c][z] + value
     for c in range(2):
         for z in range(2):
-            outs[c][pl.ds(z, tile, stride=2), :] = sums[c][z]
+            if last:
+                outs[c][pl.ds(z, tile, stride=2), :] = sums[c][z]
+            else:
+                outs[0][c, z] = sums[c][z]
 
 
 def call(kernel, ins, outs, scratch=(), flops=0, bytes_accessed=0):
@@ -412,25 +428,40 @@
     shifts, spots = layer_shifts.T, positions[0].T
     tables = jnp.asarray(fourier_tables())
 
-    *windows, slot, probe, measured = call(
-        window_kernel,
-        [SMEM] * 3 + [HBM] * 4,
-        [message] * angles + [((N + 16, N), f32), (illumination_field.shape, f32), (amplitudes.shape[1:], f32)],
-        [slab, slab, padded, pltpu.SemaphoreType.DMA((2,)), pltpu.SemaphoreType.DMA((2,))],
-    )(
-        shifts,
-        spots,
-        scan_counts,
-        *(
-            pltpu.with_memory_space_constraint(value, pltpu.HBM)
-            for value in (delta_obj.reshape(slab), beta_obj.reshape(slab), illumination_field, amplitudes[0])
-        ),
-    )
+    arguments = [
+        pltpu.with_memory_space_constraint(value, pltpu.HBM)
+        for value in (
+            shifts,
+            spots,
+            delta_obj.reshape(slab),
+            beta_obj.reshape(slab),
+            illumination_field,
+            amplitudes[0],
+        )
+    ]
+    spots, slab_delta, slab_beta, probe, measured, shifts, following, slot = call(
+        functools.partial(first_kernel, angles),
+        [SMEM] + [HBM] * len(arguments),
+        [
+            *((value.shape, value.dtype) for value in arguments[1:]),
+            ((2 * angles, N), i32),
+            message,
+            ((N + 16, N), f32),
+        ],
+        [
+            *(pltpu.SMEM(value.shape, i32) for value in arguments[:2]),
+            padded,
+            pltpu.SemaphoreType.DMA((4,)),
+            pltpu.SemaphoreType.DMA((4,)),
+        ],
+    )(scan_counts, *arguments)
+    *others, own = call(window_kernel, [VMEM] * 3, [message] * (angles - 1), [padded])(shifts, slab_delta, slab_beta)
+    windows = [own, following, *others]
     received = exchange(windows)
     previous = on_rows(slot, lambda i: i + 1)
     proj, core, cross = call(
         assemble_kernel,
-        [SMEM] + [VMEM] * (angles + 1),
+        [VMEM] * (angles + 2),
         [field, halo, halo],
         [(angles, 2 * tile, N)],
     )(spots, previous, *received)
@@ -438,7 +469,7 @@
     cross = on_rows(cross, lambda i: i + 1 if i % 2 else i - 1)
     trans, inner = call(
         inner_kernel,
-        [SMEM] * 2 + [VMEM] * 4,
+        [VMEM, SMEM] + [VMEM] * 4,
         [field, field],
         [(N + 2 * SHIFT, N)],
         flops=3 * 10**9,
@@ -446,13 +477,22 @@
     )(spots, scan_counts, proj, probe, measured, tables)
     outgoing = call(
         edge_kernel,
-        [SMEM] * 2 + [VMEM] * 8,
+        [VMEM, SMEM] + [VMEM] * 8,
         [message] * angles,
         [field[0], (2, 2, tile + N, N), (2, 2 * tile + 8, N), padded],
     )(spots, scan_counts, previous, core, cross, trans, inner, probe, measured, tables)
-    grad_delta, grad_beta = call(slab_kernel, [SMEM] + [VMEM] * angles, [(slab, f32)] * 2)(
-        shifts, *exchange(outgoing)
-    )
+    received = exchange(outgoing)
+    early = list(range(angles - 1))
+    sums = call(
+        functools.partial(slab_kernel, angles, early, False),
+        [VMEM] * angles,
+        [((2, 2, tile, N), f32)],
+        flops=10**9,
+        bytes_accessed=10**6,
+    )(shifts, *received[:-1])[0]
+    grad_delta, grad_beta = call(
+        functools.partial(slab_kernel, angles, [angles - 1], True), [VMEM] * 3, [(slab, f32)] * 2
+    )(shifts, received[-1], sums)
     return grad_delta.reshape(tile, 2, N), grad_beta.reshape(tile, 2, N)
 
 

time: 36.6 us -> 34 us (0.929)
  Pallas kernels: 10.8 us -> 8.35 us
  waiting for transfers between devices: 9.85 us -> 11.4 us
  starting transfers between devices: 13.8 us -> 12.7 us
  local copies, waits for them, and re-layouts: 0.68 us -> 0.01 us
    pallas_call x5 -> x7, Pallas kernels: 10.8 us -> 8.35 us  [the longest x1 2.36 us: on_device(): call(inner_kernel, [VMEM, SMEM] + [VMEM] * 4, [field, field], [(N + 2 * S...]
    ppermute x6, waiting for transfers between devices: 5.17 us -> 6.04 us  [exchange(): lax.ppermute(messages[d], 'ang', [(i, (i + d) % count) for i in range(cou...]
    ppermute x3, waiting for transfers between devices: 4.68 us -> 5.37 us  [on_rows(): lax.ppermute(value, 'rows', [(i, target(i) % count) for i in range(count)])]
    unnamed x6 -> x2, local copies, waits for them, and re-layouts: 0.68 us -> 0.01 us
    ppermute x6, starting transfers between devices: 11.5 us -> 10.9 us  [exchange(): lax.ppermute(messages[d], 'ang', [(i, (i + d) % count) for i in range(cou...]
    ppermute x3, starting transfers between devices: 2.28 us -> 1.74 us  [on_rows(): lax.ppermute(value, 'rows', [(i, target(i) % count) for i in range(count)])]
  transfers between devices with their start and end apart: 9 -> 9, of which waited for: 4 -> 4; matrix products, arithmetic and copies ran while one was open for 0% -> 0% of each run, Pallas kernels for 8% -> 10%
where the time goes in v3:
time: 34 us; the launch traced here: 33.8 us
  starting transfers between devices  12.7 us (37%)
  waiting for transfers between devices  11.4 us (34%)
  Pallas kernels  8.35 us (25%)
  between operations  1.36 us (4%)
    ppermute x6, starting transfers between devices, exchange(): lax.ppermute(messages[d], 'ang', [(i, (i + d) % count) for i in range(cou...  10.9 us
    ppermute x6, waiting for transfers between devices, exchange(): lax.ppermute(messages[d], 'ang', [(i, (i + d) % count) for i in range(cou...  6.04 us
    ppermute x3, waiting for transfers between devices, on_rows(): lax.ppermute(value, 'rows', [(i, target(i) % count) for i in range(count)])  5.37 us
    pallas_call x1, Pallas kernels, on_device(): call(inner_kernel, [VMEM, SMEM] + [VMEM] * 4, [field, field], [(N + 2 * S...  2.36 us
    pallas_call x1, Pallas kernels, on_device(): call(edge_kernel, [VMEM, SMEM] + [VMEM] * 8, [message] * angles, [field[0...  2.26 us
    ppermute x3, starting transfers between devices, on_rows(): lax.ppermute(value, 'rows', [(i, target(i) % count) for i in range(count)])  1.74 us
    pallas_call x1, Pallas kernels, on_device(): call(functools.partial(first_kernel, angles), [SMEM] + [HBM] * len(argume...  1.41 us
    pallas_call x1, Pallas kernels, on_device(): call(functools.partial(slab_kernel, angles, [angles - 1], True), [VMEM] *...  0.87 us
  transfers between devices with their start and end apart: 9, of which 4 were waited for; matrix products, arithmetic and copies ran while one was open for 0% of the time, Pallas kernels for 10%

profile of v3, /device:TPU:0, one launch (start us, length us, event | category | flops | bytes accessed | tf_op | source)
XLA Modules:
  0.0 33.8 jit_solution(4225103050715906172)
XLA Ops:
  1.3 1.4 %shard_map.95 = (s32[2,4]{1,0:T(2,128)S(1)}, f32[272,128]{1,0:T(8,128)S(1)}, f32[272,128]{1,0:T(8,128)S(1)}, f32[2,128,128]{2,1,0:T(8,128)S(1)}, f32[4,128,128]{...) custom-call(s32[1,1]{1,0:T(1,128)S(6)} %copy.10.counts, ...), custom_call_target="tpu_custom_call" | custom-call | tf_op jit(solution)/shard_map/pallas_call | solution.py:442
  2.7 0.0 copy-start
  2.7 3.1 %collective-permute-start.1 = (bf16[320,128]{1,0:T(8,128)(2,1)S(1)}, bf16[320,128]{1,0:T(8,128)(2,1)S(1)}, u32[]{:S(2)}, u32[]{:S(2)}) collective-permute-start(bf16[320,128]{1,0:T(8,128)(2,1)S(1)} %get-tuple-element.30), channel_id=1, source_target_pairs={{0,1},{1,2},{2,3},{3,0},{4,5},{5,6},{6,7},{7,4},{8,9},{9,10},{10,1... | collective-permute-start | bytes 245768 | tf_op jit(solution)/shard_map/ppermute | solution.py:411
  5.8 0.5 %shard_map.96 = (bf16[320,128]{1,0:T(8,128)(2,1)S(1)}, bf16[320,128]{1,0:T(8,128)(2,1)S(1)}, bf16[320,128]{1,0:T(8,128)(2,1)S(1)}) custom-call(s32[8,128]{1,0:T(8,128)S(1)} %get-tuple-element.24.shifts, f32[272,128]{1,0:T(8,128)S(1)} %get-tuple-element.27.slab_delta, f32[272,128]{1,0:T(8,128)S(1)} %get-tuple-element.28.slab_beta), custom_call_target="tpu_custom_call" | custom-call | tf_op jit(solution)/shard_map/pallas_call | solution.py:458
  6.3 2.6 %collective-permute-start.2 = (bf16[320,128]{1,0:T(8,128)(2,1)S(1)}, bf16[320,128]{1,0:T(8,128)(2,1)S(1)}, u32[]{:S(2)}, u32[]{:S(2)}) collective-permute-start(bf16[320,128]{1,0:T(8,128)(2,1)S(1)} %get-tuple-element.31), channel_id=1, source_target_pairs={{0,2},{1,3},{2,0},{3,1},{4,6},{5,7},{6,4},{7,5},{8,10},{9,11},{10,... | collective-permute-start | bytes 245768 | tf_op jit(solution)/shard_map/ppermute | solution.py:411
  9.0 1.3 %collective-permute-start.3 = (bf16[320,128]{1,0:T(8,128)(2,1)S(1)}, bf16[320,128]{1,0:T(8,128)(2,1)S(1)}, u32[]{:S(2)}, u32[]{:S(2)}) collective-permute-start(bf16[320,128]{1,0:T(8,128)(2,1)S(1)} %get-tuple-element.32), channel_id=1, source_target_pairs={{0,3},{1,0},{2,1},{3,2},{4,7},{5,4},{6,5},{7,6},{8,11},{9,8},{10,9... | collective-permute-start | bytes 245768 | tf_op jit(solution)/shard_map/ppermute | solution.py:411
  10.3 0.0 collective-permute-start
  10.3 4.7 %collective-permute-done.slot = f32[144,128]{1,0:T(8,128)S(1)} collective-permute-done((f32[144,128]{1,0:T(8,128)S(1)}, f32[144,128]{1,0:T(8,128)S(1)}, u32[]{:S(2)}, u32[]{:S(2)}) %collective-permute-start) | collective-permute-done | bytes 73760 | tf_op jit(solution)/shard_map/ppermute | solution.py:417
  15.0 0.0 collective-permute-done.1.refs_1_
  15.0 0.6 %shard_map.97 = (f32[2,4,136,128]{3,2,1,0:T(8,128)S(1)}, bf16[256,128]{1,0:T(8,128)(2,1)S(1)}, bf16[256,128]{1,0:T(8,128)(2,1)S(1)}) custom-call(s32[2,4]{1,0:T(2,128)S(1)} %get-tuple-element.25.spots, f32[144,128]{1,0:T(8,128)S(1)} %collective-permute-done.slot, bf16[320,128]{1,0:T(8,128)(2,1)S(1)} %get-tuple-element.29.refs_0_, ...), custom_call_target="tpu_custom_call" | custom-call | tf_op jit(solution)/shard_map/pallas_call | solution.py:462
  15.6 0.1 collective-permute-start.4
  15.7 1.7 %collective-permute-start.5 = (bf16[256,128]{1,0:T(8,128)(2,1)S(1)}, bf16[256,128]{1,0:T(8,128)(2,1)S(1)}, u32[]{:S(2)}, u32[]{:S(2)}) collective-permute-start(bf16[256,128]{1,0:T(8,128)(2,1)S(1)} %get-tuple-element.34), channel_id=1, source_target_pairs={{0,28},{4,8},{8,4},{12,16},{16,12},{20,24},{24,20},{28,0},{1,29},{... | collective-permute-start | bytes 196616 | tf_op jit(solution)/shard_map/ppermute | solution.py:417
  17.4 2.4 %shard_map.98 = (f32[2,4,136,128]{3,2,1,0:T(8,128)S(1)}, f32[2,4,136,128]{3,2,1,0:T(8,128)S(1)}) custom-call(s32[2,4]{1,0:T(2,128)S(1)} %get-tuple-element.25.spots, s32[1,1]{1,0:T(1,128)S(6)} %copy.10.counts, f32[2,4,136,128]{3,2,1,0:T(8,128)S(1)} %get-tuple-element.35.proj, f32[2,128,128]{2,1,0:T(8,128)S(1)} %get-tuple-element.36.probe, ...), custom_call_target="tpu_custom_call" | custom-call | flops 3000000000 | bytes 3000000 | tf_op jit(solution)/shard_map/pallas_call | solution.py:470
  19.7 0.0 collective-permute-done.4.core
  19.7 0.7 %collective-permute-done.5.cross = bf16[256,128]{1,0:T(8,128)(2,1)S(1)} collective-permute-done((bf16[256,128]{1,0:T(8,128)(2,1)S(1)}, bf16[256,128]{1,0:T(8,128)(2,1)S(1)}, u32[]{:S(2)}, u32[]{:S(2)}) %collective-permute-start.5) | collective-permute-done | bytes 65568 | tf_op jit(solution)/shard_map/ppermute | solution.py:417
  20.4 2.3 %shard_map.99 = (bf16[320,128]{1,0:T(8,128)(2,1)S(1)}, bf16[320,128]{1,0:T(8,128)(2,1)S(1)}, bf16[320,128]{1,0:T(8,128)(2,1)S(1)}, bf16[320,128]{1,0:T(8,128)(2,1)S(1)}) custom-call(s32[2,4]{1,0:T(2,128)S(1)} %get-tuple-element.25.spots, s32[1,1]{1,0:T(1,128)S(6)} %copy.10.counts, f32[144,128]{1,0:T(8,128)S(1)} %collective-permute-done.slot, ...), custom_call_target="tpu_custom_call" | custom-call | tf_op jit(solution)/shard_map/pallas_call | solution.py:478
  22.7 1.4 %collective-permute-start.7 = (bf16[320,128]{1,0:T(8,128)(2,1)S(1)}, bf16[320,128]{1,0:T(8,128)(2,1)S(1)}, u32[]{:S(2)}, u32[]{:S(2)}) collective-permute-start(bf16[320,128]{1,0:T(8,128)(2,1)S(1)} %get-tuple-element.42), channel_id=1, source_target_pairs={{0,1},{1,2},{2,3},{3,0},{4,5},{5,6},{6,7},{7,4},{8,9},{9,10},{10,1... | collective-permute-start | bytes 245768 | tf_op jit(solution)/shard_map/ppermute | solution.py:411
  24.1 1.9 %collective-permute-start.8 = (bf16[320,128]{1,0:T(8,128)(2,1)S(1)}, bf16[320,128]{1,0:T(8,128)(2,1)S(1)}, u32[]{:S(2)}, u32[]{:S(2)}) collective-permute-start(bf16[320,128]{1,0:T(8,128)(2,1)S(1)} %get-tuple-element.43), channel_id=1, source_target_pairs={{0,2},{1,3},{2,0},{3,1},{4,6},{5,7},{6,4},{7,5},{8,10},{9,11},{10,... | collective-permute-start | bytes 245768 | tf_op jit(solution)/shard_map/ppermute | solution.py:411
  25.9 0.7 %collective-permute-start.6 = (bf16[320,128]{1,0:T(8,128)(2,1)S(1)}, bf16[320,128]{1,0:T(8,128)(2,1)S(1)}, u32[]{:S(2)}, u32[]{:S(2)}) collective-permute-start(bf16[320,128]{1,0:T(8,128)(2,1)S(1)} %get-tuple-element.40), channel_id=1, source_target_pairs={{0,3},{1,0},{2,1},{3,2},{4,7},{5,4},{6,5},{7,6},{8,11},{9,8},{10,9... | collective-permute-start | bytes 245768 | tf_op jit(solution)/shard_map/ppermute | solution.py:411
  26.6 3.4 %collective-permute-done.7.refs_1_ = bf16[320,128]{1,0:T(8,128)(2,1)S(1)} collective-permute-done((bf16[320,128]{1,0:T(8,128)(2,1)S(1)}, bf16[320,128]{1,0:T(8,128)(2,1)S(1)}, u32[]{:S(2)}, u32[]{:S(2)}) %collective-permute-start.7) | collective-permute-done | bytes 81952 | tf_op jit(solution)/shard_map/ppermute | solution.py:411
  29.9 2.7 %collective-permute-done.8.refs_2_ = bf16[320,128]{1,0:T(8,128)(2,1)S(1)} collective-permute-done((bf16[320,128]{1,0:T(8,128)(2,1)S(1)}, bf16[320,128]{1,0:T(8,128)(2,1)S(1)}, u32[]{:S(2)}, u32[]{:S(2)}) %collective-permute-start.8) | collective-permute-done | bytes 81952 | tf_op jit(solution)/shard_map/ppermute | solution.py:411
  32.6 0.3 shard_map.100.refs_1_
  32.9 0.0 collective-permute-done.6.refs_0_
  32.9 0.9 %shard_map.101 = (f32[272,128]{1,0:T(8,128)}, f32[272,128]{1,0:T(8,128)}) custom-call(s32[8,128]{1,0:T(8,128)S(1)} %get-tuple-element.24.shifts, bf16[320,128]{1,0:T(8,128)(2,1)S(1)} %collective-permute-done.6.refs_0_, f32[2,2,136,128]{3,2,1,0:T(8,128)S(1)} %shard_map.100.refs_1_), custom_call_target="tpu_custom_call" | custom-call | tf_op jit(solution)/shard_map/pallas_call | solution.py:493
  (3 shorter events, 0.0 us)
Async XLA Ops:
  2.7 14.7 %copy-start = (bf16[4,256,256]{2,1,0:T(8,128)(2,1)S(1)}, bf16[4,256,256]{2,1,0:T(8,128)(2,1)}, u32[]{:S(2)}) copy-start(bf16[4,256,256]{2,1,0:T(8,128)(2,1)} %constant.2.clone.tables) | copy-start | bytes 1572868
  2.7 12.3 %collective-permute-start.1 = (bf16[320,128]{1,0:T(8,128)(2,1)S(1)}, bf16[320,128]{1,0:T(8,128)(2,1)S(1)}, u32[]{:S(2)}, u32[]{:S(2)}) collective-permute-start(bf16[320,128]{1,0:T(8,128)(2,1)S(1)} %get-tuple-element.30), channel_id=1, source_target_pairs={{0,1},{1,2},{2,3},{3,0},{4,5},{5,6},{6,7},{7,4},{8,9},{9,10},{10,1... | collective-permute-start | bytes 245768 | tf_op jit(solution)/shard_map/ppermute | solution.py:411
  6.3 8.7 %collective-permute-start.2 = (bf16[320,128]{1,0:T(8,128)(2,1)S(1)}, bf16[320,128]{1,0:T(8,128)(2,1)S(1)}, u32[]{:S(2)}, u32[]{:S(2)}) collective-permute-start(bf16[320,128]{1,0:T(8,128)(2,1)S(1)} %get-tuple-element.31), channel_id=1, source_target_pairs={{0,2},{1,3},{2,0},{3,1},{4,6},{5,7},{6,4},{7,5},{8,10},{9,11},{10,... | collective-permute-start | bytes 245768 | tf_op jit(solution)/shard_map/ppermute | solution.py:411
  9.0 6.0 %collective-permute-start.3 = (bf16[320,128]{1,0:T(8,128)(2,1)S(1)}, bf16[320,128]{1,0:T(8,128)(2,1)S(1)}, u32[]{:S(2)}, u32[]{:S(2)}) collective-permute-start(bf16[320,128]{1,0:T(8,128)(2,1)S(1)} %get-tuple-element.32), channel_id=1, source_target_pairs={{0,3},{1,0},{2,1},{3,2},{4,7},{5,4},{6,5},{7,6},{8,11},{9,8},{10,9... | collective-permute-start | bytes 245768 | tf_op jit(solution)/shard_map/ppermute | solution.py:411
  10.3 4.7 %collective-permute-start = (f32[144,128]{1,0:T(8,128)S(1)}, f32[144,128]{1,0:T(8,128)S(1)}, u32[]{:S(2)}, u32[]{:S(2)}) collective-permute-start(f32[144,128]{1,0:T(8,128)S(1)} %get-tuple-element.26), channel_id=1, source_target_pairs={{0,4},{4,8},{8,12},{12,16},{16,20},{20,24},{24,28},{28,0},{1,5},{5... | collective-permute-start | bytes 221192 | tf_op jit(solution)/shard_map/ppermute | solution.py:417
  15.6 4.1 %collective-permute-start.4 = (bf16[256,128]{1,0:T(8,128)(2,1)S(1)}, bf16[256,128]{1,0:T(8,128)(2,1)S(1)}, u32[]{:S(2)}, u32[]{:S(2)}) collective-permute-start(bf16[256,128]{1,0:T(8,128)(2,1)S(1)} %get-tuple-element.33), channel_id=1, source_target_pairs={{0,4},{4,0},{8,12},{12,8},{16,20},{20,16},{24,28},{28,24},{1,5},{5... | collective-permute-start | bytes 196616 | tf_op jit(solution)/shard_map/ppermute | solution.py:417
  15.7 4.7 %collective-permute-start.5 = (bf16[256,128]{1,0:T(8,128)(2,1)S(1)}, bf16[256,128]{1,0:T(8,128)(2,1)S(1)}, u32[]{:S(2)}, u32[]{:S(2)}) collective-permute-start(bf16[256,128]{1,0:T(8,128)(2,1)S(1)} %get-tuple-element.34), channel_id=1, source_target_pairs={{0,28},{4,8},{8,4},{12,16},{16,12},{20,24},{24,20},{28,0},{1,29},{... | collective-permute-start | bytes 196616 | tf_op jit(solution)/shard_map/ppermute | solution.py:417
  22.7 7.2 %collective-permute-start.7 = (bf16[320,128]{1,0:T(8,128)(2,1)S(1)}, bf16[320,128]{1,0:T(8,128)(2,1)S(1)}, u32[]{:S(2)}, u32[]{:S(2)}) collective-permute-start(bf16[320,128]{1,0:T(8,128)(2,1)S(1)} %get-tuple-element.42), channel_id=1, source_target_pairs={{0,1},{1,2},{2,3},{3,0},{4,5},{5,6},{6,7},{7,4},{8,9},{9,10},{10,1... | collective-permute-start | bytes 245768 | tf_op jit(solution)/shard_map/ppermute | solution.py:411
  24.1 8.5 %collective-permute-start.8 = (bf16[320,128]{1,0:T(8,128)(2,1)S(1)}, bf16[320,128]{1,0:T(8,128)(2,1)S(1)}, u32[]{:S(2)}, u32[]{:S(2)}) collective-permute-start(bf16[320,128]{1,0:T(8,128)(2,1)S(1)} %get-tuple-element.43), channel_id=1, source_target_pairs={{0,2},{1,3},{2,0},{3,1},{4,6},{5,7},{6,4},{7,5},{8,10},{9,11},{10,... | collective-permute-start | bytes 245768 | tf_op jit(solution)/shard_map/ppermute | solution.py:411
  25.9 7.0 %collective-permute-start.6 = (bf16[320,128]{1,0:T(8,128)(2,1)S(1)}, bf16[320,128]{1,0:T(8,128)(2,1)S(1)}, u32[]{:S(2)}, u32[]{:S(2)}) collective-permute-start(bf16[320,128]{1,0:T(8,128)(2,1)S(1)} %get-tuple-element.40), channel_id=1, source_target_pairs={{0,3},{1,0},{2,1},{3,2},{4,7},{5,4},{6,5},{7,6},{8,11},{9,8},{10,9... | collective-permute-start | bytes 245768 | tf_op jit(solution)/shard_map/ppermute | solution.py:411

commit v4 on v3

--- a/solution.py
+++ b/solution.py
@@ -70,14 +70,14 @@
     return jnp.concatenate(parts, 0)
 
 
-def window_message(d, shifts, slab_delta, slab_beta, scratch):
+def window_message(shift_of, slab_delta, slab_beta, scratch):
     tile = slab_delta.shape[0] // 2
     lane = lane_iota(tile)
     mains, margins = [], []
     for ref in (slab_delta, slab_beta):
         main = margin = None
         for z in range(2):
-            s = shifts[2 * d + z, 0]
+            s = shift_of(z)
             rolled = pltpu.roll(ref[pl.ds(z, tile, stride=2), :], lax.rem(N - s, N), 1)
             source = lane + s
             inside = (source >= 0) & (source < N)
@@ -109,11 +109,12 @@
     for copy in first:
         copy.wait()
     me = lax.axis_index("ang")
+    first_angle = lax.rem(me + 1, angles)
+    out[...] = window_message(lambda z: scalar_shifts[z, first_angle], slab_delta, slab_beta, scratch)
     for d in range(angles):
         angle = lax.rem(me + d, angles)
         for z in range(2):
             shifts[2 * d + z : 2 * d + z + 1, :] = jnp.full((1, N), scalar_shifts[z, angle], i32)
-    out[...] = window_message(1, shifts, slab_delta, slab_beta, scratch)
     for copy in second:
         copy.wait()
     slot[0:N, :] = measured[0]
@@ -126,7 +127,7 @@
     outs, scratch = refs[:-1], refs[-1]
     angles = len(outs) + 1
     for out, d in zip(outs, [*range(2, angles), 0]):
-        out[...] = window_message(d, shifts, slab_delta, slab_beta, scratch)
+        out[...] = window_message(lambda z: shifts[2 * d + z, 0], slab_delta, slab_beta, scratch)
 
 
 def slot_position(slot):
@@ -142,18 +143,21 @@
     return lax.rem(lax.axis_index("rows"), 2) == 0
 
 
-def assemble_kernel(spots, slot, *refs):
-    proj, core, cross, margins = refs[-4:]
-    received = refs[:-4]
-    blocks = len(received)
+def unpack_kernel(blocks, steps, *refs):
+    received, (proj, margins) = refs[: len(steps)], refs[-2:]
     tile = proj.shape[2]
     me = lax.axis_index("ang")
-    for d, ref in enumerate(received):
+    for d, ref in zip(steps, received):
         block = lax.rem(me + (blocks - d), blocks)
         message = ref[...].astype(f32)
         proj[0, block] = message[:tile]
         proj[1, block] = message[tile : 2 * tile]
         margins[block] = margins_of(message, 2 * tile)
+
+
+def assemble_kernel(spots, slot, message, proj_in, margins_in, core, cross, proj, margins):
+    blocks, tile = proj.shape[1], proj.shape[2]
+    unpack_kernel(blocks, [blocks - 1], message, proj, margins)
     lane = lane_iota(tile)
     for block in range(blocks):
         before, after = (block - 1) % blocks, (block + 1) % blocks
@@ -268,6 +272,11 @@
     return pair
 
 
+def chain_back(patch, grad):
+    (tr, ti), (gr, gi) = patch, grad
+    return tr * gi - ti * gr, -(tr * gr + ti * gi)
+
+
 def add_patch(total, c, rows, value, lane, offset, first, second):
     placed = roll_lanes(value, offset)
     total[c, first, rows, :] += jnp.where(lane >= offset, placed, 0.0)
@@ -296,15 +305,35 @@
     for slot in range(1, slots):
         row = jnp.minimum(spots[0, slot], EDGE_ROWS)
         first, second, offset = block_of(spots[1, slot], blocks)
+        chained = chain_back(patches[slot - 1], grads[slot - 1])
         for c in range(2):
-            frame[SHIFT : SHIFT + N, :] = grads[slot - 1][c]
+            frame[SHIFT : SHIFT + N, :] = chained[c]
             add_patch(grad, c, slice(None), frame[pl.ds(SHIFT - row, tile), :], lane, offset, first, second)
 
 
-def edge_kernel(spots, counts, slot, core, cross, trans, inner, probe, measured, tables, *refs):
-    outs, (total, patch, frame, scratch) = refs[:-4], refs[-4:]
+def gradient_message(block, total, scratch):
+    blocks, tile = total.shape[1], total.shape[2]
+    scratch[2 * tile :, :] = jnp.zeros((scratch.shape[0] - 2 * tile, N), f32)
+    lane = lane_iota(tile)
+    before, after = lax.rem(block + (blocks - 1), blocks), lax.rem(block + 1, blocks)
+    mains, margins = [], []
+    for c in range(2):
+        mains.append(total[c, block])
+        margin = jnp.where(lane < SHIFT, total[c, after], 0.0)
+        margins.append(jnp.where(lane >= N - SHIFT, total[c, before], margin))
+    return packed_message(jnp.concatenate(mains, 0), jnp.concatenate(margins, 0), scratch)
+
+
+def cut_kernel(total, *refs):
+    outs, scratch = refs[:-1], refs[-1]
+    blocks = total.shape[1]
+    me = lax.axis_index("ang")
+    for out, d in zip(outs, [*range(2, blocks), 0]):
+        out[...] = gradient_message(lax.rem(me + d, blocks), total, scratch)
+
+
+def edge_kernel(spots, counts, slot, core, cross, trans, inner, probe, measured, tables, out, total, patch, frame, scratch):
     blocks, tile = trans.shape[1], trans.shape[2]
-    scratch[2 * tile :, :] = jnp.zeros((scratch.shape[0] - 2 * tile, N), f32)
     even = is_even()
     own_row, own_column = spots[0, 0], spots[1, 0]
     prev_row, prev_column = slot_position(slot)
@@ -335,34 +364,21 @@
     ]
     weights = [jnp.where(flag, 1.0, 0.0).astype(f32) for flag in (counts[0, 0] > 0, reaches)]
     grads = scan_gradients(patches, [measured[0], slot[0:N, :]], weights, probe, tables)
-    total[...] = inner[...]
+    chained = [chain_back(pair, grad) for pair, grad in zip(patches, grads)]
+    first, second, offset = own_block
     for c in range(2):
         frame[c, 0:tile, :] = jnp.zeros((tile, N), f32)
-        frame[c, tile : tile + N, :] = grads[0][c]
+        frame[c, tile : tile + N, :] = chained[0][c]
         frame[c, tile + N :, :] = jnp.zeros((frame.shape[1] - tile - N, N), f32)
-    for c in range(2):
-        add_patch(total, c, slice(None), frame[c, pl.ds(tile - own_row, tile), :], lane_iota(tile), offset=own_block[2], first=own_block[0], second=own_block[1])
-    for c in range(2):
-        frame[c, 0:N, :] = grads[1][c]
+        rows = frame[c, pl.ds(tile - own_row, tile), :]
+        add_patch(total, c, slice(None), rows, lane_iota(tile), offset, first, second)
+    first, second, offset = prev_block
+    for c in range(2):
+        frame[c, 0:N, :] = chained[1][c]
         frame[c, N : 2 * N, :] = jnp.zeros((N, N), f32)
-    for c in range(2):
-        add_patch(total, c, slice(0, N), frame[c, pl.ds(tile - start, N), :], lane_iota(N), offset=prev_block[2], first=prev_block[0], second=prev_block[1])
-    for block in range(blocks):
-        tr, ti = trans[0, block], trans[1, block]
-        gr, gi = total[0, block], total[1, block]
-        total[0, block] = tr * gi - ti * gr
-        total[1, block] = -(tr * gr + ti * gi)
-    me = lax.axis_index("ang")
-    lane = lane_iota(tile)
-    for d, out in enumerate(outs):
-        block = lax.rem(me + d, blocks)
-        before, after = lax.rem(block + (blocks - 1), blocks), lax.rem(block + 1, blocks)
-        mains, margins = [], []
-        for c in range(2):
-            mains.append(total[c, block])
-            margin = jnp.where(lane < SHIFT, total[c, after], 0.0)
-            margins.append(jnp.where(lane >= N - SHIFT, total[c, before], margin))
-        out[...] = packed_message(jnp.concatenate(mains, 0), jnp.concatenate(margins, 0), scratch)
+        rows = frame[c, pl.ds(tile - start, N), :]
+        add_patch(total, c, slice(0, N), rows, lane_iota(N), offset, first, second)
+    out[...] = gradient_message(lax.rem(lax.axis_index("ang") + 1, blocks), total, scratch)
 
 
 def slab_kernel(angles, steps, last, shifts, *refs):
@@ -391,7 +407,7 @@
                 outs[0][c, z] = sums[c][z]
 
 
-def call(kernel, ins, outs, scratch=(), flops=0, bytes_accessed=0):
+def call(kernel, ins, outs, scratch=(), flops=0, bytes_accessed=0, aliases=()):
     scratch = [pltpu.VMEM(item, f32) if isinstance(item, tuple) else item for item in scratch]
     return pl.pallas_call(
         kernel,
@@ -399,6 +415,7 @@
         out_specs=[VMEM] * len(outs),
         out_shape=[jax.ShapeDtypeStruct(shape, dtype) for shape, dtype in outs],
         scratch_shapes=scratch,
+        input_output_aliases=dict(aliases),
         compiler_params=pltpu.CompilerParams(vmem_limit_bytes=32 * 1024 * 1024),
         cost_estimate=pl.CostEstimate(flops=flops, bytes_accessed=bytes_accessed, transcendentals=0),
     )
@@ -459,12 +476,18 @@
     windows = [own, following, *others]
     received = exchange(windows)
     previous = on_rows(slot, lambda i: i + 1)
-    proj, core, cross = call(
-        assemble_kernel,
-        [VMEM] * (angles + 2),
-        [field, halo, halo],
-        [(angles, 2 * tile, N)],
-    )(spots, previous, *received)
+    rows = ((angles, 2 * tile, N), f32)
+    early = list(range(angles - 1))
+    partly = call(
+        functools.partial(unpack_kernel, angles, early),
+        [VMEM] * (angles - 1),
+        [field, rows],
+        flops=10**9,
+        bytes_accessed=10**6,
+    )(*received[:-1])
+    core, cross, proj, _ = call(
+        assemble_kernel, [VMEM] * 5, [halo, halo, field, rows], aliases={3: 2, 4: 3}
+    )(spots, previous, received[-1], *partly)
     core = on_rows(core, lambda i: i ^ 1)
     cross = on_rows(cross, lambda i: i + 1 if i % 2 else i - 1)
     trans, inner = call(
@@ -475,14 +498,15 @@
         flops=3 * 10**9,
         bytes_accessed=3 * 10**6,
     )(spots, scan_counts, proj, probe, measured, tables)
-    outgoing = call(
+    following, total = call(
         edge_kernel,
         [VMEM, SMEM] + [VMEM] * 8,
-        [message] * angles,
-        [field[0], (2, 2, tile + N, N), (2, 2 * tile + 8, N), padded],
+        [message, field],
+        [(2, 2, tile + N, N), (2, 2 * tile + 8, N), padded],
+        aliases={6: 1},
     )(spots, scan_counts, previous, core, cross, trans, inner, probe, measured, tables)
-    received = exchange(outgoing)
-    early = list(range(angles - 1))
+    *others, own = call(cut_kernel, [VMEM], [message] * (angles - 1), [padded])(total)
+    received = exchange([own, following, *others])
     sums = call(
         functools.partial(slab_kernel, angles, early, False),
         [VMEM] * angles,

time: 34 us -> 33.4 us (0.982)
  waiting for transfers between devices: 11.4 us -> 9.75 us
  starting transfers between devices: 12.7 us -> 13.8 us
    ppermute x3, waiting for transfers between devices: 5.37 us -> 0.01 us  [on_rows(): lax.ppermute(value, 'rows', [(i, target(i) % count) for i in range(count)])]
    ppermute x6, waiting for transfers between devices: 6.04 us -> 9.75 us  [exchange(): lax.ppermute(messages[d], 'ang', [(i, (i + d) % count) for i in range(cou...]
    ppermute x3, starting transfers between devices: 1.74 us -> 2.62 us  [on_rows(): lax.ppermute(value, 'rows', [(i, target(i) % count) for i in range(count)])]
    pallas_call x2 -> x4, Pallas kernels: 2.86 us -> 2.8 us  [the longest x1 1.96 us: on_device(): call(edge_kernel, [VMEM, SMEM] + [VMEM] * 8, [message, field], [(2, 2, ti...]
  transfers between devices with their start and end apart: 9 -> 9, of which waited for: 4 -> 3; matrix products, arithmetic and copies ran while one was open for 0% -> 0% of each run, Pallas kernels for 10% -> 10%
where the time goes in v4:
time: 33.4 us; the launch traced here: 33.2 us
  starting transfers between devices  13.8 us (41%)
  waiting for transfers between devices  9.75 us (29%)
  Pallas kernels  8.25 us (25%)
  between operations  1.37 us (4%)
    ppermute x6, starting transfers between devices, exchange(): lax.ppermute(messages[d], 'ang', [(i, (i + d) % count) for i in range(cou...  11.2 us
    ppermute x6, waiting for transfers between devices, exchange(): lax.ppermute(messages[d], 'ang', [(i, (i + d) % count) for i in range(cou...  9.75 us
    ppermute x3, starting transfers between devices, on_rows(): lax.ppermute(value, 'rows', [(i, target(i) % count) for i in range(count)])  2.62 us
    pallas_call x1, Pallas kernels, on_device(): call(inner_kernel, [VMEM, SMEM] + [VMEM] * 4, [field, field], [(N + 2 * S...  2.36 us
    pallas_call x1, Pallas kernels, on_device(): call(edge_kernel, [VMEM, SMEM] + [VMEM] * 8, [message, field], [(2, 2, ti...  1.96 us
    pallas_call x1, Pallas kernels, on_device(): call(functools.partial(first_kernel, angles), [SMEM] + [HBM] * len(argume...  1.36 us
    pallas_call x1, Pallas kernels, on_device(): call(functools.partial(slab_kernel, angles, [angles - 1], True), [VMEM] *...  0.87 us
  transfers between devices with their start and end apart: 9, of which 3 were waited for; matrix products, arithmetic and copies ran while one was open for 0% of the time, Pallas kernels for 10%

profile of v4, /device:TPU:0, one launch (start us, length us, event | category | flops | bytes accessed | tf_op | source)
XLA Modules:
  0.0 33.2 jit_solution(7587968960265345188)
XLA Ops:
  1.3 1.4 %shard_map.95 = (s32[2,4]{1,0:T(2,128)S(1)}, f32[272,128]{1,0:T(8,128)S(1)}, f32[272,128]{1,0:T(8,128)S(1)}, f32[2,128,128]{2,1,0:T(8,128)S(1)}, f32[4,128,128]{...) custom-call(s32[1,1]{1,0:T(1,128)S(6)} %copy.16.counts, ...), custom_call_target="tpu_custom_call" | custom-call | tf_op jit(solution)/shard_map/pallas_call | solution.py:459
  2.6 3.1 %collective-permute-start.2 = (bf16[320,128]{1,0:T(8,128)(2,1)S(1)}, bf16[320,128]{1,0:T(8,128)(2,1)S(1)}, u32[]{:S(2)}, u32[]{:S(2)}) collective-permute-start(bf16[320,128]{1,0:T(8,128)(2,1)S(1)} %get-tuple-element.34), channel_id=1, source_target_pairs={{0,1},{1,2},{2,3},{3,0},{4,5},{5,6},{6,7},{7,4},{8,9},{9,10},{10,1... | collective-permute-start | bytes 245768 | tf_op jit(solution)/shard_map/ppermute | solution.py:428
  5.7 0.5 %shard_map.96 = (bf16[320,128]{1,0:T(8,128)(2,1)S(1)}, bf16[320,128]{1,0:T(8,128)(2,1)S(1)}, bf16[320,128]{1,0:T(8,128)(2,1)S(1)}) custom-call(s32[8,128]{1,0:T(8,128)S(1)} %get-tuple-element.27.shifts, f32[272,128]{1,0:T(8,128)S(1)} %get-tuple-element.30.slab_delta, f32[272,128]{1,0:T(8,128)S(1)} %get-tuple-element.31.slab_beta), custom_call_target="tpu_custom_call" | custom-call | tf_op jit(solution)/shard_map/pallas_call | solution.py:475
  6.3 2.6 %collective-permute-start.3 = (bf16[320,128]{1,0:T(8,128)(2,1)S(1)}, bf16[320,128]{1,0:T(8,128)(2,1)S(1)}, u32[]{:S(2)}, u32[]{:S(2)}) collective-permute-start(bf16[320,128]{1,0:T(8,128)(2,1)S(1)} %get-tuple-element.35), channel_id=1, source_target_pairs={{0,2},{1,3},{2,0},{3,1},{4,6},{5,7},{6,4},{7,5},{8,10},{9,11},{10,... | collective-permute-start | bytes 245768 | tf_op jit(solution)/shard_map/ppermute | solution.py:428
  8.9 0.0 collective-permute-start
  8.9 1.3 %collective-permute-start.1 = (bf16[320,128]{1,0:T(8,128)(2,1)S(1)}, bf16[320,128]{1,0:T(8,128)(2,1)S(1)}, u32[]{:S(2)}, u32[]{:S(2)}) collective-permute-start(bf16[320,128]{1,0:T(8,128)(2,1)S(1)} %get-tuple-element.32), channel_id=1, source_target_pairs={{0,3},{1,0},{2,1},{3,2},{4,7},{5,4},{6,5},{7,6},{8,11},{9,8},{10,9... | collective-permute-start | bytes 245768 | tf_op jit(solution)/shard_map/ppermute | solution.py:428
  10.2 0.0 collective-permute-done.2.refs_1_
  10.3 3.6 %collective-permute-done.3.refs_2_ = bf16[320,128]{1,0:T(8,128)(2,1)S(1)} collective-permute-done((bf16[320,128]{1,0:T(8,128)(2,1)S(1)}, bf16[320,128]{1,0:T(8,128)(2,1)S(1)}, u32[]{:S(2)}, u32[]{:S(2)}) %collective-permute-start.3) | collective-permute-done | bytes 81952 | tf_op jit(solution)/shard_map/ppermute | solution.py:428
  13.9 0.1 shard_map.97
  14.0 0.0 collective-permute-done.slot
  14.0 0.8 %collective-permute-done.1.message = bf16[320,128]{1,0:T(8,128)(2,1)S(1)} collective-permute-done((bf16[320,128]{1,0:T(8,128)(2,1)S(1)}, bf16[320,128]{1,0:T(8,128)(2,1)S(1)}, u32[]{:S(2)}, u32[]{:S(2)}) %collective-permute-start.1) | collective-permute-done | bytes 81952 | tf_op jit(solution)/shard_map/ppermute | solution.py:428
  14.8 0.5 %shard_map.98 = (bf16[256,128]{1,0:T(8,128)(2,1)S(1)}, bf16[256,128]{1,0:T(8,128)(2,1)S(1)}, f32[2,4,136,128]{3,2,1,0:T(8,128)S(1)}, f32[4,272,128]{2,1,0:T(8,128)S(1)}) custom-call(s32[2,4]{1,0:T(2,128)S(1)} %get-tuple-element.28.spots, f32[144,128]{1,0:T(8,128)S(1)} %collective-permute-done.slot, ...), custom_call_target="tpu_custom_call", output_to_operand_aliasing={{2}: (3, {}), {3}: (4, {})} | custom-call | tf_op jit(solution)/shard_map/pallas_call | solution.py:488
  15.4 0.2 collective-permute-start.4
  15.6 2.4 %collective-permute-start.5 = (bf16[256,128]{1,0:T(8,128)(2,1)S(1)}, bf16[256,128]{1,0:T(8,128)(2,1)S(1)}, u32[]{:S(2)}, u32[]{:S(2)}) collective-permute-start(bf16[256,128]{1,0:T(8,128)(2,1)S(1)} %get-tuple-element.39), channel_id=1, source_target_pairs={{0,28},{4,8},{8,4},{12,16},{16,12},{20,24},{24,20},{28,0},{1,29},{... | collective-permute-start | bytes 196616 | tf_op jit(solution)/shard_map/ppermute | solution.py:434
  18.0 2.4 %shard_map.99 = (f32[2,4,136,128]{3,2,1,0:T(8,128)S(1)}, f32[2,4,136,128]{3,2,1,0:T(8,128)S(1)}) custom-call(s32[2,4]{1,0:T(2,128)S(1)} %get-tuple-element.28.spots, s32[1,1]{1,0:T(1,128)S(6)} %copy.16.counts, f32[2,4,136,128]{3,2,1,0:T(8,128)S(1)} %get-tuple-element.40.proj, f32[2,128,128]{2,1,0:T(8,128)S(1)} %get-tuple-element.41.probe, ...), custom_call_target="tpu_custom_call" | custom-call | flops 3000000000 | bytes 3000000 | tf_op jit(solution)/shard_map/pallas_call | solution.py:493
  20.4 0.0 collective-permute-done.4.core
  20.4 2.0 %shard_map.100 = (bf16[320,128]{1,0:T(8,128)(2,1)S(1)}, f32[2,4,136,128]{3,2,1,0:T(8,128)S(1)}) custom-call(s32[2,4]{1,0:T(2,128)S(1)} %get-tuple-element.28.spots, s32[1,1]{1,0:T(1,128)S(6)} %copy.16.counts, f32[144,128]{1,0:T(8,128)S(1)} %collective-permute-done.slot, ...), custom_call_target="tpu_custom_call", output_to_operand_aliasing={{1}: (6, {})} | custom-call | tf_op jit(solution)/shard_map/pallas_call | solution.py:501
  22.3 0.2 shard_map.101
  22.5 0.3 collective-permute-start.8
  22.8 3.0 %collective-permute-start.7 = (bf16[320,128]{1,0:T(8,128)(2,1)S(1)}, bf16[320,128]{1,0:T(8,128)(2,1)S(1)}, u32[]{:S(2)}, u32[]{:S(2)}) collective-permute-start(bf16[320,128]{1,0:T(8,128)(2,1)S(1)} %get-tuple-element.48), channel_id=1, source_target_pairs={{0,1},{1,2},{2,3},{3,0},{4,5},{5,6},{6,7},{7,4},{8,9},{9,10},{10,1... | collective-permute-start | bytes 245768 | tf_op jit(solution)/shard_map/ppermute | solution.py:428
  25.9 0.8 %collective-permute-start.6 = (bf16[320,128]{1,0:T(8,128)(2,1)S(1)}, bf16[320,128]{1,0:T(8,128)(2,1)S(1)}, u32[]{:S(2)}, u32[]{:S(2)}) collective-permute-start(bf16[320,128]{1,0:T(8,128)(2,1)S(1)} %get-tuple-element.46), channel_id=1, source_target_pairs={{0,3},{1,0},{2,1},{3,2},{4,7},{5,4},{6,5},{7,6},{8,11},{9,8},{10,9... | collective-permute-start | bytes 245768 | tf_op jit(solution)/shard_map/ppermute | solution.py:428
  26.7 5.3 %collective-permute-done.8.refs_2_ = bf16[320,128]{1,0:T(8,128)(2,1)S(1)} collective-permute-done((bf16[320,128]{1,0:T(8,128)(2,1)S(1)}, bf16[320,128]{1,0:T(8,128)(2,1)S(1)}, u32[]{:S(2)}, u32[]{:S(2)}) %collective-permute-start.8) | collective-permute-done | bytes 81952 | tf_op jit(solution)/shard_map/ppermute | solution.py:428
  32.0 0.3 shard_map.102.refs_1_
  32.3 0.9 %shard_map.103 = (f32[272,128]{1,0:T(8,128)}, f32[272,128]{1,0:T(8,128)}) custom-call(s32[8,128]{1,0:T(8,128)S(1)} %get-tuple-element.27.shifts, bf16[320,128]{1,0:T(8,128)(2,1)S(1)} %collective-permute-done.6.refs_0_, f32[2,2,136,128]{3,2,1,0:T(8,128)S(1)} %shard_map.102.refs_1_), custom_call_target="tpu_custom_call" | custom-call | tf_op jit(solution)/shard_map/pallas_call | solution.py:517
  (5 shorter events, 0.0 us)
Async XLA Ops:
  2.6 7.6 %collective-permute-start.2 = (bf16[320,128]{1,0:T(8,128)(2,1)S(1)}, bf16[320,128]{1,0:T(8,128)(2,1)S(1)}, u32[]{:S(2)}, u32[]{:S(2)}) collective-permute-start(bf16[320,128]{1,0:T(8,128)(2,1)S(1)} %get-tuple-element.34), channel_id=1, source_target_pairs={{0,1},{1,2},{2,3},{3,0},{4,5},{5,6},{6,7},{7,4},{8,9},{9,10},{10,1... | collective-permute-start | bytes 245768 | tf_op jit(solution)/shard_map/ppermute | solution.py:428
  6.3 7.6 %collective-permute-start.3 = (bf16[320,128]{1,0:T(8,128)(2,1)S(1)}, bf16[320,128]{1,0:T(8,128)(2,1)S(1)}, u32[]{:S(2)}, u32[]{:S(2)}) collective-permute-start(bf16[320,128]{1,0:T(8,128)(2,1)S(1)} %get-tuple-element.35), channel_id=1, source_target_pairs={{0,2},{1,3},{2,0},{3,1},{4,6},{5,7},{6,4},{7,5},{8,10},{9,11},{10,... | collective-permute-start | bytes 245768 | tf_op jit(solution)/shard_map/ppermute | solution.py:428
  8.9 5.1 %collective-permute-start = (f32[144,128]{1,0:T(8,128)S(1)}, f32[144,128]{1,0:T(8,128)S(1)}, u32[]{:S(2)}, u32[]{:S(2)}) collective-permute-start(f32[144,128]{1,0:T(8,128)S(1)} %get-tuple-element.29), channel_id=1, source_target_pairs={{0,4},{4,8},{8,12},{12,16},{16,20},{20,24},{24,28},{28,0},{1,5},{5... | collective-permute-start | bytes 221192 | tf_op jit(solution)/shard_map/ppermute | solution.py:434
  8.9 5.9 %collective-permute-start.1 = (bf16[320,128]{1,0:T(8,128)(2,1)S(1)}, bf16[320,128]{1,0:T(8,128)(2,1)S(1)}, u32[]{:S(2)}, u32[]{:S(2)}) collective-permute-start(bf16[320,128]{1,0:T(8,128)(2,1)S(1)} %get-tuple-element.32), channel_id=1, source_target_pairs={{0,3},{1,0},{2,1},{3,2},{4,7},{5,4},{6,5},{7,6},{8,11},{9,8},{10,9... | collective-permute-start | bytes 245768 | tf_op jit(solution)/shard_map/ppermute | solution.py:428
  14.8 3.2 %copy-start = (bf16[4,256,256]{2,1,0:T(8,128)(2,1)S(1)}, bf16[4,256,256]{2,1,0:T(8,128)(2,1)}, u32[]{:S(2)}) copy-start(bf16[4,256,256]{2,1,0:T(8,128)(2,1)} %constant.2.clone.tables) | copy-start | bytes 1572868
  15.4 5.0 %collective-permute-start.4 = (bf16[256,128]{1,0:T(8,128)(2,1)S(1)}, bf16[256,128]{1,0:T(8,128)(2,1)S(1)}, u32[]{:S(2)}, u32[]{:S(2)}) collective-permute-start(bf16[256,128]{1,0:T(8,128)(2,1)S(1)} %get-tuple-element.38), channel_id=1, source_target_pairs={{0,4},{4,0},{8,12},{12,8},{16,20},{20,16},{24,28},{28,24},{1,5},{5... | collective-permute-start | bytes 196616 | tf_op jit(solution)/shard_map/ppermute | solution.py:434
  15.6 4.8 %collective-permute-start.5 = (bf16[256,128]{1,0:T(8,128)(2,1)S(1)}, bf16[256,128]{1,0:T(8,128)(2,1)S(1)}, u32[]{:S(2)}, u32[]{:S(2)}) collective-permute-start(bf16[256,128]{1,0:T(8,128)(2,1)S(1)} %get-tuple-element.39), channel_id=1, source_target_pairs={{0,28},{4,8},{8,4},{12,16},{16,12},{20,24},{24,20},{28,0},{1,29},{... | collective-permute-start | bytes 196616 | tf_op jit(solution)/shard_map/ppermute | solution.py:434
  22.5 9.4 %collective-permute-start.8 = (bf16[320,128]{1,0:T(8,128)(2,1)S(1)}, bf16[320,128]{1,0:T(8,128)(2,1)S(1)}, u32[]{:S(2)}, u32[]{:S(2)}) collective-permute-start(bf16[320,128]{1,0:T(8,128)(2,1)S(1)} %get-tuple-element.49), channel_id=1, source_target_pairs={{0,2},{1,3},{2,0},{3,1},{4,6},{5,7},{6,4},{7,5},{8,10},{9,11},{10,... | collective-permute-start | bytes 245768 | tf_op jit(solution)/shard_map/ppermute | solution.py:428
  22.8 9.1 %collective-permute-start.7 = (bf16[320,128]{1,0:T(8,128)(2,1)S(1)}, bf16[320,128]{1,0:T(8,128)(2,1)S(1)}, u32[]{:S(2)}, u32[]{:S(2)}) collective-permute-start(bf16[320,128]{1,0:T(8,128)(2,1)S(1)} %get-tuple-element.48), channel_id=1, source_target_pairs={{0,1},{1,2},{2,3},{3,0},{4,5},{5,6},{6,7},{7,4},{8,9},{9,10},{10,1... | collective-permute-start | bytes 245768 | tf_op jit(solution)/shard_map/ppermute | solution.py:428
  25.9 6.4 %collective-permute-start.6 = (bf16[320,128]{1,0:T(8,128)(2,1)S(1)}, bf16[320,128]{1,0:T(8,128)(2,1)S(1)}, u32[]{:S(2)}, u32[]{:S(2)}) collective-permute-start(bf16[320,128]{1,0:T(8,128)(2,1)S(1)} %get-tuple-element.46), channel_id=1, source_target_pairs={{0,3},{1,0},{2,1},{3,2},{4,7},{5,4},{6,5},{7,6},{8,11},{9,8},{10,9... | collective-permute-start | bytes 245768 | tf_op jit(solution)/shard_map/ppermute | solution.py:428

commit v5 on v4

--- a/solution.py
+++ b/solution.py
@@ -13,7 +13,7 @@
 N = 128
 SHIFT = 8
 AMP_FLOOR = 0.1
-PACK_ROWS = 48
+PACK_ROWS = 40
 EDGE_ROWS = 8
 
 f32, bf16, i32 = jnp.float32, jnp.bfloat16, jnp.int32
@@ -90,44 +90,60 @@
     return packed_message(jnp.concatenate(mains, 0), jnp.concatenate(margins, 0), scratch)
 
 
-def first_kernel(angles, counts, *refs):
-    sources, targets = refs[:6], refs[6:11]
-    shifts, out, slot, scalar_shifts, scalar_spots, scratch, first_sems, second_sems = refs[11:]
-    spots, slab_delta, slab_beta, _, measured = targets
-    first = [
-        pltpu.make_async_copy(source, target, first_sems.at[k])
+def first_kernel(
+    angles, shifts_in, spots_in, delta, beta, measured_in,
+    slab_delta, slab_beta, shifts, out, slot, scalar_shifts, scalar_spots, scratch, sems,
+):
+    copies = [
+        pltpu.make_async_copy(source, target, sems.at[k])
         for k, (source, target) in enumerate(
-            [*zip(sources[:4], (scalar_shifts, scalar_spots, slab_delta, slab_beta))]
+            [
+                (shifts_in, scalar_shifts),
+                (spots_in, scalar_spots),
+                (delta, slab_delta),
+                (beta, slab_beta),
+                (measured_in.at[0], slot.at[0:N]),
+            ]
         )
     ]
-    second = [
-        pltpu.make_async_copy(source, target, second_sems.at[k])
-        for k, (source, target) in enumerate([(sources[1], spots), *zip(sources[4:], targets[3:])])
-    ]
-    for copy in first + second:
+    for copy in copies:
         copy.start()
-    for copy in first:
+    me = lax.axis_index("ang")
+    for copy in copies[:2]:
         copy.wait()
-    me = lax.axis_index("ang")
-    first_angle = lax.rem(me + 1, angles)
-    out[...] = window_message(lambda z: scalar_shifts[z, first_angle], slab_delta, slab_beta, scratch)
     for d in range(angles):
         angle = lax.rem(me + d, angles)
         for z in range(2):
             shifts[2 * d + z : 2 * d + z + 1, :] = jnp.full((1, N), scalar_shifts[z, angle], i32)
-    for copy in second:
+    slot[N : N + 8, :] = jnp.full((8, N), scalar_spots[0, 0], i32).astype(f32)
+    slot[N + 8 :, :] = jnp.full((8, N), scalar_spots[1, 0], i32).astype(f32)
+    following = lax.rem(me + 1, angles)
+    for copy in copies[2:]:
         copy.wait()
-    slot[0:N, :] = measured[0]
-    row = jnp.where(counts[0, 0] > 0, scalar_spots[0, 0], 0)
-    slot[N : N + 8, :] = jnp.full((8, N), row, i32).astype(f32)
-    slot[N + 8 :, :] = jnp.full((8, N), scalar_spots[1, 0], i32).astype(f32)
+    out[...] = window_message(lambda z: scalar_shifts[z, following], slab_delta, slab_beta, scratch)
 
 
 def window_kernel(shifts, slab_delta, slab_beta, *refs):
     outs, scratch = refs[:-1], refs[-1]
-    angles = len(outs) + 1
-    for out, d in zip(outs, [*range(2, angles), 0]):
+    for k, out in enumerate(outs):
+        d = k + 2
         out[...] = window_message(lambda z: shifts[2 * d + z, 0], slab_delta, slab_beta, scratch)
+
+
+def load_kernel(
+    counts_in, shifts, slab_delta, slab_beta, _, spots_in, probe_in, measured_in,
+    own, counts, spots, probe, measured, scratch, sems,
+):
+    copies = [
+        pltpu.make_async_copy(source, target, sems.at[k])
+        for k, (source, target) in enumerate([(spots_in, spots), (probe_in, probe), (measured_in, measured)])
+    ]
+    for copy in copies:
+        copy.start()
+    own[...] = window_message(lambda z: shifts[z, 0], slab_delta, slab_beta, scratch)
+    counts[...] = jnp.full(counts.shape, counts_in[0, 0], i32)
+    for copy in copies:
+        copy.wait()
 
 
 def slot_position(slot):
@@ -167,24 +183,14 @@
             extra += jnp.where(lane >= N - SHIFT, margins[after, part], 0.0)
             proj[c, block] += extra
     _, previous = slot_position(slot)
+    own = spots[1, 0]
     lane = lane_iota(N)
     even = is_even()
-    for upper in (True, False):
-        first, second, offset = block_of(spots[1, 0] if upper else previous, blocks)
-        start = EDGE_ROWS if upper else 0
-        for c in range(2):
-            left = roll_left(proj[c, first, start : start + N, :], offset)
-            right = roll_left(proj[c, second, start : start + N, :], offset)
-            value = jnp.where(lane < N - offset, left, right).astype(bf16)
-            part = slice(c * N, (c + 1) * N)
-
-            @pl.when(even == upper)
-            def _():
-                core[part, :] = value
-
-            @pl.when(even != upper)
-            def _():
-                cross[part, :] = value
+    for out, upper in ((core, even), (cross, jnp.logical_not(even))):
+        first, second, offset = block_of(jnp.where(upper, own, previous), blocks)
+        rows = pl.ds(pl.multiple_of(jnp.where(upper, EDGE_ROWS, 0), 8), N)
+        pair = patch_of(proj, lane, offset, first, second, rows)
+        out[...] = jnp.concatenate(pair, 0).astype(bf16)
 
 
 def transmit(phase, absorb):
@@ -324,15 +330,8 @@
     return packed_message(jnp.concatenate(mains, 0), jnp.concatenate(margins, 0), scratch)
 
 
-def cut_kernel(total, *refs):
-    outs, scratch = refs[:-1], refs[-1]
-    blocks = total.shape[1]
-    me = lax.axis_index("ang")
-    for out, d in zip(outs, [*range(2, blocks), 0]):
-        out[...] = gradient_message(lax.rem(me + d, blocks), total, scratch)
-
-
-def edge_kernel(spots, counts, slot, core, cross, trans, inner, probe, measured, tables, out, total, patch, frame, scratch):
+def edge_kernel(spots, counts, slot, core, cross, trans, inner, probe, measured, tables, *refs):
+    outs, (total, patch, frame, scratch) = refs[:-4], refs[-4:]
     blocks, tile = trans.shape[1], trans.shape[2]
     even = is_even()
     own_row, own_column = spots[0, 0], spots[1, 0]
@@ -378,7 +377,9 @@
         frame[c, N : 2 * N, :] = jnp.zeros((N, N), f32)
         rows = frame[c, pl.ds(tile - start, N), :]
         add_patch(total, c, slice(0, N), rows, lane_iota(N), offset, first, second)
-    out[...] = gradient_message(lax.rem(lax.axis_index("ang") + 1, blocks), total, scratch)
+    me = lax.axis_index("ang")
+    for d, out in enumerate(outs):
+        out[...] = gradient_message(lax.rem(me + d, blocks), total, scratch)
 
 
 def slab_kernel(angles, steps, last, shifts, *refs):
@@ -442,37 +443,27 @@
     field = ((2, angles, tile, N), f32)
     slab = (2 * tile, N)
     halo = ((2 * N, N), bf16)
-    shifts, spots = layer_shifts.T, positions[0].T
     tables = jnp.asarray(fourier_tables())
 
-    arguments = [
-        pltpu.with_memory_space_constraint(value, pltpu.HBM)
-        for value in (
-            shifts,
-            spots,
-            delta_obj.reshape(slab),
-            beta_obj.reshape(slab),
-            illumination_field,
-            amplitudes[0],
-        )
-    ]
-    spots, slab_delta, slab_beta, probe, measured, shifts, following, slot = call(
+    in_hbm = functools.partial(pltpu.with_memory_space_constraint, memory_space=pltpu.HBM)
+    shifts, spots, probe, measured = (
+        in_hbm(value) for value in (layer_shifts.T, positions[0].T, illumination_field, amplitudes[0])
+    )
+    slab_delta, slab_beta, shifts, following, slot = call(
         functools.partial(first_kernel, angles),
-        [SMEM] + [HBM] * len(arguments),
-        [
-            *((value.shape, value.dtype) for value in arguments[1:]),
-            ((2 * angles, N), i32),
-            message,
-            ((N + 16, N), f32),
-        ],
-        [
-            *(pltpu.SMEM(value.shape, i32) for value in arguments[:2]),
-            padded,
-            pltpu.SemaphoreType.DMA((4,)),
-            pltpu.SemaphoreType.DMA((4,)),
-        ],
-    )(scan_counts, *arguments)
-    *others, own = call(window_kernel, [VMEM] * 3, [message] * (angles - 1), [padded])(shifts, slab_delta, slab_beta)
+        [HBM] * 5,
+        [(slab, f32), (slab, f32), ((2 * angles, N), i32), message, ((N + 16, N), f32)],
+        [pltpu.SMEM(shifts.shape, i32), pltpu.SMEM(spots.shape, i32), padded, pltpu.SemaphoreType.DMA((5,))],
+    )(shifts, spots, in_hbm(delta_obj.reshape(slab)), in_hbm(beta_obj.reshape(slab)), measured)
+    others = call(window_kernel, [VMEM] * 3, [message] * (angles - 2), [padded])(shifts, slab_delta, slab_beta)
+    own, counts, spots, probe, measured = call(
+        load_kernel,
+        [SMEM] + [VMEM] * 4 + [HBM] * 3,
+        [message, ((8, N), i32)] + [(value.shape, value.dtype) for value in (spots, probe, measured)],
+        [padded, pltpu.SemaphoreType.DMA((3,))],
+        flops=10**9,
+        bytes_accessed=10**6,
+    )(scan_counts, shifts, slab_delta, slab_beta, others[-1], spots, probe, measured)
     windows = [own, following, *others]
     received = exchange(windows)
     previous = on_rows(slot, lambda i: i + 1)
@@ -492,21 +483,21 @@
     cross = on_rows(cross, lambda i: i + 1 if i % 2 else i - 1)
     trans, inner = call(
         inner_kernel,
-        [VMEM, SMEM] + [VMEM] * 4,
+        [VMEM] * 6,
         [field, field],
         [(N + 2 * SHIFT, N)],
         flops=3 * 10**9,
         bytes_accessed=3 * 10**6,
-    )(spots, scan_counts, proj, probe, measured, tables)
-    following, total = call(
+    )(spots, counts, proj, probe, measured, tables)
+    *outgoing, _ = call(
         edge_kernel,
-        [VMEM, SMEM] + [VMEM] * 8,
-        [message, field],
+        [VMEM] * 10,
+        [message] * angles + [field],
         [(2, 2, tile + N, N), (2, 2 * tile + 8, N), padded],
-        aliases={6: 1},
-    )(spots, scan_counts, previous, core, cross, trans, inner, probe, measured, tables)
-    *others, own = call(cut_kernel, [VMEM], [message] * (angles - 1), [padded])(total)
-    received = exchange([own, following, *others])
+        aliases={6: angles},
+    )(spots, counts, previous, core, cross, trans, inner, probe, measured, tables)
+    received = exchange(outgoing)
+    early = list(range(angles - 1))
     sums = call(
         functools.partial(slab_kernel, angles, early, False),
         [VMEM] * angles,

time: 33.4 us -> 32.4 us (0.970)
  waiting for transfers between devices: 9.75 us -> 8.16 us
  Pallas kernels: 8.25 us -> 8.92 us
    ppermute x6, waiting for transfers between devices: 9.75 us -> 8.04 us  [exchange(): lax.ppermute(messages[d], 'ang', [(i, (i + d) % count) for i in range(cou...]
    pallas_call x5, Pallas kernels: 6.4 us -> 7.28 us  [the longest x1 2.35 us: on_device(): call(inner_kernel, [VMEM] * 6, [field, field], [(N + 2 * SHIFT, N)], flop...]
  transfers between devices with their start and end apart: 9 -> 9, of which waited for: 3 -> 5; matrix products, arithmetic and copies ran while one was open for 0% -> 0% of each run, Pallas kernels for 10% -> 14%
where the time goes in v5:
time: 32.4 us; the launch traced here: 32.2 us
  starting transfers between devices  13.7 us (42%)
  Pallas kernels  8.92 us (28%)
  waiting for transfers between devices  8.16 us (25%)
  between operations  1.37 us (4%)
    ppermute x6, starting transfers between devices, exchange(): lax.ppermute(messages[d], 'ang', [(i, (i + d) % count) for i in range(cou...  10.9 us
    ppermute x6, waiting for transfers between devices, exchange(): lax.ppermute(messages[d], 'ang', [(i, (i + d) % count) for i in range(cou...  8.04 us
    ppermute x3, starting transfers between devices, on_rows(): lax.ppermute(value, 'rows', [(i, target(i) % count) for i in range(count)])  2.78 us
    pallas_call x1, Pallas kernels, on_device(): call(inner_kernel, [VMEM] * 6, [field, field], [(N + 2 * SHIFT, N)], flop...  2.35 us
    pallas_call x1, Pallas kernels, on_device(): call(edge_kernel, [VMEM] * 10, [message] * angles + [field], [(2, 2, tile...  2.09 us
    pallas_call x1, Pallas kernels, on_device(): call(functools.partial(first_kernel, angles), [HBM] * 5, [(slab, f32), (s...  1.24 us
    pallas_call x1, Pallas kernels, on_device(): call(load_kernel, [SMEM] + [VMEM] * 4 + [HBM] * 3, [message, ((8, N), i32...  1.21 us
    pallas_call x1, Pallas kernels, on_device(): call(functools.partial(slab_kernel, angles, [angles - 1], True), [VMEM] *...  0.87 us
  transfers between devices with their start and end apart: 9, of which 5 were waited for; matrix products, arithmetic and copies ran while one was open for 0% of the time, Pallas kernels for 14%

profile of v5, /device:TPU:0, one launch (start us, length us, event | category | flops | bytes accessed | tf_op | source)
XLA Modules:
  0.0 32.2 jit_solution(13792542409010292998)
XLA Ops:
  0.6 1.2 %shard_map.95 = (f32[272,128]{1,0:T(8,128)S(1)}, f32[272,128]{1,0:T(8,128)S(1)}, s32[8,128]{1,0:T(8,128)S(1)}, bf16[312,128]{1,0:T(8,128)(2,1)S(1)}, f32[144,128]{1,0:T(8,128)S(1)}) custom-call(s32[2,4]{1,0:T(2,128)} %bitcast.13, s32[2,4]{1,0:T(2,128)} %bitcast.14, f32[272,128]{1,0:T(8,128)} %bitcast.11, f32[272,128]{1,0:T(8,128)} %bitcast.12, ...), custom_call_target="tpu_custom_call" | custom-call | tf_op jit(solution)/shard_map/pallas_call | solution.py:452
  1.9 0.5 %collective-permute-start = (f32[144,128]{1,0:T(8,128)S(1)}, f32[144,128]{1,0:T(8,128)S(1)}, u32[]{:S(2)}, u32[]{:S(2)}) collective-permute-start(f32[144,128]{1,0:T(8,128)S(1)} %get-tuple-element.33), channel_id=1, source_target_pairs={{0,4},{4,8},{8,12},{12,16},{16,20},{20,24},{24,28},{28,0},{1,5},{5... | collective-permute-start | bytes 221192 | tf_op jit(solution)/shard_map/ppermute | solution.py:435
  2.4 2.6 %collective-permute-start.2 = (bf16[312,128]{1,0:T(8,128)(2,1)S(1)}, bf16[312,128]{1,0:T(8,128)(2,1)S(1)}, u32[]{:S(2)}, u32[]{:S(2)}) collective-permute-start(bf16[312,128]{1,0:T(8,128)(2,1)S(1)} %get-tuple-element.35), channel_id=1, source_target_pairs={{0,1},{1,2},{2,3},{3,0},{4,5},{5,6},{6,7},{7,4},{8,9},{9,10},{10,1... | collective-permute-start | bytes 239624 | tf_op jit(solution)/shard_map/ppermute | solution.py:429
  5.0 0.4 %shard_map.96 = (bf16[312,128]{1,0:T(8,128)(2,1)S(1)}, bf16[312,128]{1,0:T(8,128)(2,1)S(1)}) custom-call(s32[8,128]{1,0:T(8,128)S(1)} %get-tuple-element.27.shifts, f32[272,128]{1,0:T(8,128)S(1)} %get-tuple-element.28.slab_delta, f32[272,128]{1,0:T(8,128)S(1)} %get-tuple-element.29.slab_beta), custom_call_target="tpu_custom_call" | custom-call | tf_op jit(solution)/shard_map/pallas_call | solution.py:458
  5.4 2.7 %collective-permute-start.3 = (bf16[312,128]{1,0:T(8,128)(2,1)S(1)}, bf16[312,128]{1,0:T(8,128)(2,1)S(1)}, u32[]{:S(2)}, u32[]{:S(2)}) collective-permute-start(bf16[312,128]{1,0:T(8,128)(2,1)S(1)} %get-tuple-element.36), channel_id=1, source_target_pairs={{0,2},{1,3},{2,0},{3,1},{4,6},{5,7},{6,4},{7,5},{8,10},{9,11},{10,... | collective-permute-start | bytes 239624 | tf_op jit(solution)/shard_map/ppermute | solution.py:429
  8.1 1.3 %collective-permute-start.1 = (bf16[312,128]{1,0:T(8,128)(2,1)S(1)}, bf16[312,128]{1,0:T(8,128)(2,1)S(1)}, u32[]{:S(2)}, u32[]{:S(2)}) collective-permute-start(bf16[312,128]{1,0:T(8,128)(2,1)S(1)} %get-tuple-element.30._), channel_id=1, source_target_pairs={{0,3},{1,0},{2,1},{3,2},{4,7},{5,4},{6,5},{7,6},{8,11},{9,8},{10,9... | collective-permute-start | bytes 239624 | tf_op jit(solution)/shard_map/ppermute | solution.py:429
  10.1 1.2 %shard_map.97 = (bf16[312,128]{1,0:T(8,128)(2,1)S(1)}, s32[8,128]{1,0:T(8,128)S(1)}, s32[2,4]{1,0:T(2,128)S(1)}, f32[2,128,128]{2,1,0:T(8,128)S(1)}, f32[4,128,128]{2,1,0:T(8,128)S(1)}) custom-call(s32[1,1]{1,0:T(1,128)S(6)} %copy.16.counts_in, s32[8,128]{1,0:T(8,128)S(1)} %get-tuple-element.27.shifts, f32[272,128]{1,0:T(8,128)S(1)} %get-tuple-element.28.slab_delta, ...), custom_call_target="tpu_custom_call" | custom-call | flops 1000000000 | bytes 1000000 | tf_op jit(solution)/shard_map/pallas_call | solution.py:459
  11.3 2.5 %collective-permute-done.3.refs_2_ = bf16[312,128]{1,0:T(8,128)(2,1)S(1)} collective-permute-done((bf16[312,128]{1,0:T(8,128)(2,1)S(1)}, bf16[312,128]{1,0:T(8,128)(2,1)S(1)}, u32[]{:S(2)}, u32[]{:S(2)}) %collective-permute-start.3) | collective-permute-done | bytes 79904 | tf_op jit(solution)/shard_map/ppermute | solution.py:429
  13.8 0.1 shard_map.98
  13.9 0.3 %collective-permute-done.1.message = bf16[312,128]{1,0:T(8,128)(2,1)S(1)} collective-permute-done((bf16[312,128]{1,0:T(8,128)(2,1)S(1)}, bf16[312,128]{1,0:T(8,128)(2,1)S(1)}, u32[]{:S(2)}, u32[]{:S(2)}) %collective-permute-start.1) | collective-permute-done | bytes 79904 | tf_op jit(solution)/shard_map/ppermute | solution.py:429
  14.3 0.3 %shard_map.99 = (bf16[256,128]{1,0:T(8,128)(2,1)S(1)}, bf16[256,128]{1,0:T(8,128)(2,1)S(1)}, f32[2,4,136,128]{3,2,1,0:T(8,128)S(1)}, f32[4,272,128]{2,1,0:T(8,128)S(1)}) custom-call(s32[2,4]{1,0:T(2,128)S(1)} %get-tuple-element.31.spots, f32[144,128]{1,0:T(8,128)S(1)} %collective-permute-done.slot, ...), custom_call_target="tpu_custom_call", output_to_operand_aliasing={{2}: (3, {}), {3}: (4, {})} | custom-call | tf_op jit(solution)/shard_map/pallas_call | solution.py:479
  14.6 0.2 collective-permute-start.4
  14.8 2.1 %collective-permute-start.5 = (bf16[256,128]{1,0:T(8,128)(2,1)S(1)}, bf16[256,128]{1,0:T(8,128)(2,1)S(1)}, u32[]{:S(2)}, u32[]{:S(2)}) collective-permute-start(bf16[256,128]{1,0:T(8,128)(2,1)S(1)} %get-tuple-element.40), channel_id=1, source_target_pairs={{0,28},{4,8},{8,4},{12,16},{16,12},{20,24},{24,20},{28,0},{1,29},{... | collective-permute-start | bytes 196616 | tf_op jit(solution)/shard_map/ppermute | solution.py:435
  16.9 2.4 %shard_map.100 = (f32[2,4,136,128]{3,2,1,0:T(8,128)S(1)}, f32[2,4,136,128]{3,2,1,0:T(8,128)S(1)}) custom-call(s32[2,4]{1,0:T(2,128)S(1)} %get-tuple-element.31.spots, s32[8,128]{1,0:T(8,128)S(1)} %get-tuple-element.32.counts, f32[2,4,136,128]{3,2,1,0:T(8,128)S(1)} %get-tuple-element.41.proj, f32[2,128,128]{2,1,0:T(8,128)S(1)} %get-tuple-element.42.probe, ...), custom_call_target="tpu_custom_call" | custom-call | flops 3000000000 | bytes 3000000 | tf_op jit(solution)/shard_map/pallas_call | solution.py:484
  19.3 0.1 collective-permute-done.5.cross
  19.4 2.1 %shard_map.101 = (bf16[312,128]{1,0:T(8,128)(2,1)S(1)}, bf16[312,128]{1,0:T(8,128)(2,1)S(1)}, bf16[312,128]{1,0:T(8,128)(2,1)S(1)}, bf16[312,128]{1,0:T(8,128)(2,1)S(1)}, f32[2,4,136,128]{3,2,1,0:T(8,128)S(1)}) custom-call(s32[2,4]{1,0:T(2,128)S(1)} %get-tuple-element.31.spots, ...), custom_call_target="tpu_custom_call", output_to_operand_aliasing={{4}: (6, {})} | custom-call | tf_op jit(solution)/shard_map/pallas_call | solution.py:492
  21.5 1.8 %collective-permute-start.7 = (bf16[312,128]{1,0:T(8,128)(2,1)S(1)}, bf16[312,128]{1,0:T(8,128)(2,1)S(1)}, u32[]{:S(2)}, u32[]{:S(2)}) collective-permute-start(bf16[312,128]{1,0:T(8,128)(2,1)S(1)} %get-tuple-element.48), channel_id=1, source_target_pairs={{0,1},{1,2},{2,3},{3,0},{4,5},{5,6},{6,7},{7,4},{8,9},{9,10},{10,1... | collective-permute-start | bytes 239624 | tf_op jit(solution)/shard_map/ppermute | solution.py:429
  23.3 1.8 %collective-permute-start.8 = (bf16[312,128]{1,0:T(8,128)(2,1)S(1)}, bf16[312,128]{1,0:T(8,128)(2,1)S(1)}, u32[]{:S(2)}, u32[]{:S(2)}) collective-permute-start(bf16[312,128]{1,0:T(8,128)(2,1)S(1)} %get-tuple-element.49), channel_id=1, source_target_pairs={{0,2},{1,3},{2,0},{3,1},{4,6},{5,7},{6,4},{7,5},{8,10},{9,11},{10,... | collective-permute-start | bytes 239624 | tf_op jit(solution)/shard_map/ppermute | solution.py:429
  25.1 0.6 %collective-permute-start.6 = (bf16[312,128]{1,0:T(8,128)(2,1)S(1)}, bf16[312,128]{1,0:T(8,128)(2,1)S(1)}, u32[]{:S(2)}, u32[]{:S(2)}) collective-permute-start(bf16[312,128]{1,0:T(8,128)(2,1)S(1)} %get-tuple-element.46), channel_id=1, source_target_pairs={{0,3},{1,0},{2,1},{3,2},{4,7},{5,4},{6,5},{7,6},{8,11},{9,8},{10,9... | collective-permute-start | bytes 239624 | tf_op jit(solution)/shard_map/ppermute | solution.py:429
  25.8 2.9 %collective-permute-done.7.refs_1_ = bf16[312,128]{1,0:T(8,128)(2,1)S(1)} collective-permute-done((bf16[312,128]{1,0:T(8,128)(2,1)S(1)}, bf16[312,128]{1,0:T(8,128)(2,1)S(1)}, u32[]{:S(2)}, u32[]{:S(2)}) %collective-permute-start.7) | collective-permute-done | bytes 79904 | tf_op jit(solution)/shard_map/ppermute | solution.py:429
  28.7 2.2 %collective-permute-done.8.refs_2_ = bf16[312,128]{1,0:T(8,128)(2,1)S(1)} collective-permute-done((bf16[312,128]{1,0:T(8,128)(2,1)S(1)}, bf16[312,128]{1,0:T(8,128)(2,1)S(1)}, u32[]{:S(2)}, u32[]{:S(2)}) %collective-permute-start.8) | collective-permute-done | bytes 79904 | tf_op jit(solution)/shard_map/ppermute | solution.py:429
  30.9 0.3 %shard_map.102.refs_1_ = f32[2,2,136,128]{3,2,1,0:T(8,128)S(1)} custom-call(s32[8,128]{1,0:T(8,128)S(1)} %get-tuple-element.27.shifts, bf16[312,128]{1,0:T(8,128)(2,1)S(1)} %get-tuple-element.47.refs_0_, bf16[312,128]{1,0:T(8,128)(2,1)S(1)} %collective-permute-done.7.refs_1_, bf16[312,128]{1,0:T(8,128)(2,1)S(1)} %collective-permute-done.8.refs_2_), custom_call_target="tpu_custom_call" | custom-call | flops 1000000000 | bytes 1000000 | tf_op jit(solution)/shard_map/pallas_call | solution.py:501
  31.3 0.0 collective-permute-done.6.refs_0_
  31.3 0.9 %shard_map.103 = (f32[272,128]{1,0:T(8,128)}, f32[272,128]{1,0:T(8,128)}) custom-call(s32[8,128]{1,0:T(8,128)S(1)} %get-tuple-element.27.shifts, bf16[312,128]{1,0:T(8,128)(2,1)S(1)} %collective-permute-done.6.refs_0_, f32[2,2,136,128]{3,2,1,0:T(8,128)S(1)} %shard_map.102.refs_1_), custom_call_target="tpu_custom_call" | custom-call | tf_op jit(solution)/shard_map/pallas_call | solution.py:508
  (5 shorter events, 0.0 us)
Async XLA Ops:
  1.9 12.1 %collective-permute-start = (f32[144,128]{1,0:T(8,128)S(1)}, f32[144,128]{1,0:T(8,128)S(1)}, u32[]{:S(2)}, u32[]{:S(2)}) collective-permute-start(f32[144,128]{1,0:T(8,128)S(1)} %get-tuple-element.33), channel_id=1, source_target_pairs={{0,4},{4,8},{8,12},{12,16},{16,20},{20,24},{24,28},{28,0},{1,5},{5... | collective-permute-start | bytes 221192 | tf_op jit(solution)/shard_map/ppermute | solution.py:435
  2.4 8.9 %collective-permute-start.2 = (bf16[312,128]{1,0:T(8,128)(2,1)S(1)}, bf16[312,128]{1,0:T(8,128)(2,1)S(1)}, u32[]{:S(2)}, u32[]{:S(2)}) collective-permute-start(bf16[312,128]{1,0:T(8,128)(2,1)S(1)} %get-tuple-element.35), channel_id=1, source_target_pairs={{0,1},{1,2},{2,3},{3,0},{4,5},{5,6},{6,7},{7,4},{8,9},{9,10},{10,1... | collective-permute-start | bytes 239624 | tf_op jit(solution)/shard_map/ppermute | solution.py:429
  5.4 8.4 %collective-permute-start.3 = (bf16[312,128]{1,0:T(8,128)(2,1)S(1)}, bf16[312,128]{1,0:T(8,128)(2,1)S(1)}, u32[]{:S(2)}, u32[]{:S(2)}) collective-permute-start(bf16[312,128]{1,0:T(8,128)(2,1)S(1)} %get-tuple-element.36), channel_id=1, source_target_pairs={{0,2},{1,3},{2,0},{3,1},{4,6},{5,7},{6,4},{7,5},{8,10},{9,11},{10,... | collective-permute-start | bytes 239624 | tf_op jit(solution)/shard_map/ppermute | solution.py:429
  8.1 6.2 %collective-permute-start.1 = (bf16[312,128]{1,0:T(8,128)(2,1)S(1)}, bf16[312,128]{1,0:T(8,128)(2,1)S(1)}, u32[]{:S(2)}, u32[]{:S(2)}) collective-permute-start(bf16[312,128]{1,0:T(8,128)(2,1)S(1)} %get-tuple-element.30._), channel_id=1, source_target_pairs={{0,3},{1,0},{2,1},{3,2},{4,7},{5,4},{6,5},{7,6},{8,11},{9,8},{10,9... | collective-permute-start | bytes 239624 | tf_op jit(solution)/shard_map/ppermute | solution.py:429
  14.3 2.6 %copy-start = (bf16[4,256,256]{2,1,0:T(8,128)(2,1)S(1)}, bf16[4,256,256]{2,1,0:T(8,128)(2,1)}, u32[]{:S(2)}) copy-start(bf16[4,256,256]{2,1,0:T(8,128)(2,1)} %constant.2.clone.tables) | copy-start | bytes 1572868
  14.6 4.6 %collective-permute-start.4 = (bf16[256,128]{1,0:T(8,128)(2,1)S(1)}, bf16[256,128]{1,0:T(8,128)(2,1)S(1)}, u32[]{:S(2)}, u32[]{:S(2)}) collective-permute-start(bf16[256,128]{1,0:T(8,128)(2,1)S(1)} %get-tuple-element.39), channel_id=1, source_target_pairs={{0,4},{4,0},{8,12},{12,8},{16,20},{20,16},{24,28},{28,24},{1,5},{5... | collective-permute-start | bytes 196616 | tf_op jit(solution)/shard_map/ppermute | solution.py:435
  14.8 4.6 %collective-permute-start.5 = (bf16[256,128]{1,0:T(8,128)(2,1)S(1)}, bf16[256,128]{1,0:T(8,128)(2,1)S(1)}, u32[]{:S(2)}, u32[]{:S(2)}) collective-permute-start(bf16[256,128]{1,0:T(8,128)(2,1)S(1)} %get-tuple-element.40), channel_id=1, source_target_pairs={{0,28},{4,8},{8,4},{12,16},{16,12},{20,24},{24,20},{28,0},{1,29},{... | collective-permute-start | bytes 196616 | tf_op jit(solution)/shard_map/ppermute | solution.py:435
  21.5 7.2 %collective-permute-start.7 = (bf16[312,128]{1,0:T(8,128)(2,1)S(1)}, bf16[312,128]{1,0:T(8,128)(2,1)S(1)}, u32[]{:S(2)}, u32[]{:S(2)}) collective-permute-start(bf16[312,128]{1,0:T(8,128)(2,1)S(1)} %get-tuple-element.48), channel_id=1, source_target_pairs={{0,1},{1,2},{2,3},{3,0},{4,5},{5,6},{6,7},{7,4},{8,9},{9,10},{10,1... | collective-permute-start | bytes 239624 | tf_op jit(solution)/shard_map/ppermute | solution.py:429
  23.3 7.6 %collective-permute-start.8 = (bf16[312,128]{1,0:T(8,128)(2,1)S(1)}, bf16[312,128]{1,0:T(8,128)(2,1)S(1)}, u32[]{:S(2)}, u32[]{:S(2)}) collective-permute-start(bf16[312,128]{1,0:T(8,128)(2,1)S(1)} %get-tuple-element.49), channel_id=1, source_target_pairs={{0,2},{1,3},{2,0},{3,1},{4,6},{5,7},{6,4},{7,5},{8,10},{9,11},{10,... | collective-permute-start | bytes 239624 | tf_op jit(solution)/shard_map/ppermute | solution.py:429
  25.1 6.1 %collective-permute-start.6 = (bf16[312,128]{1,0:T(8,128)(2,1)S(1)}, bf16[312,128]{1,0:T(8,128)(2,1)S(1)}, u32[]{:S(2)}, u32[]{:S(2)}) collective-permute-start(bf16[312,128]{1,0:T(8,128)(2,1)S(1)} %get-tuple-element.46), channel_id=1, source_target_pairs={{0,3},{1,0},{2,1},{3,2},{4,7},{5,4},{6,5},{7,6},{8,11},{9,8},{10,9... | collective-permute-start | bytes 239624 | tf_op jit(solution)/shard_map/ppermute | solution.py:429

commit v6 on v5

--- a/solution.py
+++ b/solution.py
@@ -123,8 +123,9 @@
     out[...] = window_message(lambda z: scalar_shifts[z, following], slab_delta, slab_beta, scratch)
 
 
-def window_kernel(shifts, slab_delta, slab_beta, *refs):
-    outs, scratch = refs[:-1], refs[-1]
+def window_kernel(shifts, slab_delta, slab_beta, _, *refs):
+    outs, slot, scratch = refs[:-2], refs[-2], refs[-1]
+    slot[N:, :] = slot[N:, :] + 0.0
     for k, out in enumerate(outs):
         d = k + 2
         out[...] = window_message(lambda z: shifts[2 * d + z, 0], slab_delta, slab_beta, scratch)
@@ -289,7 +290,43 @@
     total[c, second, rows, :] += jnp.where(lane < offset, placed, 0.0)
 
 
-def inner_kernel(spots, counts, proj, probe, measured, tables, trans, grad, frame):
+def edge_patch(is_own, spots, slot, halo, trans, patch):
+    blocks, tile = trans.shape[1], trans.shape[2]
+    prev_row, prev_column = slot_position(slot)
+    columns = block_of(jnp.where(is_own, spots[1, 0], prev_column), blocks)
+    start = jnp.where(is_own, spots[0, 0], jnp.maximum(prev_row, EDGE_ROWS))
+    first, second, offset = columns
+    here = pl.ds(pl.multiple_of(jnp.where(is_own, 0, tile), 8), tile)
+    there = pl.ds(pl.multiple_of(jnp.where(is_own, tile, EDGE_ROWS), 8), N)
+    last = lax.axis_index("rows") == lax.axis_size("rows") - 1
+    value = jnp.where(is_own & last, 0.0, halo[...].astype(f32))
+    outside = transmit(value[:N], value[N:])
+    inside = patch_of(trans, lane_iota(tile), offset, first, second, slice(None))
+    for c in range(2):
+        patch[c, here, :] = inside[c]
+        patch[c, there, :] = outside[c]
+    pair = [patch[c, pl.ds(start, N), :] for c in range(2)]
+    return pair, columns, jnp.where(is_own, start, start - tile)
+
+
+def edge_weight(is_own, counts, slot):
+    prev_row, _ = slot_position(slot)
+    reaches = (prev_row > EDGE_ROWS) & (lax.axis_index("rows") > 0)
+    return jnp.where(jnp.where(is_own, counts[0, 0] > 0, reaches), 1.0, 0.0).astype(f32)
+
+
+def add_edge(total, chained, columns, place, frame):
+    tile = total.shape[2]
+    first, second, offset = columns
+    for c in range(2):
+        frame[c, 0:tile, :] = jnp.zeros((tile, N), f32)
+        frame[c, tile : tile + N, :] = chained[c]
+        frame[c, tile + N :, :] = jnp.zeros((tile, N), f32)
+        rows = frame[c, pl.ds(tile - place, tile), :]
+        add_patch(total, c, slice(None), rows, lane_iota(tile), offset, first, second)
+
+
+def inner_kernel(spots, counts, proj, slot0, core, probe, measured, tables, trans, grad, patch, frame, edge_frame):
     blocks, tile = proj.shape[1], proj.shape[2]
     for block in range(blocks):
         re, im = transmit(proj[0, block], proj[1, block])
@@ -300,18 +337,23 @@
     frame[SHIFT + N :, :] = jnp.zeros((SHIFT, N), f32)
     slots = measured.shape[0]
     lane = lane_iota(N)
-    patches, weights = [], []
+    is_own = is_even()
+    pair, columns, place = edge_patch(is_own, spots, slot0, core, trans, patch)
+    patches, weights = [pair], [edge_weight(is_own, counts, slot0)]
+    patterns = [jnp.where(is_own, measured[0], slot0[0:N, :])]
     for slot in range(1, slots):
         row = jnp.minimum(spots[0, slot], EDGE_ROWS)
         first, second, offset = block_of(spots[1, slot], blocks)
         patches.append(patch_of(trans, lane, offset, first, second, pl.ds(row, N)))
         weights.append(jnp.where(slot < counts[0, 0], 1.0, 0.0).astype(f32))
-    grads = scan_gradients(patches, [measured[slot] for slot in range(1, slots)], weights, probe, tables)
+        patterns.append(measured[slot])
+    grads = scan_gradients(patches, patterns, weights, probe, tables)
+    add_edge(grad, chain_back(patches[0], grads[0]), columns, place, edge_frame)
     lane = lane_iota(tile)
     for slot in range(1, slots):
         row = jnp.minimum(spots[0, slot], EDGE_ROWS)
         first, second, offset = block_of(spots[1, slot], blocks)
-        chained = chain_back(patches[slot - 1], grads[slot - 1])
+        chained = chain_back(patches[slot], grads[slot])
         for c in range(2):
             frame[SHIFT : SHIFT + N, :] = chained[c]
             add_patch(grad, c, slice(None), frame[pl.ds(SHIFT - row, tile), :], lane, offset, first, second)
@@ -330,56 +372,22 @@
     return packed_message(jnp.concatenate(mains, 0), jnp.concatenate(margins, 0), scratch)
 
 
-def edge_kernel(spots, counts, slot, core, cross, trans, inner, probe, measured, tables, *refs):
+def edge_kernel(spots, counts, slot0, cross, trans, _, probe, measured, tables, *refs):
     outs, (total, patch, frame, scratch) = refs[:-4], refs[-4:]
-    blocks, tile = trans.shape[1], trans.shape[2]
-    even = is_even()
-    own_row, own_column = spots[0, 0], spots[1, 0]
-    prev_row, prev_column = slot_position(slot)
-    own_block, prev_block = block_of(own_column, blocks), block_of(prev_column, blocks)
-    last = lax.axis_index("rows") == lax.axis_size("rows") - 1
-    near, away = core[...].astype(f32), cross[...].astype(f32)
-    below = jnp.where(last, 0.0, jnp.where(even, near, away))
-    above = jnp.where(even, away, near)
-    re, im = transmit(below[:N], below[N:])
-    patch[0, 0, tile:, :] = re
-    patch[0, 1, tile:, :] = im
-    re, im = transmit(above[:N], above[N:])
-    patch[1, 0, EDGE_ROWS:tile, :] = re
-    patch[1, 1, EDGE_ROWS:tile, :] = im
-    first, second, offset = own_block
-    pair = patch_of(trans, lane_iota(tile), offset, first, second, slice(None))
-    for c in range(2):
-        patch[0, c, 0:tile, :] = pair[c]
-    first, second, offset = prev_block
-    pair = patch_of(trans, lane_iota(N), offset, first, second, slice(0, N))
-    for c in range(2):
-        patch[1, c, tile:, :] = pair[c]
-    reaches = (prev_row > EDGE_ROWS) & (lax.axis_index("rows") > 0)
-    start = jnp.maximum(prev_row, EDGE_ROWS)
-    patches = [
-        [patch[0, c, pl.ds(own_row, N), :] for c in range(2)],
-        [patch[1, c, pl.ds(start, N), :] for c in range(2)],
-    ]
-    weights = [jnp.where(flag, 1.0, 0.0).astype(f32) for flag in (counts[0, 0] > 0, reaches)]
-    grads = scan_gradients(patches, [measured[0], slot[0:N, :]], weights, probe, tables)
-    chained = [chain_back(pair, grad) for pair, grad in zip(patches, grads)]
-    first, second, offset = own_block
-    for c in range(2):
-        frame[c, 0:tile, :] = jnp.zeros((tile, N), f32)
-        frame[c, tile : tile + N, :] = chained[0][c]
-        frame[c, tile + N :, :] = jnp.zeros((frame.shape[1] - tile - N, N), f32)
-        rows = frame[c, pl.ds(tile - own_row, tile), :]
-        add_patch(total, c, slice(None), rows, lane_iota(tile), offset, first, second)
-    first, second, offset = prev_block
-    for c in range(2):
-        frame[c, 0:N, :] = chained[1][c]
-        frame[c, N : 2 * N, :] = jnp.zeros((N, N), f32)
-        rows = frame[c, pl.ds(tile - start, N), :]
-        add_patch(total, c, slice(0, N), rows, lane_iota(N), offset, first, second)
+    blocks = trans.shape[1]
+    is_own = jnp.logical_not(is_even())
+    pair, columns, place = edge_patch(is_own, spots, slot0, cross, trans, patch)
+    pattern = jnp.where(is_own, measured[0], slot0[0:N, :])
+    weight = edge_weight(is_own, counts, slot0)
+    grads = scan_gradients([pair], [pattern], [weight], probe, tables)
+    add_edge(total, chain_back(pair, grads[0]), columns, place, frame)
     me = lax.axis_index("ang")
-    for d, out in enumerate(outs):
-        out[...] = gradient_message(lax.rem(me + d, blocks), total, scratch)
+    for k, out in enumerate(outs):
+        out[...] = gradient_message(lax.rem(me + k + 1, blocks), total, scratch)
+
+
+def own_kernel(total, _, out, scratch):
+    out[...] = gradient_message(lax.axis_index("ang"), total, scratch)
 
 
 def slab_kernel(angles, steps, last, shifts, *refs):
@@ -455,7 +463,9 @@
         [(slab, f32), (slab, f32), ((2 * angles, N), i32), message, ((N + 16, N), f32)],
         [pltpu.SMEM(shifts.shape, i32), pltpu.SMEM(spots.shape, i32), padded, pltpu.SemaphoreType.DMA((5,))],
     )(shifts, spots, in_hbm(delta_obj.reshape(slab)), in_hbm(beta_obj.reshape(slab)), measured)
-    others = call(window_kernel, [VMEM] * 3, [message] * (angles - 2), [padded])(shifts, slab_delta, slab_beta)
+    *others, slot = call(
+        window_kernel, [VMEM] * 4, [message] * (angles - 2) + [((N + 16, N), f32)], [padded], aliases={3: angles - 2}
+    )(shifts, slab_delta, slab_beta, slot)
     own, counts, spots, probe, measured = call(
         load_kernel,
         [SMEM] + [VMEM] * 4 + [HBM] * 3,
@@ -481,22 +491,24 @@
     )(spots, previous, received[-1], *partly)
     core = on_rows(core, lambda i: i ^ 1)
     cross = on_rows(cross, lambda i: i + 1 if i % 2 else i - 1)
+    patch, frame = (2, 2 * tile, N), (2, 2 * tile + N, N)
     trans, inner = call(
         inner_kernel,
-        [VMEM] * 6,
+        [VMEM] * 8,
         [field, field],
-        [(N + 2 * SHIFT, N)],
+        [patch, (N + 2 * SHIFT, N), frame],
         flops=3 * 10**9,
         bytes_accessed=3 * 10**6,
-    )(spots, counts, proj, probe, measured, tables)
-    *outgoing, _ = call(
+    )(spots, counts, proj, previous, core, probe, measured, tables)
+    *outgoing, total = call(
         edge_kernel,
-        [VMEM] * 10,
-        [message] * angles + [field],
-        [(2, 2, tile + N, N), (2, 2 * tile + 8, N), padded],
-        aliases={6: angles},
-    )(spots, counts, previous, core, cross, trans, inner, probe, measured, tables)
-    received = exchange(outgoing)
+        [VMEM] * 9,
+        [message] * (angles - 1) + [field],
+        [patch, frame, padded],
+        aliases={5: angles - 1},
+    )(spots, counts, previous, cross, trans, inner, probe, measured, tables)
+    own = call(own_kernel, [VMEM] * 2, [message], [padded])(total, outgoing[-1])[0]
+    received = exchange([own, *outgoing])
     early = list(range(angles - 1))
     sums = call(
         functools.partial(slab_kernel, angles, early, False),

time: 32.4 us -> 31.4 us (0.969)
  waiting for transfers between devices: 8.16 us -> 7.33 us
    ppermute x6, waiting for transfers between devices: 8.04 us -> 7.13 us  [exchange(): lax.ppermute(messages[d], 'ang', [(i, (i + d) % count) for i in range(cou...]
    pallas_call x3 -> x4, Pallas kernels: 4.82 us -> 4.55 us  [the longest x1 2.55 us: on_device(): call(inner_kernel, [VMEM] * 8, [field, field], [patch, (N + 2 * SHIFT, N)...]
  transfers between devices with their start and end apart: 9 -> 9, of which waited for: 5 -> 5; matrix products, arithmetic and copies ran while one was open for 0% -> 0% of each run, Pallas kernels for 14% -> 15%
where the time goes in v6:
time: 31.4 us; the launch traced here: 31.3 us
  starting transfers between devices  13.9 us (44%)
  Pallas kernels  8.64 us (28%)
  waiting for transfers between devices  7.33 us (23%)
  between operations  1.37 us (4%)
    ppermute x6, starting transfers between devices, exchange(): lax.ppermute(messages[d], 'ang', [(i, (i + d) % count) for i in range(cou...  11.2 us
    ppermute x6, waiting for transfers between devices, exchange(): lax.ppermute(messages[d], 'ang', [(i, (i + d) % count) for i in range(cou...  7.13 us
    ppermute x3, starting transfers between devices, on_rows(): lax.ppermute(value, 'rows', [(i, target(i) % count) for i in range(count)])  2.75 us
    pallas_call x1, Pallas kernels, on_device(): call(inner_kernel, [VMEM] * 8, [field, field], [patch, (N + 2 * SHIFT, N)...  2.55 us
    pallas_call x1, Pallas kernels, on_device(): call(edge_kernel, [VMEM] * 9, [message] * (angles - 1) + [field], [patch,...  1.51 us
    pallas_call x1, Pallas kernels, on_device(): call(functools.partial(first_kernel, angles), [HBM] * 5, [(slab, f32), (s...  1.24 us
    pallas_call x1, Pallas kernels, on_device(): call(load_kernel, [SMEM] + [VMEM] * 4 + [HBM] * 3, [message, ((8, N), i32...  1.21 us
    pallas_call x1, Pallas kernels, on_device(): call(functools.partial(slab_kernel, angles, [angles - 1], True), [VMEM] *...  0.87 us
  transfers between devices with their start and end apart: 9, of which 5 were waited for; matrix products, arithmetic and copies ran while one was open for 0% of the time, Pallas kernels for 15%

profile of v6, /device:TPU:0, one launch (start us, length us, event | category | flops | bytes accessed | tf_op | source)
XLA Modules:
  0.0 31.3 jit_solution(10576682784491556364)
XLA Ops:
  0.6 1.2 %shard_map.95 = (f32[272,128]{1,0:T(8,128)S(1)}, f32[272,128]{1,0:T(8,128)S(1)}, s32[8,128]{1,0:T(8,128)S(1)}, bf16[312,128]{1,0:T(8,128)(2,1)S(1)}, f32[144,128]{1,0:T(8,128)S(1)}) custom-call(s32[2,4]{1,0:T(2,128)} %bitcast.13, s32[2,4]{1,0:T(2,128)} %bitcast.14, f32[272,128]{1,0:T(8,128)} %bitcast.11, f32[272,128]{1,0:T(8,128)} %bitcast.12, ...), custom_call_target="tpu_custom_call" | custom-call | tf_op jit(solution)/shard_map/pallas_call | solution.py:460
  1.9 3.1 %collective-permute-start.2 = (bf16[312,128]{1,0:T(8,128)(2,1)S(1)}, bf16[312,128]{1,0:T(8,128)(2,1)S(1)}, u32[]{:S(2)}, u32[]{:S(2)}) collective-permute-start(bf16[312,128]{1,0:T(8,128)(2,1)S(1)} %get-tuple-element.37), channel_id=1, source_target_pairs={{0,1},{1,2},{2,3},{3,0},{4,5},{5,6},{6,7},{7,4},{8,9},{9,10},{10,1... | collective-permute-start | bytes 239624 | tf_op jit(solution)/shard_map/ppermute | solution.py:437
  5.0 0.4 %shard_map.96 = (bf16[312,128]{1,0:T(8,128)(2,1)S(1)}, bf16[312,128]{1,0:T(8,128)(2,1)S(1)}, f32[144,128]{1,0:T(8,128)S(1)}) custom-call(s32[8,128]{1,0:T(8,128)S(1)} %get-tuple-element.28.shifts, f32[272,128]{1,0:T(8,128)S(1)} %get-tuple-element.29.slab_delta, f32[272,128]{1,0:T(8,128)S(1)} %get-tuple-element.30.slab_beta, ...), custom_call_target="tpu_custom_call", output_to_operand_aliasing={{2}: (3, {})} | custom-call | tf_op jit(solution)/shard_map/pallas_call | solution.py:466
  5.3 0.1 collective-permute-start
  5.4 2.7 %collective-permute-start.3 = (bf16[312,128]{1,0:T(8,128)(2,1)S(1)}, bf16[312,128]{1,0:T(8,128)(2,1)S(1)}, u32[]{:S(2)}, u32[]{:S(2)}) collective-permute-start(bf16[312,128]{1,0:T(8,128)(2,1)S(1)} %get-tuple-element.38), channel_id=1, source_target_pairs={{0,2},{1,3},{2,0},{3,1},{4,6},{5,7},{6,4},{7,5},{8,10},{9,11},{10,... | collective-permute-start | bytes 239624 | tf_op jit(solution)/shard_map/ppermute | solution.py:437
  8.1 1.3 %collective-permute-start.1 = (bf16[312,128]{1,0:T(8,128)(2,1)S(1)}, bf16[312,128]{1,0:T(8,128)(2,1)S(1)}, u32[]{:S(2)}, u32[]{:S(2)}) collective-permute-start(bf16[312,128]{1,0:T(8,128)(2,1)S(1)} %get-tuple-element.32._), channel_id=1, source_target_pairs={{0,3},{1,0},{2,1},{3,2},{4,7},{5,4},{6,5},{7,6},{8,11},{9,8},{10,9... | collective-permute-start | bytes 239624 | tf_op jit(solution)/shard_map/ppermute | solution.py:437
  10.1 1.2 %shard_map.97 = (bf16[312,128]{1,0:T(8,128)(2,1)S(1)}, s32[8,128]{1,0:T(8,128)S(1)}, s32[2,4]{1,0:T(2,128)S(1)}, f32[2,128,128]{2,1,0:T(8,128)S(1)}, f32[4,128,128]{2,1,0:T(8,128)S(1)}) custom-call(s32[1,1]{1,0:T(1,128)S(6)} %copy.18.counts_in, s32[8,128]{1,0:T(8,128)S(1)} %get-tuple-element.28.shifts, f32[272,128]{1,0:T(8,128)S(1)} %get-tuple-element.29.slab_delta, ...), custom_call_target="tpu_custom_call" | custom-call | flops 1000000000 | bytes 1000000 | tf_op jit(solution)/shard_map/pallas_call | solution.py:469
  11.3 1.2 %collective-permute-done.3.refs_2_ = bf16[312,128]{1,0:T(8,128)(2,1)S(1)} collective-permute-done((bf16[312,128]{1,0:T(8,128)(2,1)S(1)}, bf16[312,128]{1,0:T(8,128)(2,1)S(1)}, u32[]{:S(2)}, u32[]{:S(2)}) %collective-permute-start.3) | collective-permute-done | bytes 79904 | tf_op jit(solution)/shard_map/ppermute | solution.py:437
  12.5 0.1 shard_map.98
  12.7 0.8 %collective-permute-done.1.message = bf16[312,128]{1,0:T(8,128)(2,1)S(1)} collective-permute-done((bf16[312,128]{1,0:T(8,128)(2,1)S(1)}, bf16[312,128]{1,0:T(8,128)(2,1)S(1)}, u32[]{:S(2)}, u32[]{:S(2)}) %collective-permute-start.1) | collective-permute-done | bytes 79904 | tf_op jit(solution)/shard_map/ppermute | solution.py:437
  13.5 0.3 %shard_map.99 = (bf16[256,128]{1,0:T(8,128)(2,1)S(1)}, bf16[256,128]{1,0:T(8,128)(2,1)S(1)}, f32[2,4,136,128]{3,2,1,0:T(8,128)S(1)}, f32[4,272,128]{2,1,0:T(8,128)S(1)}) custom-call(s32[2,4]{1,0:T(2,128)S(1)} %get-tuple-element.33.spots, f32[144,128]{1,0:T(8,128)S(1)} %collective-permute-done.slot.slot0, ...), custom_call_target="tpu_custom_call", output_to_operand_aliasing={{2}: (3, {}), {3}: (4, {})} | custom-call | tf_op jit(solution)/shard_map/pallas_call | solution.py:489
  13.8 0.4 %collective-permute-start.5 = (bf16[256,128]{1,0:T(8,128)(2,1)S(1)}, bf16[256,128]{1,0:T(8,128)(2,1)S(1)}, u32[]{:S(2)}, u32[]{:S(2)}) collective-permute-start(bf16[256,128]{1,0:T(8,128)(2,1)S(1)} %get-tuple-element.43), channel_id=1, source_target_pairs={{0,4},{4,0},{8,12},{12,8},{16,20},{20,16},{24,28},{28,24},{1,5},{5... | collective-permute-start | bytes 196616 | tf_op jit(solution)/shard_map/ppermute | solution.py:443
  14.2 2.3 %collective-permute-start.4 = (bf16[256,128]{1,0:T(8,128)(2,1)S(1)}, bf16[256,128]{1,0:T(8,128)(2,1)S(1)}, u32[]{:S(2)}, u32[]{:S(2)}) collective-permute-start(bf16[256,128]{1,0:T(8,128)(2,1)S(1)} %get-tuple-element.41), channel_id=1, source_target_pairs={{0,28},{4,8},{8,4},{12,16},{16,12},{20,24},{24,20},{28,0},{1,29},{... | collective-permute-start | bytes 196616 | tf_op jit(solution)/shard_map/ppermute | solution.py:443
  16.5 2.5 %shard_map.100 = (f32[2,4,136,128]{3,2,1,0:T(8,128)S(1)}, f32[2,4,136,128]{3,2,1,0:T(8,128)S(1)}) custom-call(s32[2,4]{1,0:T(2,128)S(1)} %get-tuple-element.33.spots, s32[8,128]{1,0:T(8,128)S(1)} %get-tuple-element.34.counts, f32[2,4,136,128]{3,2,1,0:T(8,128)S(1)} %get-tuple-element.42.proj, f32[144,128]{1,0:T(8,128)S(1)} %collective-permute-done.slot.slot0, ...), custom_call_target="tpu_custom_call" | custom-call | flops 3000000000 | bytes 3000000 | tf_op jit(solution)/shard_map/pallas_call | solution.py:495
  19.0 0.2 collective-permute-done.4.cross
  19.2 1.5 %shard_map.101 = (bf16[312,128]{1,0:T(8,128)(2,1)S(1)}, bf16[312,128]{1,0:T(8,128)(2,1)S(1)}, bf16[312,128]{1,0:T(8,128)(2,1)S(1)}, f32[2,4,136,128]{3,2,1,0:T(8,128)S(1)}) custom-call(s32[2,4]{1,0:T(2,128)S(1)} %get-tuple-element.33.spots, s32[8,128]{1,0:T(8,128)S(1)} %get-tuple-element.34.counts, ...), custom_call_target="tpu_custom_call", output_to_operand_aliasing={{3}: (5, {})} | custom-call | tf_op jit(solution)/shard_map/pallas_call | solution.py:503
  20.8 1.6 %collective-permute-start.7 = (bf16[312,128]{1,0:T(8,128)(2,1)S(1)}, bf16[312,128]{1,0:T(8,128)(2,1)S(1)}, u32[]{:S(2)}, u32[]{:S(2)}) collective-permute-start(bf16[312,128]{1,0:T(8,128)(2,1)S(1)} %get-tuple-element.50), channel_id=1, source_target_pairs={{0,1},{1,2},{2,3},{3,0},{4,5},{5,6},{6,7},{7,4},{8,9},{9,10},{10,1... | collective-permute-start | bytes 239624 | tf_op jit(solution)/shard_map/ppermute | solution.py:437
  22.4 2.1 %collective-permute-start.8 = (bf16[312,128]{1,0:T(8,128)(2,1)S(1)}, bf16[312,128]{1,0:T(8,128)(2,1)S(1)}, u32[]{:S(2)}, u32[]{:S(2)}) collective-permute-start(bf16[312,128]{1,0:T(8,128)(2,1)S(1)} %get-tuple-element.51), channel_id=1, source_target_pairs={{0,2},{1,3},{2,0},{3,1},{4,6},{5,7},{6,4},{7,5},{8,10},{9,11},{10,... | collective-permute-start | bytes 239624 | tf_op jit(solution)/shard_map/ppermute | solution.py:437
  24.5 0.3 %collective-permute-start.6 = (bf16[312,128]{1,0:T(8,128)(2,1)S(1)}, bf16[312,128]{1,0:T(8,128)(2,1)S(1)}, u32[]{:S(2)}, u32[]{:S(2)}) collective-permute-start(bf16[312,128]{1,0:T(8,128)(2,1)S(1)} %get-tuple-element.48._), channel_id=1, source_target_pairs={{0,3},{1,0},{2,1},{3,2},{4,7},{5,4},{6,5},{7,6},{8,11},{9,8},{10,9... | collective-permute-start | bytes 239624 | tf_op jit(solution)/shard_map/ppermute | solution.py:437
  24.8 0.1 shard_map.102.refs_0_
  24.9 3.0 %collective-permute-done.7.refs_1_ = bf16[312,128]{1,0:T(8,128)(2,1)S(1)} collective-permute-done((bf16[312,128]{1,0:T(8,128)(2,1)S(1)}, bf16[312,128]{1,0:T(8,128)(2,1)S(1)}, u32[]{:S(2)}, u32[]{:S(2)}) %collective-permute-start.7) | collective-permute-done | bytes 79904 | tf_op jit(solution)/shard_map/ppermute | solution.py:437
  27.9 2.1 %collective-permute-done.8.refs_2_ = bf16[312,128]{1,0:T(8,128)(2,1)S(1)} collective-permute-done((bf16[312,128]{1,0:T(8,128)(2,1)S(1)}, bf16[312,128]{1,0:T(8,128)(2,1)S(1)}, u32[]{:S(2)}, u32[]{:S(2)}) %collective-permute-start.8) | collective-permute-done | bytes 79904 | tf_op jit(solution)/shard_map/ppermute | solution.py:437
  30.0 0.3 %shard_map.103.refs_1_ = f32[2,2,136,128]{3,2,1,0:T(8,128)S(1)} custom-call(s32[8,128]{1,0:T(8,128)S(1)} %get-tuple-element.28.shifts, bf16[312,128]{1,0:T(8,128)(2,1)S(1)} %shard_map.102.refs_0_, bf16[312,128]{1,0:T(8,128)(2,1)S(1)} %collective-permute-done.7.refs_1_, bf16[312,128]{1,0:T(8,128)(2,1)S(1)} %collective-permute-done.8.refs_2_), custom_call_target="tpu_custom_call" | custom-call | flops 1000000000 | bytes 1000000 | tf_op jit(solution)/shard_map/pallas_call | solution.py:513
  30.4 0.9 %shard_map.104 = (f32[272,128]{1,0:T(8,128)}, f32[272,128]{1,0:T(8,128)}) custom-call(s32[8,128]{1,0:T(8,128)S(1)} %get-tuple-element.28.shifts, bf16[312,128]{1,0:T(8,128)(2,1)S(1)} %collective-permute-done.6.refs_0_, f32[2,2,136,128]{3,2,1,0:T(8,128)S(1)} %shard_map.103.refs_1_), custom_call_target="tpu_custom_call" | custom-call | tf_op jit(solution)/shard_map/pallas_call | solution.py:520
  (6 shorter events, 0.0 us)
Async XLA Ops:
  1.9 9.4 %collective-permute-start.2 = (bf16[312,128]{1,0:T(8,128)(2,1)S(1)}, bf16[312,128]{1,0:T(8,128)(2,1)S(1)}, u32[]{:S(2)}, u32[]{:S(2)}) collective-permute-start(bf16[312,128]{1,0:T(8,128)(2,1)S(1)} %get-tuple-element.37), channel_id=1, source_target_pairs={{0,1},{1,2},{2,3},{3,0},{4,5},{5,6},{6,7},{7,4},{8,9},{9,10},{10,1... | collective-permute-start | bytes 239624 | tf_op jit(solution)/shard_map/ppermute | solution.py:437
  5.3 7.3 %collective-permute-start = (f32[144,128]{1,0:T(8,128)S(1)}, f32[144,128]{1,0:T(8,128)S(1)}, u32[]{:S(2)}, u32[]{:S(2)}) collective-permute-start(f32[144,128]{1,0:T(8,128)S(1)} %get-tuple-element.35), channel_id=1, source_target_pairs={{0,4},{4,8},{8,12},{12,16},{16,20},{20,24},{24,28},{28,0},{1,5},{5... | collective-permute-start | bytes 221192 | tf_op jit(solution)/shard_map/ppermute | solution.py:443
  5.4 7.1 %collective-permute-start.3 = (bf16[312,128]{1,0:T(8,128)(2,1)S(1)}, bf16[312,128]{1,0:T(8,128)(2,1)S(1)}, u32[]{:S(2)}, u32[]{:S(2)}) collective-permute-start(bf16[312,128]{1,0:T(8,128)(2,1)S(1)} %get-tuple-element.38), channel_id=1, source_target_pairs={{0,2},{1,3},{2,0},{3,1},{4,6},{5,7},{6,4},{7,5},{8,10},{9,11},{10,... | collective-permute-start | bytes 239624 | tf_op jit(solution)/shard_map/ppermute | solution.py:437
  8.1 5.4 %collective-permute-start.1 = (bf16[312,128]{1,0:T(8,128)(2,1)S(1)}, bf16[312,128]{1,0:T(8,128)(2,1)S(1)}, u32[]{:S(2)}, u32[]{:S(2)}) collective-permute-start(bf16[312,128]{1,0:T(8,128)(2,1)S(1)} %get-tuple-element.32._), channel_id=1, source_target_pairs={{0,3},{1,0},{2,1},{3,2},{4,7},{5,4},{6,5},{7,6},{8,11},{9,8},{10,9... | collective-permute-start | bytes 239624 | tf_op jit(solution)/shard_map/ppermute | solution.py:437
  13.5 3.0 %copy-start = (bf16[4,256,256]{2,1,0:T(8,128)(2,1)S(1)}, bf16[4,256,256]{2,1,0:T(8,128)(2,1)}, u32[]{:S(2)}) copy-start(bf16[4,256,256]{2,1,0:T(8,128)(2,1)} %constant.2.clone.tables) | copy-start | bytes 1572868
  13.8 2.7 %collective-permute-start.5 = (bf16[256,128]{1,0:T(8,128)(2,1)S(1)}, bf16[256,128]{1,0:T(8,128)(2,1)S(1)}, u32[]{:S(2)}, u32[]{:S(2)}) collective-permute-start(bf16[256,128]{1,0:T(8,128)(2,1)S(1)} %get-tuple-element.43), channel_id=1, source_target_pairs={{0,4},{4,0},{8,12},{12,8},{16,20},{20,16},{24,28},{28,24},{1,5},{5... | collective-permute-start | bytes 196616 | tf_op jit(solution)/shard_map/ppermute | solution.py:443
  14.2 5.0 %collective-permute-start.4 = (bf16[256,128]{1,0:T(8,128)(2,1)S(1)}, bf16[256,128]{1,0:T(8,128)(2,1)S(1)}, u32[]{:S(2)}, u32[]{:S(2)}) collective-permute-start(bf16[256,128]{1,0:T(8,128)(2,1)S(1)} %get-tuple-element.41), channel_id=1, source_target_pairs={{0,28},{4,8},{8,4},{12,16},{16,12},{20,24},{24,20},{28,0},{1,29},{... | collective-permute-start | bytes 196616 | tf_op jit(solution)/shard_map/ppermute | solution.py:443
  20.8 7.2 %collective-permute-start.7 = (bf16[312,128]{1,0:T(8,128)(2,1)S(1)}, bf16[312,128]{1,0:T(8,128)(2,1)S(1)}, u32[]{:S(2)}, u32[]{:S(2)}) collective-permute-start(bf16[312,128]{1,0:T(8,128)(2,1)S(1)} %get-tuple-element.50), channel_id=1, source_target_pairs={{0,1},{1,2},{2,3},{3,0},{4,5},{5,6},{6,7},{7,4},{8,9},{9,10},{10,1... | collective-permute-start | bytes 239624 | tf_op jit(solution)/shard_map/ppermute | solution.py:437
  22.4 7.7 %collective-permute-start.8 = (bf16[312,128]{1,0:T(8,128)(2,1)S(1)}, bf16[312,128]{1,0:T(8,128)(2,1)S(1)}, u32[]{:S(2)}, u32[]{:S(2)}) collective-permute-start(bf16[312,128]{1,0:T(8,128)(2,1)S(1)} %get-tuple-element.51), channel_id=1, source_target_pairs={{0,2},{1,3},{2,0},{3,1},{4,6},{5,7},{6,4},{7,5},{8,10},{9,11},{10,... | collective-permute-start | bytes 239624 | tf_op jit(solution)/shard_map/ppermute | solution.py:437
  24.5 5.9 %collective-permute-start.6 = (bf16[312,128]{1,0:T(8,128)(2,1)S(1)}, bf16[312,128]{1,0:T(8,128)(2,1)S(1)}, u32[]{:S(2)}, u32[]{:S(2)}) collective-permute-start(bf16[312,128]{1,0:T(8,128)(2,1)S(1)} %get-tuple-element.48._), channel_id=1, source_target_pairs={{0,3},{1,0},{2,1},{3,2},{4,7},{5,4},{6,5},{7,6},{8,11},{9,8},{10,9... | collective-permute-start | bytes 239624 | tf_op jit(solution)/shard_map/ppermute | solution.py:437

commit v7 on v6

--- a/solution.py
+++ b/solution.py
@@ -443,6 +443,21 @@
     return lax.ppermute(value, "rows", [(i, target(i) % count) for i in range(count)])
 
 
+def across_chips(value):
+    rows, angles = lax.axis_size("rows"), lax.axis_size("ang")
+    pairs = []
+    for i in range(rows):
+        for a in range(angles):
+            if i not in (0, rows - 1):
+                target = (i + 1 if i % 2 else i - 1, a)
+            elif angles % 2:
+                target = (rows - 1 - i, a)
+            else:
+                target = (i, a ^ 1)
+            pairs.append((i * angles + a, target[0] * angles + target[1]))
+    return lax.ppermute(value, ("rows", "ang"), pairs)
+
+
 def on_device(delta_obj, beta_obj, layer_shifts, illumination_field, amplitudes, positions, scan_counts):
     tile = delta_obj.shape[0]
     angles = lax.axis_size("ang")
@@ -490,7 +505,7 @@
         assemble_kernel, [VMEM] * 5, [halo, halo, field, rows], aliases={3: 2, 4: 3}
     )(spots, previous, received[-1], *partly)
     core = on_rows(core, lambda i: i ^ 1)
-    cross = on_rows(cross, lambda i: i + 1 if i % 2 else i - 1)
+    cross = across_chips(cross)
     patch, frame = (2, 2 * tile, N), (2, 2 * tile + N, N)
     trans, inner = call(
         inner_kernel,

time: 31.4 us -> 31 us (0.987)
  waiting for transfers between devices: 7.33 us -> 6.5 us
  starting transfers between devices: 13.9 us -> 14.3 us
    ppermute x3 -> x2, starting transfers between devices: 2.75 us -> 0.5 us  [on_rows(): lax.ppermute(value, 'rows', [(i, target(i) % count) for i in range(count)])]
    ppermute x0 -> x1, starting transfers between devices: none -> 1.62 us  [across_chips(): return lax.ppermute(value, ('rows', 'ang'), pairs)]
    ppermute x6, starting transfers between devices: 11.2 us -> 12.2 us  [exchange(): lax.ppermute(messages[d], 'ang', [(i, (i + d) % count) for i in range(cou...]
    ppermute x6, waiting for transfers between devices: 7.13 us -> 6.42 us  [exchange(): lax.ppermute(messages[d], 'ang', [(i, (i + d) % count) for i in range(cou...]
where the time goes in v7:
time: 31 us; the launch traced here: 30.8 us
  starting transfers between devices  14.3 us (46%)
  Pallas kernels  8.64 us (28%)
  waiting for transfers between devices  6.5 us (21%)
  between operations  1.37 us (4%)
    ppermute x6, starting transfers between devices, exchange(): lax.ppermute(messages[d], 'ang', [(i, (i + d) % count) for i in range(cou...  12.2 us
    ppermute x6, waiting for transfers between devices, exchange(): lax.ppermute(messages[d], 'ang', [(i, (i + d) % count) for i in range(cou...  6.42 us
    pallas_call x1, Pallas kernels, on_device(): call(inner_kernel, [VMEM] * 8, [field, field], [patch, (N + 2 * SHIFT, N)...  2.56 us
    ppermute x1, starting transfers between devices, across_chips(): return lax.ppermute(value, ('rows', 'ang'), pairs)  1.62 us
    pallas_call x1, Pallas kernels, on_device(): call(edge_kernel, [VMEM] * 9, [message] * (angles - 1) + [field], [patch,...  1.5 us
    pallas_call x1, Pallas kernels, on_device(): call(functools.partial(first_kernel, angles), [HBM] * 5, [(slab, f32), (s...  1.24 us
    pallas_call x1, Pallas kernels, on_device(): call(load_kernel, [SMEM] + [VMEM] * 4 + [HBM] * 3, [message, ((8, N), i32...  1.21 us
    pallas_call x1, Pallas kernels, on_device(): call(functools.partial(slab_kernel, angles, [angles - 1], True), [VMEM] *...  0.87 us
  transfers between devices with their start and end apart: 9, of which 5 were waited for; matrix products, arithmetic and copies ran while one was open for 0% of the time, Pallas kernels for 15%

profile of v7, /device:TPU:0, one launch (start us, length us, event | category | flops | bytes accessed | tf_op | source)
XLA Modules:
  0.0 30.8 jit_solution(6026249269810255307)
XLA Ops:
  0.6 1.2 %shard_map.95 = (f32[272,128]{1,0:T(8,128)S(1)}, f32[272,128]{1,0:T(8,128)S(1)}, s32[8,128]{1,0:T(8,128)S(1)}, bf16[312,128]{1,0:T(8,128)(2,1)S(1)}, f32[144,128]{1,0:T(8,128)S(1)}) custom-call(s32[2,4]{1,0:T(2,128)} %bitcast.13, s32[2,4]{1,0:T(2,128)} %bitcast.14, f32[272,128]{1,0:T(8,128)} %bitcast.11, f32[272,128]{1,0:T(8,128)} %bitcast.12, ...), custom_call_target="tpu_custom_call" | custom-call | tf_op jit(solution)/shard_map/pallas_call | solution.py:475
  1.9 3.1 %collective-permute-start.2 = (bf16[312,128]{1,0:T(8,128)(2,1)S(1)}, bf16[312,128]{1,0:T(8,128)(2,1)S(1)}, u32[]{:S(2)}, u32[]{:S(2)}) collective-permute-start(bf16[312,128]{1,0:T(8,128)(2,1)S(1)} %get-tuple-element.37), channel_id=1, source_target_pairs={{0,1},{1,2},{2,3},{3,0},{4,5},{5,6},{6,7},{7,4},{8,9},{9,10},{10,1... | collective-permute-start | bytes 239624 | tf_op jit(solution)/shard_map/ppermute | solution.py:437
  5.0 0.4 %shard_map.96 = (bf16[312,128]{1,0:T(8,128)(2,1)S(1)}, bf16[312,128]{1,0:T(8,128)(2,1)S(1)}, f32[144,128]{1,0:T(8,128)S(1)}) custom-call(s32[8,128]{1,0:T(8,128)S(1)} %get-tuple-element.28.shifts, f32[272,128]{1,0:T(8,128)S(1)} %get-tuple-element.29.slab_delta, f32[272,128]{1,0:T(8,128)S(1)} %get-tuple-element.30.slab_beta, ...), custom_call_target="tpu_custom_call", output_to_operand_aliasing={{2}: (3, {})} | custom-call | tf_op jit(solution)/shard_map/pallas_call | solution.py:481
  5.3 0.1 collective-permute-start
  5.4 2.7 %collective-permute-start.3 = (bf16[312,128]{1,0:T(8,128)(2,1)S(1)}, bf16[312,128]{1,0:T(8,128)(2,1)S(1)}, u32[]{:S(2)}, u32[]{:S(2)}) collective-permute-start(bf16[312,128]{1,0:T(8,128)(2,1)S(1)} %get-tuple-element.38), channel_id=1, source_target_pairs={{0,2},{1,3},{2,0},{3,1},{4,6},{5,7},{6,4},{7,5},{8,10},{9,11},{10,... | collective-permute-start | bytes 239624 | tf_op jit(solution)/shard_map/ppermute | solution.py:437
  8.1 1.3 %collective-permute-start.1 = (bf16[312,128]{1,0:T(8,128)(2,1)S(1)}, bf16[312,128]{1,0:T(8,128)(2,1)S(1)}, u32[]{:S(2)}, u32[]{:S(2)}) collective-permute-start(bf16[312,128]{1,0:T(8,128)(2,1)S(1)} %get-tuple-element.32._), channel_id=1, source_target_pairs={{0,3},{1,0},{2,1},{3,2},{4,7},{5,4},{6,5},{7,6},{8,11},{9,8},{10,9... | collective-permute-start | bytes 239624 | tf_op jit(solution)/shard_map/ppermute | solution.py:437
  10.1 1.2 %shard_map.97 = (bf16[312,128]{1,0:T(8,128)(2,1)S(1)}, s32[8,128]{1,0:T(8,128)S(1)}, s32[2,4]{1,0:T(2,128)S(1)}, f32[2,128,128]{2,1,0:T(8,128)S(1)}, f32[4,128,128]{2,1,0:T(8,128)S(1)}) custom-call(s32[1,1]{1,0:T(1,128)S(6)} %copy.18.counts_in, s32[8,128]{1,0:T(8,128)S(1)} %get-tuple-element.28.shifts, f32[272,128]{1,0:T(8,128)S(1)} %get-tuple-element.29.slab_delta, ...), custom_call_target="tpu_custom_call" | custom-call | flops 1000000000 | bytes 1000000 | tf_op jit(solution)/shard_map/pallas_call | solution.py:484
  11.3 1.2 %collective-permute-done.3.refs_2_ = bf16[312,128]{1,0:T(8,128)(2,1)S(1)} collective-permute-done((bf16[312,128]{1,0:T(8,128)(2,1)S(1)}, bf16[312,128]{1,0:T(8,128)(2,1)S(1)}, u32[]{:S(2)}, u32[]{:S(2)}) %collective-permute-start.3) | collective-permute-done | bytes 79904 | tf_op jit(solution)/shard_map/ppermute | solution.py:437
  12.5 0.1 shard_map.98
  12.7 0.8 %collective-permute-done.1.message = bf16[312,128]{1,0:T(8,128)(2,1)S(1)} collective-permute-done((bf16[312,128]{1,0:T(8,128)(2,1)S(1)}, bf16[312,128]{1,0:T(8,128)(2,1)S(1)}, u32[]{:S(2)}, u32[]{:S(2)}) %collective-permute-start.1) | collective-permute-done | bytes 79904 | tf_op jit(solution)/shard_map/ppermute | solution.py:437
  13.5 0.3 %shard_map.99 = (bf16[256,128]{1,0:T(8,128)(2,1)S(1)}, bf16[256,128]{1,0:T(8,128)(2,1)S(1)}, f32[2,4,136,128]{3,2,1,0:T(8,128)S(1)}, f32[4,272,128]{2,1,0:T(8,128)S(1)}) custom-call(s32[2,4]{1,0:T(2,128)S(1)} %get-tuple-element.33.spots, f32[144,128]{1,0:T(8,128)S(1)} %collective-permute-done.slot.slot0, ...), custom_call_target="tpu_custom_call", output_to_operand_aliasing={{2}: (3, {}), {3}: (4, {})} | custom-call | tf_op jit(solution)/shard_map/pallas_call | solution.py:504
  13.8 0.4 %collective-permute-start.5 = (bf16[256,128]{1,0:T(8,128)(2,1)S(1)}, bf16[256,128]{1,0:T(8,128)(2,1)S(1)}, u32[]{:S(2)}, u32[]{:S(2)}) collective-permute-start(bf16[256,128]{1,0:T(8,128)(2,1)S(1)} %get-tuple-element.43), channel_id=1, source_target_pairs={{0,4},{4,0},{8,12},{12,8},{16,20},{20,16},{24,28},{28,24},{1,5},{5... | collective-permute-start | bytes 196616 | tf_op jit(solution)/shard_map/ppermute | solution.py:443
  14.2 1.6 %collective-permute-start.4 = (bf16[256,128]{1,0:T(8,128)(2,1)S(1)}, bf16[256,128]{1,0:T(8,128)(2,1)S(1)}, u32[]{:S(2)}, u32[]{:S(2)}) collective-permute-start(bf16[256,128]{1,0:T(8,128)(2,1)S(1)} %get-tuple-element.41), channel_id=1, source_target_pairs={{0,1},{1,0},{2,3},{3,2},{4,8},{5,9},{6,10},{7,11},{8,4},{9,5},{10,... | collective-permute-start | bytes 196616 | tf_op jit(solution)/shard_map/ppermute | solution.py:458
  15.8 2.6 %shard_map.100 = (f32[2,4,136,128]{3,2,1,0:T(8,128)S(1)}, f32[2,4,136,128]{3,2,1,0:T(8,128)S(1)}) custom-call(s32[2,4]{1,0:T(2,128)S(1)} %get-tuple-element.33.spots, s32[8,128]{1,0:T(8,128)S(1)} %get-tuple-element.34.counts, f32[2,4,136,128]{3,2,1,0:T(8,128)S(1)} %get-tuple-element.42.proj, f32[144,128]{1,0:T(8,128)S(1)} %collective-permute-done.slot.slot0, ...), custom_call_target="tpu_custom_call" | custom-call | flops 3000000000 | bytes 3000000 | tf_op jit(solution)/shard_map/pallas_call | solution.py:510
  18.4 0.1 collective-permute-done.4.cross
  18.5 1.5 %shard_map.101 = (bf16[312,128]{1,0:T(8,128)(2,1)S(1)}, bf16[312,128]{1,0:T(8,128)(2,1)S(1)}, bf16[312,128]{1,0:T(8,128)(2,1)S(1)}, f32[2,4,136,128]{3,2,1,0:T(8,128)S(1)}) custom-call(s32[2,4]{1,0:T(2,128)S(1)} %get-tuple-element.33.spots, s32[8,128]{1,0:T(8,128)S(1)} %get-tuple-element.34.counts, ...), custom_call_target="tpu_custom_call", output_to_operand_aliasing={{3}: (5, {})} | custom-call | tf_op jit(solution)/shard_map/pallas_call | solution.py:518
  20.0 1.7 %collective-permute-start.7 = (bf16[312,128]{1,0:T(8,128)(2,1)S(1)}, bf16[312,128]{1,0:T(8,128)(2,1)S(1)}, u32[]{:S(2)}, u32[]{:S(2)}) collective-permute-start(bf16[312,128]{1,0:T(8,128)(2,1)S(1)} %get-tuple-element.50), channel_id=1, source_target_pairs={{0,1},{1,2},{2,3},{3,0},{4,5},{5,6},{6,7},{7,4},{8,9},{9,10},{10,1... | collective-permute-start | bytes 239624 | tf_op jit(solution)/shard_map/ppermute | solution.py:437
  21.7 2.2 %collective-permute-start.8 = (bf16[312,128]{1,0:T(8,128)(2,1)S(1)}, bf16[312,128]{1,0:T(8,128)(2,1)S(1)}, u32[]{:S(2)}, u32[]{:S(2)}) collective-permute-start(bf16[312,128]{1,0:T(8,128)(2,1)S(1)} %get-tuple-element.51), channel_id=1, source_target_pairs={{0,2},{1,3},{2,0},{3,1},{4,6},{5,7},{6,4},{7,5},{8,10},{9,11},{10,... | collective-permute-start | bytes 239624 | tf_op jit(solution)/shard_map/ppermute | solution.py:437
  23.9 1.2 %collective-permute-start.6 = (bf16[312,128]{1,0:T(8,128)(2,1)S(1)}, bf16[312,128]{1,0:T(8,128)(2,1)S(1)}, u32[]{:S(2)}, u32[]{:S(2)}) collective-permute-start(bf16[312,128]{1,0:T(8,128)(2,1)S(1)} %get-tuple-element.48._), channel_id=1, source_target_pairs={{0,3},{1,0},{2,1},{3,2},{4,7},{5,4},{6,5},{7,6},{8,11},{9,8},{10,9... | collective-permute-start | bytes 239624 | tf_op jit(solution)/shard_map/ppermute | solution.py:437
  25.1 0.1 shard_map.102.refs_0_
  25.2 2.0 %collective-permute-done.7.refs_1_ = bf16[312,128]{1,0:T(8,128)(2,1)S(1)} collective-permute-done((bf16[312,128]{1,0:T(8,128)(2,1)S(1)}, bf16[312,128]{1,0:T(8,128)(2,1)S(1)}, u32[]{:S(2)}, u32[]{:S(2)}) %collective-permute-start.7) | collective-permute-done | bytes 79904 | tf_op jit(solution)/shard_map/ppermute | solution.py:437
  27.3 2.4 %collective-permute-done.8.refs_2_ = bf16[312,128]{1,0:T(8,128)(2,1)S(1)} collective-permute-done((bf16[312,128]{1,0:T(8,128)(2,1)S(1)}, bf16[312,128]{1,0:T(8,128)(2,1)S(1)}, u32[]{:S(2)}, u32[]{:S(2)}) %collective-permute-start.8) | collective-permute-done | bytes 79904 | tf_op jit(solution)/shard_map/ppermute | solution.py:437
  29.6 0.3 %shard_map.103.refs_1_ = f32[2,2,136,128]{3,2,1,0:T(8,128)S(1)} custom-call(s32[8,128]{1,0:T(8,128)S(1)} %get-tuple-element.28.shifts, bf16[312,128]{1,0:T(8,128)(2,1)S(1)} %shard_map.102.refs_0_, bf16[312,128]{1,0:T(8,128)(2,1)S(1)} %collective-permute-done.7.refs_1_, bf16[312,128]{1,0:T(8,128)(2,1)S(1)} %collective-permute-done.8.refs_2_), custom_call_target="tpu_custom_call" | custom-call | flops 1000000000 | bytes 1000000 | tf_op jit(solution)/shard_map/pallas_call | solution.py:528
  30.0 0.9 %shard_map.104 = (f32[272,128]{1,0:T(8,128)}, f32[272,128]{1,0:T(8,128)}) custom-call(s32[8,128]{1,0:T(8,128)S(1)} %get-tuple-element.28.shifts, bf16[312,128]{1,0:T(8,128)(2,1)S(1)} %collective-permute-done.6.refs_0_, f32[2,2,136,128]{3,2,1,0:T(8,128)S(1)} %shard_map.103.refs_1_), custom_call_target="tpu_custom_call" | custom-call | tf_op jit(solution)/shard_map/pallas_call | solution.py:535
  (6 shorter events, 0.0 us)
Async XLA Ops:
  1.9 9.4 %collective-permute-start.2 = (bf16[312,128]{1,0:T(8,128)(2,1)S(1)}, bf16[312,128]{1,0:T(8,128)(2,1)S(1)}, u32[]{:S(2)}, u32[]{:S(2)}) collective-permute-start(bf16[312,128]{1,0:T(8,128)(2,1)S(1)} %get-tuple-element.37), channel_id=1, source_target_pairs={{0,1},{1,2},{2,3},{3,0},{4,5},{5,6},{6,7},{7,4},{8,9},{9,10},{10,1... | collective-permute-start | bytes 239624 | tf_op jit(solution)/shard_map/ppermute | solution.py:437
  5.3 7.3 %collective-permute-start = (f32[144,128]{1,0:T(8,128)S(1)}, f32[144,128]{1,0:T(8,128)S(1)}, u32[]{:S(2)}, u32[]{:S(2)}) collective-permute-start(f32[144,128]{1,0:T(8,128)S(1)} %get-tuple-element.35), channel_id=1, source_target_pairs={{0,4},{4,8},{8,12},{12,16},{16,20},{20,24},{24,28},{28,0},{1,5},{5... | collective-permute-start | bytes 221192 | tf_op jit(solution)/shard_map/ppermute | solution.py:443
  5.4 7.1 %collective-permute-start.3 = (bf16[312,128]{1,0:T(8,128)(2,1)S(1)}, bf16[312,128]{1,0:T(8,128)(2,1)S(1)}, u32[]{:S(2)}, u32[]{:S(2)}) collective-permute-start(bf16[312,128]{1,0:T(8,128)(2,1)S(1)} %get-tuple-element.38), channel_id=1, source_target_pairs={{0,2},{1,3},{2,0},{3,1},{4,6},{5,7},{6,4},{7,5},{8,10},{9,11},{10,... | collective-permute-start | bytes 239624 | tf_op jit(solution)/shard_map/ppermute | solution.py:437
  8.1 5.4 %collective-permute-start.1 = (bf16[312,128]{1,0:T(8,128)(2,1)S(1)}, bf16[312,128]{1,0:T(8,128)(2,1)S(1)}, u32[]{:S(2)}, u32[]{:S(2)}) collective-permute-start(bf16[312,128]{1,0:T(8,128)(2,1)S(1)} %get-tuple-element.32._), channel_id=1, source_target_pairs={{0,3},{1,0},{2,1},{3,2},{4,7},{5,4},{6,5},{7,6},{8,11},{9,8},{10,9... | collective-permute-start | bytes 239624 | tf_op jit(solution)/shard_map/ppermute | solution.py:437
  13.5 2.4 %copy-start = (bf16[4,256,256]{2,1,0:T(8,128)(2,1)S(1)}, bf16[4,256,256]{2,1,0:T(8,128)(2,1)}, u32[]{:S(2)}) copy-start(bf16[4,256,256]{2,1,0:T(8,128)(2,1)} %constant.2.clone.tables) | copy-start | bytes 1572868
  13.8 2.1 %collective-permute-start.5 = (bf16[256,128]{1,0:T(8,128)(2,1)S(1)}, bf16[256,128]{1,0:T(8,128)(2,1)S(1)}, u32[]{:S(2)}, u32[]{:S(2)}) collective-permute-start(bf16[256,128]{1,0:T(8,128)(2,1)S(1)} %get-tuple-element.43), channel_id=1, source_target_pairs={{0,4},{4,0},{8,12},{12,8},{16,20},{20,16},{24,28},{28,24},{1,5},{5... | collective-permute-start | bytes 196616 | tf_op jit(solution)/shard_map/ppermute | solution.py:443
  14.2 4.3 %collective-permute-start.4 = (bf16[256,128]{1,0:T(8,128)(2,1)S(1)}, bf16[256,128]{1,0:T(8,128)(2,1)S(1)}, u32[]{:S(2)}, u32[]{:S(2)}) collective-permute-start(bf16[256,128]{1,0:T(8,128)(2,1)S(1)} %get-tuple-element.41), channel_id=1, source_target_pairs={{0,1},{1,0},{2,3},{3,2},{4,8},{5,9},{6,10},{7,11},{8,4},{9,5},{10,... | collective-permute-start | bytes 196616 | tf_op jit(solution)/shard_map/ppermute | solution.py:458
  20.0 7.3 %collective-permute-start.7 = (bf16[312,128]{1,0:T(8,128)(2,1)S(1)}, bf16[312,128]{1,0:T(8,128)(2,1)S(1)}, u32[]{:S(2)}, u32[]{:S(2)}) collective-permute-start(bf16[312,128]{1,0:T(8,128)(2,1)S(1)} %get-tuple-element.50), channel_id=1, source_target_pairs={{0,1},{1,2},{2,3},{3,0},{4,5},{5,6},{6,7},{7,4},{8,9},{9,10},{10,1... | collective-permute-start | bytes 239624 | tf_op jit(solution)/shard_map/ppermute | solution.py:437
  21.7 8.0 %collective-permute-start.8 = (bf16[312,128]{1,0:T(8,128)(2,1)S(1)}, bf16[312,128]{1,0:T(8,128)(2,1)S(1)}, u32[]{:S(2)}, u32[]{:S(2)}) collective-permute-start(bf16[312,128]{1,0:T(8,128)(2,1)S(1)} %get-tuple-element.51), channel_id=1, source_target_pairs={{0,2},{1,3},{2,0},{3,1},{4,6},{5,7},{6,4},{7,5},{8,10},{9,11},{10,... | collective-permute-start | bytes 239624 | tf_op jit(solution)/shard_map/ppermute | solution.py:437
  23.9 6.1 %collective-permute-start.6 = (bf16[312,128]{1,0:T(8,128)(2,1)S(1)}, bf16[312,128]{1,0:T(8,128)(2,1)S(1)}, u32[]{:S(2)}, u32[]{:S(2)}) collective-permute-start(bf16[312,128]{1,0:T(8,128)(2,1)S(1)} %get-tuple-element.48._), channel_id=1, source_target_pairs={{0,3},{1,0},{2,1},{3,2},{4,7},{5,4},{6,5},{7,6},{8,11},{9,8},{10,9... | collective-permute-start | bytes 239624 | tf_op jit(solution)/shard_map/ppermute | solution.py:437

commit v8 on v7

--- a/solution.py
+++ b/solution.py
@@ -195,21 +195,16 @@
 
 
 def transmit(phase, absorb):
-    turns = jnp.round(phase * (2.0 / math.pi))
-    r = phase - turns * 1.5703125
-    r = r - turns * 4.837512969970703125e-4
-    r = r - turns * 7.54978995489188e-8
+    turns = jnp.round(phase * (1.0 / math.pi))
+    r = (phase - turns * 3.140625) - turns * 9.67653589793e-4
     z = r * r
-    sine = r + r * z * (-1.6666654611e-1 + z * (8.3321608736e-3 - z * 1.9515295891e-4))
-    cosine = 1.0 - 0.5 * z + z * z * (4.166664568298827e-2 + z * (-1.388731625493765e-3 + z * 2.443315711809948e-5))
-    quarter = turns.astype(i32)
-    odd = (quarter & 1) == 1
+    sine = r + r * z * (-1.66666597e-1 + z * (8.33307858e-3 + z * (-1.98106050e-4 + z * 2.60541672e-6)))
+    cosine = 1.0 + z * (
+        -0.5 + z * (4.16666418e-2 + z * (-1.38883968e-3 + z * (2.47596343e-5 - z * 2.60512e-7)))
+    )
     damping = jnp.exp(-absorb)
-    out_cos = jnp.where(odd, sine, cosine)
-    out_sin = jnp.where(odd, cosine, sine)
-    out_cos = jnp.where(((quarter + 1) & 2) == 2, -out_cos, out_cos)
-    out_sin = jnp.where((quarter & 2) == 2, -out_sin, out_sin)
-    return damping * out_cos, damping * out_sin
+    damping = jnp.where((turns.astype(i32) & 1) == 1, -damping, damping)
+    return damping * cosine, damping * sine
 
 
 def split(value):
@@ -228,7 +223,9 @@
 
 def times_left(high, low, value):
     vh, vl = split(value)
-    return dot(high, vh) + (dot(high, vl) + dot(low, vh))
+    n = value.shape[1]
+    both = dot(high, jnp.concatenate([vh, vl], 1))
+    return both[:, :n] + (both[:, n:] + dot(low, vh))
 
 
 def scan_gradients(patches, measured, weights, probe, tables):

time: 31 us -> 30.9 us (level)
  no operation moved by 1% of the time
where the time goes in v8:
time: 30.9 us; the launch traced here: 30.7 us
  starting transfers between devices  14.2 us (46%)
  Pallas kernels  8.46 us (27%)
  waiting for transfers between devices  6.66 us (22%)
  between operations  1.37 us (4%)
    ppermute x6, starting transfers between devices, exchange(): lax.ppermute(messages[d], 'ang', [(i, (i + d) % count) for i in range(cou...  12.1 us
    ppermute x6, waiting for transfers between devices, exchange(): lax.ppermute(messages[d], 'ang', [(i, (i + d) % count) for i in range(cou...  6.5 us
    pallas_call x1, Pallas kernels, on_device(): call(inner_kernel, [VMEM] * 8, [field, field], [patch, (N + 2 * SHIFT, N)...  2.48 us
    ppermute x1, starting transfers between devices, across_chips(): return lax.ppermute(value, ('rows', 'ang'), pairs)  1.62 us
    pallas_call x1, Pallas kernels, on_device(): call(edge_kernel, [VMEM] * 9, [message] * (angles - 1) + [field], [patch,...  1.4 us
    pallas_call x1, Pallas kernels, on_device(): call(functools.partial(first_kernel, angles), [HBM] * 5, [(slab, f32), (s...  1.24 us
    pallas_call x1, Pallas kernels, on_device(): call(load_kernel, [SMEM] + [VMEM] * 4 + [HBM] * 3, [message, ((8, N), i32...  1.21 us
    pallas_call x1, Pallas kernels, on_device(): call(functools.partial(slab_kernel, angles, [angles - 1], True), [VMEM] *...  0.87 us
  transfers between devices with their start and end apart: 9, of which 5 were waited for; matrix products, arithmetic and copies ran while one was open for 0% of the time, Pallas kernels for 15%

profile of v8, /device:TPU:0, one launch (start us, length us, event | category | flops | bytes accessed | tf_op | source)
XLA Modules:
  0.0 30.7 jit_solution(1319636753177357565)
XLA Ops:
  0.6 1.2 %shard_map.95 = (f32[272,128]{1,0:T(8,128)S(1)}, f32[272,128]{1,0:T(8,128)S(1)}, s32[8,128]{1,0:T(8,128)S(1)}, bf16[312,128]{1,0:T(8,128)(2,1)S(1)}, f32[144,128]{1,0:T(8,128)S(1)}) custom-call(s32[2,4]{1,0:T(2,128)} %bitcast.13, s32[2,4]{1,0:T(2,128)} %bitcast.14, f32[272,128]{1,0:T(8,128)} %bitcast.11, f32[272,128]{1,0:T(8,128)} %bitcast.12, ...), custom_call_target="tpu_custom_call" | custom-call | tf_op jit(solution)/shard_map/pallas_call | solution.py:472
  1.9 3.1 %collective-permute-start.2 = (bf16[312,128]{1,0:T(8,128)(2,1)S(1)}, bf16[312,128]{1,0:T(8,128)(2,1)S(1)}, u32[]{:S(2)}, u32[]{:S(2)}) collective-permute-start(bf16[312,128]{1,0:T(8,128)(2,1)S(1)} %get-tuple-element.37), channel_id=1, source_target_pairs={{0,1},{1,2},{2,3},{3,0},{4,5},{5,6},{6,7},{7,4},{8,9},{9,10},{10,1... | collective-permute-start | bytes 239624 | tf_op jit(solution)/shard_map/ppermute | solution.py:434
  5.0 0.4 %shard_map.96 = (bf16[312,128]{1,0:T(8,128)(2,1)S(1)}, bf16[312,128]{1,0:T(8,128)(2,1)S(1)}, f32[144,128]{1,0:T(8,128)S(1)}) custom-call(s32[8,128]{1,0:T(8,128)S(1)} %get-tuple-element.28.shifts, f32[272,128]{1,0:T(8,128)S(1)} %get-tuple-element.29.slab_delta, f32[272,128]{1,0:T(8,128)S(1)} %get-tuple-element.30.slab_beta, ...), custom_call_target="tpu_custom_call", output_to_operand_aliasing={{2}: (3, {})} | custom-call | tf_op jit(solution)/shard_map/pallas_call | solution.py:478
  5.3 0.1 collective-permute-start
  5.4 2.7 %collective-permute-start.3 = (bf16[312,128]{1,0:T(8,128)(2,1)S(1)}, bf16[312,128]{1,0:T(8,128)(2,1)S(1)}, u32[]{:S(2)}, u32[]{:S(2)}) collective-permute-start(bf16[312,128]{1,0:T(8,128)(2,1)S(1)} %get-tuple-element.38), channel_id=1, source_target_pairs={{0,2},{1,3},{2,0},{3,1},{4,6},{5,7},{6,4},{7,5},{8,10},{9,11},{10,... | collective-permute-start | bytes 239624 | tf_op jit(solution)/shard_map/ppermute | solution.py:434
  8.1 1.3 %collective-permute-start.1 = (bf16[312,128]{1,0:T(8,128)(2,1)S(1)}, bf16[312,128]{1,0:T(8,128)(2,1)S(1)}, u32[]{:S(2)}, u32[]{:S(2)}) collective-permute-start(bf16[312,128]{1,0:T(8,128)(2,1)S(1)} %get-tuple-element.32._), channel_id=1, source_target_pairs={{0,3},{1,0},{2,1},{3,2},{4,7},{5,4},{6,5},{7,6},{8,11},{9,8},{10,9... | collective-permute-start | bytes 239624 | tf_op jit(solution)/shard_map/ppermute | solution.py:434
  10.1 1.2 %shard_map.97 = (bf16[312,128]{1,0:T(8,128)(2,1)S(1)}, s32[8,128]{1,0:T(8,128)S(1)}, s32[2,4]{1,0:T(2,128)S(1)}, f32[2,128,128]{2,1,0:T(8,128)S(1)}, f32[4,128,128]{2,1,0:T(8,128)S(1)}) custom-call(s32[1,1]{1,0:T(1,128)S(6)} %copy.18.counts_in, s32[8,128]{1,0:T(8,128)S(1)} %get-tuple-element.28.shifts, f32[272,128]{1,0:T(8,128)S(1)} %get-tuple-element.29.slab_delta, ...), custom_call_target="tpu_custom_call" | custom-call | flops 1000000000 | bytes 1000000 | tf_op jit(solution)/shard_map/pallas_call | solution.py:481
  11.3 1.2 %collective-permute-done.3.refs_2_ = bf16[312,128]{1,0:T(8,128)(2,1)S(1)} collective-permute-done((bf16[312,128]{1,0:T(8,128)(2,1)S(1)}, bf16[312,128]{1,0:T(8,128)(2,1)S(1)}, u32[]{:S(2)}, u32[]{:S(2)}) %collective-permute-start.3) | collective-permute-done | bytes 79904 | tf_op jit(solution)/shard_map/ppermute | solution.py:434
  12.5 0.1 shard_map.98
  12.7 0.8 %collective-permute-done.1.message = bf16[312,128]{1,0:T(8,128)(2,1)S(1)} collective-permute-done((bf16[312,128]{1,0:T(8,128)(2,1)S(1)}, bf16[312,128]{1,0:T(8,128)(2,1)S(1)}, u32[]{:S(2)}, u32[]{:S(2)}) %collective-permute-start.1) | collective-permute-done | bytes 79904 | tf_op jit(solution)/shard_map/ppermute | solution.py:434
  13.5 0.3 %shard_map.99 = (bf16[256,128]{1,0:T(8,128)(2,1)S(1)}, bf16[256,128]{1,0:T(8,128)(2,1)S(1)}, f32[2,4,136,128]{3,2,1,0:T(8,128)S(1)}, f32[4,272,128]{2,1,0:T(8,128)S(1)}) custom-call(s32[2,4]{1,0:T(2,128)S(1)} %get-tuple-element.33.spots, f32[144,128]{1,0:T(8,128)S(1)} %collective-permute-done.slot.slot0, ...), custom_call_target="tpu_custom_call", output_to_operand_aliasing={{2}: (3, {}), {3}: (4, {})} | custom-call | tf_op jit(solution)/shard_map/pallas_call | solution.py:501
  13.8 0.4 %collective-permute-start.5 = (bf16[256,128]{1,0:T(8,128)(2,1)S(1)}, bf16[256,128]{1,0:T(8,128)(2,1)S(1)}, u32[]{:S(2)}, u32[]{:S(2)}) collective-permute-start(bf16[256,128]{1,0:T(8,128)(2,1)S(1)} %get-tuple-element.43), channel_id=1, source_target_pairs={{0,4},{4,0},{8,12},{12,8},{16,20},{20,16},{24,28},{28,24},{1,5},{5... | collective-permute-start | bytes 196616 | tf_op jit(solution)/shard_map/ppermute | solution.py:440
  14.2 1.6 %collective-permute-start.4 = (bf16[256,128]{1,0:T(8,128)(2,1)S(1)}, bf16[256,128]{1,0:T(8,128)(2,1)S(1)}, u32[]{:S(2)}, u32[]{:S(2)}) collective-permute-start(bf16[256,128]{1,0:T(8,128)(2,1)S(1)} %get-tuple-element.41), channel_id=1, source_target_pairs={{0,1},{1,0},{2,3},{3,2},{4,8},{5,9},{6,10},{7,11},{8,4},{9,5},{10,... | collective-permute-start | bytes 196616 | tf_op jit(solution)/shard_map/ppermute | solution.py:455
  15.8 2.5 %shard_map.100 = (f32[2,4,136,128]{3,2,1,0:T(8,128)S(1)}, f32[2,4,136,128]{3,2,1,0:T(8,128)S(1)}) custom-call(s32[2,4]{1,0:T(2,128)S(1)} %get-tuple-element.33.spots, s32[8,128]{1,0:T(8,128)S(1)} %get-tuple-element.34.counts, f32[2,4,136,128]{3,2,1,0:T(8,128)S(1)} %get-tuple-element.42.proj, f32[144,128]{1,0:T(8,128)S(1)} %collective-permute-done.slot.slot0, ...), custom_call_target="tpu_custom_call" | custom-call | flops 3000000000 | bytes 3000000 | tf_op jit(solution)/shard_map/pallas_call | solution.py:507
  18.3 0.2 collective-permute-done.4.cross
  18.5 1.4 %shard_map.101 = (bf16[312,128]{1,0:T(8,128)(2,1)S(1)}, bf16[312,128]{1,0:T(8,128)(2,1)S(1)}, bf16[312,128]{1,0:T(8,128)(2,1)S(1)}, f32[2,4,136,128]{3,2,1,0:T(8,128)S(1)}) custom-call(s32[2,4]{1,0:T(2,128)S(1)} %get-tuple-element.33.spots, s32[8,128]{1,0:T(8,128)S(1)} %get-tuple-element.34.counts, ...), custom_call_target="tpu_custom_call", output_to_operand_aliasing={{3}: (5, {})} | custom-call | tf_op jit(solution)/shard_map/pallas_call | solution.py:515
  19.9 1.6 %collective-permute-start.7 = (bf16[312,128]{1,0:T(8,128)(2,1)S(1)}, bf16[312,128]{1,0:T(8,128)(2,1)S(1)}, u32[]{:S(2)}, u32[]{:S(2)}) collective-permute-start(bf16[312,128]{1,0:T(8,128)(2,1)S(1)} %get-tuple-element.50), channel_id=1, source_target_pairs={{0,1},{1,2},{2,3},{3,0},{4,5},{5,6},{6,7},{7,4},{8,9},{9,10},{10,1... | collective-permute-start | bytes 239624 | tf_op jit(solution)/shard_map/ppermute | solution.py:434
  21.5 2.2 %collective-permute-start.8 = (bf16[312,128]{1,0:T(8,128)(2,1)S(1)}, bf16[312,128]{1,0:T(8,128)(2,1)S(1)}, u32[]{:S(2)}, u32[]{:S(2)}) collective-permute-start(bf16[312,128]{1,0:T(8,128)(2,1)S(1)} %get-tuple-element.51), channel_id=1, source_target_pairs={{0,2},{1,3},{2,0},{3,1},{4,6},{5,7},{6,4},{7,5},{8,10},{9,11},{10,... | collective-permute-start | bytes 239624 | tf_op jit(solution)/shard_map/ppermute | solution.py:434
  23.8 1.2 %collective-permute-start.6 = (bf16[312,128]{1,0:T(8,128)(2,1)S(1)}, bf16[312,128]{1,0:T(8,128)(2,1)S(1)}, u32[]{:S(2)}, u32[]{:S(2)}) collective-permute-start(bf16[312,128]{1,0:T(8,128)(2,1)S(1)} %get-tuple-element.48._), channel_id=1, source_target_pairs={{0,3},{1,0},{2,1},{3,2},{4,7},{5,4},{6,5},{7,6},{8,11},{9,8},{10,9... | collective-permute-start | bytes 239624 | tf_op jit(solution)/shard_map/ppermute | solution.py:434
  24.9 0.1 shard_map.102.refs_0_
  25.0 2.1 %collective-permute-done.7.refs_1_ = bf16[312,128]{1,0:T(8,128)(2,1)S(1)} collective-permute-done((bf16[312,128]{1,0:T(8,128)(2,1)S(1)}, bf16[312,128]{1,0:T(8,128)(2,1)S(1)}, u32[]{:S(2)}, u32[]{:S(2)}) %collective-permute-start.7) | collective-permute-done | bytes 79904 | tf_op jit(solution)/shard_map/ppermute | solution.py:434
  27.1 2.4 %collective-permute-done.8.refs_2_ = bf16[312,128]{1,0:T(8,128)(2,1)S(1)} collective-permute-done((bf16[312,128]{1,0:T(8,128)(2,1)S(1)}, bf16[312,128]{1,0:T(8,128)(2,1)S(1)}, u32[]{:S(2)}, u32[]{:S(2)}) %collective-permute-start.8) | collective-permute-done | bytes 79904 | tf_op jit(solution)/shard_map/ppermute | solution.py:434
  29.5 0.3 %shard_map.103.refs_1_ = f32[2,2,136,128]{3,2,1,0:T(8,128)S(1)} custom-call(s32[8,128]{1,0:T(8,128)S(1)} %get-tuple-element.28.shifts, bf16[312,128]{1,0:T(8,128)(2,1)S(1)} %shard_map.102.refs_0_, bf16[312,128]{1,0:T(8,128)(2,1)S(1)} %collective-permute-done.7.refs_1_, bf16[312,128]{1,0:T(8,128)(2,1)S(1)} %collective-permute-done.8.refs_2_), custom_call_target="tpu_custom_call" | custom-call | flops 1000000000 | bytes 1000000 | tf_op jit(solution)/shard_map/pallas_call | solution.py:525
  29.8 0.9 %shard_map.104 = (f32[272,128]{1,0:T(8,128)}, f32[272,128]{1,0:T(8,128)}) custom-call(s32[8,128]{1,0:T(8,128)S(1)} %get-tuple-element.28.shifts, bf16[312,128]{1,0:T(8,128)(2,1)S(1)} %collective-permute-done.6.refs_0_, f32[2,2,136,128]{3,2,1,0:T(8,128)S(1)} %shard_map.103.refs_1_), custom_call_target="tpu_custom_call" | custom-call | tf_op jit(solution)/shard_map/pallas_call | solution.py:532
  (6 shorter events, 0.0 us)
Async XLA Ops:
  1.9 9.4 %collective-permute-start.2 = (bf16[312,128]{1,0:T(8,128)(2,1)S(1)}, bf16[312,128]{1,0:T(8,128)(2,1)S(1)}, u32[]{:S(2)}, u32[]{:S(2)}) collective-permute-start(bf16[312,128]{1,0:T(8,128)(2,1)S(1)} %get-tuple-element.37), channel_id=1, source_target_pairs={{0,1},{1,2},{2,3},{3,0},{4,5},{5,6},{6,7},{7,4},{8,9},{9,10},{10,1... | collective-permute-start | bytes 239624 | tf_op jit(solution)/shard_map/ppermute | solution.py:434
  5.3 7.3 %collective-permute-start = (f32[144,128]{1,0:T(8,128)S(1)}, f32[144,128]{1,0:T(8,128)S(1)}, u32[]{:S(2)}, u32[]{:S(2)}) collective-permute-start(f32[144,128]{1,0:T(8,128)S(1)} %get-tuple-element.35), channel_id=1, source_target_pairs={{0,4},{4,8},{8,12},{12,16},{16,20},{20,24},{24,28},{28,0},{1,5},{5... | collective-permute-start | bytes 221192 | tf_op jit(solution)/shard_map/ppermute | solution.py:440
  5.4 7.1 %collective-permute-start.3 = (bf16[312,128]{1,0:T(8,128)(2,1)S(1)}, bf16[312,128]{1,0:T(8,128)(2,1)S(1)}, u32[]{:S(2)}, u32[]{:S(2)}) collective-permute-start(bf16[312,128]{1,0:T(8,128)(2,1)S(1)} %get-tuple-element.38), channel_id=1, source_target_pairs={{0,2},{1,3},{2,0},{3,1},{4,6},{5,7},{6,4},{7,5},{8,10},{9,11},{10,... | collective-permute-start | bytes 239624 | tf_op jit(solution)/shard_map/ppermute | solution.py:434
  8.1 5.4 %collective-permute-start.1 = (bf16[312,128]{1,0:T(8,128)(2,1)S(1)}, bf16[312,128]{1,0:T(8,128)(2,1)S(1)}, u32[]{:S(2)}, u32[]{:S(2)}) collective-permute-start(bf16[312,128]{1,0:T(8,128)(2,1)S(1)} %get-tuple-element.32._), channel_id=1, source_target_pairs={{0,3},{1,0},{2,1},{3,2},{4,7},{5,4},{6,5},{7,6},{8,11},{9,8},{10,9... | collective-permute-start | bytes 239624 | tf_op jit(solution)/shard_map/ppermute | solution.py:434
  13.5 2.4 %copy-start = (bf16[4,256,256]{2,1,0:T(8,128)(2,1)S(1)}, bf16[4,256,256]{2,1,0:T(8,128)(2,1)}, u32[]{:S(2)}) copy-start(bf16[4,256,256]{2,1,0:T(8,128)(2,1)} %constant.2.clone.tables) | copy-start | bytes 1572868
  13.8 2.1 %collective-permute-start.5 = (bf16[256,128]{1,0:T(8,128)(2,1)S(1)}, bf16[256,128]{1,0:T(8,128)(2,1)S(1)}, u32[]{:S(2)}, u32[]{:S(2)}) collective-permute-start(bf16[256,128]{1,0:T(8,128)(2,1)S(1)} %get-tuple-element.43), channel_id=1, source_target_pairs={{0,4},{4,0},{8,12},{12,8},{16,20},{20,16},{24,28},{28,24},{1,5},{5... | collective-permute-start | bytes 196616 | tf_op jit(solution)/shard_map/ppermute | solution.py:440
  14.2 4.3 %collective-permute-start.4 = (bf16[256,128]{1,0:T(8,128)(2,1)S(1)}, bf16[256,128]{1,0:T(8,128)(2,1)S(1)}, u32[]{:S(2)}, u32[]{:S(2)}) collective-permute-start(bf16[256,128]{1,0:T(8,128)(2,1)S(1)} %get-tuple-element.41), channel_id=1, source_target_pairs={{0,1},{1,0},{2,3},{3,2},{4,8},{5,9},{6,10},{7,11},{8,4},{9,5},{10,... | collective-permute-start | bytes 196616 | tf_op jit(solution)/shard_map/ppermute | solution.py:455
  19.9 7.2 %collective-permute-start.7 = (bf16[312,128]{1,0:T(8,128)(2,1)S(1)}, bf16[312,128]{1,0:T(8,128)(2,1)S(1)}, u32[]{:S(2)}, u32[]{:S(2)}) collective-permute-start(bf16[312,128]{1,0:T(8,128)(2,1)S(1)} %get-tuple-element.50), channel_id=1, source_target_pairs={{0,1},{1,2},{2,3},{3,0},{4,5},{5,6},{6,7},{7,4},{8,9},{9,10},{10,1... | collective-permute-start | bytes 239624 | tf_op jit(solution)/shard_map/ppermute | solution.py:434
  21.5 8.0 %collective-permute-start.8 = (bf16[312,128]{1,0:T(8,128)(2,1)S(1)}, bf16[312,128]{1,0:T(8,128)(2,1)S(1)}, u32[]{:S(2)}, u32[]{:S(2)}) collective-permute-start(bf16[312,128]{1,0:T(8,128)(2,1)S(1)} %get-tuple-element.51), channel_id=1, source_target_pairs={{0,2},{1,3},{2,0},{3,1},{4,6},{5,7},{6,4},{7,5},{8,10},{9,11},{10,... | collective-permute-start | bytes 239624 | tf_op jit(solution)/shard_map/ppermute | solution.py:434
  23.8 6.1 %collective-permute-start.6 = (bf16[312,128]{1,0:T(8,128)(2,1)S(1)}, bf16[312,128]{1,0:T(8,128)(2,1)S(1)}, u32[]{:S(2)}, u32[]{:S(2)}) collective-permute-start(bf16[312,128]{1,0:T(8,128)(2,1)S(1)} %get-tuple-element.48._), channel_id=1, source_target_pairs={{0,3},{1,0},{2,1},{3,2},{4,7},{5,4},{6,5},{7,6},{8,11},{9,8},{10,9... | collective-permute-start | bytes 239624 | tf_op jit(solution)/shard_map/ppermute | solution.py:434

commit v9 on v8

--- a/solution.py
+++ b/solution.py
@@ -160,35 +160,57 @@
     return lax.rem(lax.axis_index("rows"), 2) == 0
 
 
-def unpack_kernel(blocks, steps, *refs):
-    received, (proj, margins) = refs[: len(steps)], refs[-2:]
+def unpack(message, block, proj, margins):
     tile = proj.shape[2]
+    message = message.astype(f32)
+    proj[0, block] = message[:tile]
+    proj[1, block] = message[tile : 2 * tile]
+    margins[block] = margins_of(message, 2 * tile)
+
+
+def add_margins(proj, margins, block, before=None, after=None):
+    tile = proj.shape[2]
+    lane = lane_iota(tile)
+    for c in range(2):
+        part = slice(c * tile, (c + 1) * tile)
+        value = proj[c, block]
+        if before is not None:
+            value += jnp.where(lane < SHIFT, margins[before, part], 0.0)
+        if after is not None:
+            value += jnp.where(lane >= N - SHIFT, margins[after, part], 0.0)
+        proj[c, block] = value
+
+
+def unpack_kernel(*refs):
+    received, (proj, margins) = refs[:-2], refs[-2:]
+    count = proj.shape[1]
     me = lax.axis_index("ang")
-    for d, ref in zip(steps, received):
-        block = lax.rem(me + (blocks - d), blocks)
-        message = ref[...].astype(f32)
-        proj[0, block] = message[:tile]
-        proj[1, block] = message[tile : 2 * tile]
-        margins[block] = margins_of(message, 2 * tile)
+    blocks = [lax.rem(me + (count - d), count) for d in range(count)]
+    for block, ref in zip(blocks, received):
+        unpack(ref[...], block, proj, margins)
+    for d in range(count - 1):
+        before = blocks[d + 1] if d < count - 2 else None
+        after = blocks[d - 1] if d > 0 else None
+        add_margins(proj, margins, blocks[d], before, after)
 
 
 def assemble_kernel(spots, slot, message, proj_in, margins_in, core, cross, proj, margins):
-    blocks, tile = proj.shape[1], proj.shape[2]
-    unpack_kernel(blocks, [blocks - 1], message, proj, margins)
-    lane = lane_iota(tile)
-    for block in range(blocks):
-        before, after = (block - 1) % blocks, (block + 1) % blocks
-        for c in range(2):
-            part = slice(c * tile, (c + 1) * tile)
-            extra = jnp.where(lane < SHIFT, margins[before, part], 0.0)
-            extra += jnp.where(lane >= N - SHIFT, margins[after, part], 0.0)
-            proj[c, block] += extra
+    blocks = proj.shape[1]
+    me = lax.axis_index("ang")
+    last, following = lax.rem(me + 1, blocks), lax.rem(me + 2, blocks)
     _, previous = slot_position(slot)
     own = spots[1, 0]
+    even = is_even()
+    places = [
+        (out, upper, block_of(jnp.where(upper, own, previous), blocks))
+        for out, upper in ((core, even), (cross, jnp.logical_not(even)))
+    ]
+    unpack(message[...], last, proj, margins)
+    add_margins(proj, margins, last, me, following)
+    add_margins(proj, margins, me, None, last)
+    add_margins(proj, margins, following, last, None)
     lane = lane_iota(N)
-    even = is_even()
-    for out, upper in ((core, even), (cross, jnp.logical_not(even))):
-        first, second, offset = block_of(jnp.where(upper, own, previous), blocks)
+    for out, upper, (first, second, offset) in places:
         rows = pl.ds(pl.multiple_of(jnp.where(upper, EDGE_ROWS, 0), 8), N)
         pair = patch_of(proj, lane, offset, first, second, rows)
         out[...] = jnp.concatenate(pair, 0).astype(bf16)
@@ -325,6 +347,10 @@
 
 def inner_kernel(spots, counts, proj, slot0, core, probe, measured, tables, trans, grad, patch, frame, edge_frame):
     blocks, tile = proj.shape[1], proj.shape[2]
+    slots = measured.shape[0]
+    inner = [
+        (jnp.minimum(spots[0, slot], EDGE_ROWS), *block_of(spots[1, slot], blocks)) for slot in range(1, slots)
+    ]
     for block in range(blocks):
         re, im = transmit(proj[0, block], proj[1, block])
         trans[0, block] = re
@@ -332,15 +358,13 @@
     grad[...] = jnp.zeros(grad.shape, f32)
     frame[0:SHIFT, :] = jnp.zeros((SHIFT, N), f32)
     frame[SHIFT + N :, :] = jnp.zeros((SHIFT, N), f32)
-    slots = measured.shape[0]
     lane = lane_iota(N)
     is_own = is_even()
     pair, columns, place = edge_patch(is_own, spots, slot0, core, trans, patch)
     patches, weights = [pair], [edge_weight(is_own, counts, slot0)]
     patterns = [jnp.where(is_own, measured[0], slot0[0:N, :])]
     for slot in range(1, slots):
-        row = jnp.minimum(spots[0, slot], EDGE_ROWS)
-        first, second, offset = block_of(spots[1, slot], blocks)
+        row, first, second, offset = inner[slot - 1]
         patches.append(patch_of(trans, lane, offset, first, second, pl.ds(row, N)))
         weights.append(jnp.where(slot < counts[0, 0], 1.0, 0.0).astype(f32))
         patterns.append(measured[slot])
@@ -348,8 +372,7 @@
     add_edge(grad, chain_back(patches[0], grads[0]), columns, place, edge_frame)
     lane = lane_iota(tile)
     for slot in range(1, slots):
-        row = jnp.minimum(spots[0, slot], EDGE_ROWS)
-        first, second, offset = block_of(spots[1, slot], blocks)
+        row, first, second, offset = inner[slot - 1]
         chained = chain_back(patches[slot], grads[slot])
         for c in range(2):
             frame[SHIFT : SHIFT + N, :] = chained[c]
@@ -370,17 +393,24 @@
 
 
 def edge_kernel(spots, counts, slot0, cross, trans, _, probe, measured, tables, *refs):
-    outs, (total, patch, frame, scratch) = refs[:-4], refs[-4:]
+    out, total, patch, frame, scratch = refs
     blocks = trans.shape[1]
     is_own = jnp.logical_not(is_even())
+    weight = edge_weight(is_own, counts, slot0)
     pair, columns, place = edge_patch(is_own, spots, slot0, cross, trans, patch)
     pattern = jnp.where(is_own, measured[0], slot0[0:N, :])
-    weight = edge_weight(is_own, counts, slot0)
     grads = scan_gradients([pair], [pattern], [weight], probe, tables)
     add_edge(total, chain_back(pair, grads[0]), columns, place, frame)
+    following = lax.rem(lax.axis_index("ang") + 1, blocks)
+    out[...] = gradient_message(following, total, scratch)
+
+
+def cut_kernel(total, *refs):
+    outs, scratch = refs[:-1], refs[-1]
+    blocks = total.shape[1]
     me = lax.axis_index("ang")
     for k, out in enumerate(outs):
-        out[...] = gradient_message(lax.rem(me + k + 1, blocks), total, scratch)
+        out[...] = gradient_message(lax.rem(me + k + 2, blocks), total, scratch)
 
 
 def own_kernel(total, _, out, scratch):
@@ -490,9 +520,8 @@
     received = exchange(windows)
     previous = on_rows(slot, lambda i: i + 1)
     rows = ((angles, 2 * tile, N), f32)
-    early = list(range(angles - 1))
     partly = call(
-        functools.partial(unpack_kernel, angles, early),
+        unpack_kernel,
         [VMEM] * (angles - 1),
         [field, rows],
         flops=10**9,
@@ -512,13 +541,14 @@
         flops=3 * 10**9,
         bytes_accessed=3 * 10**6,
     )(spots, counts, proj, previous, core, probe, measured, tables)
-    *outgoing, total = call(
+    following, total = call(
         edge_kernel,
         [VMEM] * 9,
-        [message] * (angles - 1) + [field],
+        [message, field],
         [patch, frame, padded],
-        aliases={5: angles - 1},
+        aliases={5: 1},
     )(spots, counts, previous, cross, trans, inner, probe, measured, tables)
+    outgoing = [following, *call(cut_kernel, [VMEM], [message] * (angles - 2), [padded])(total)]
     own = call(own_kernel, [VMEM] * 2, [message], [padded])(total, outgoing[-1])[0]
     received = exchange([own, *outgoing])
     early = list(range(angles - 1))

time: 30.9 us -> 31 us (level)
    pallas_call x2 -> x3, Pallas kernels: 1.53 us -> 1.65 us  [the longest x1 1.31 us: on_device(): call(edge_kernel, [VMEM] * 9, [message, field], [patch, frame, padded], a...]
  transfers between devices with their start and end apart: 9 -> 9, of which waited for: 5 -> 6; matrix products, arithmetic and copies ran while one was open for 0% -> 0% of each run, Pallas kernels for 15% -> 15%
where the time goes in v9:
time: 31 us; the launch traced here: 30.8 us
  starting transfers between devices  14.3 us (46%)
  Pallas kernels  8.49 us (27%)
  waiting for transfers between devices  6.67 us (22%)
  between operations  1.37 us (4%)
    ppermute x6, starting transfers between devices, exchange(): lax.ppermute(messages[d], 'ang', [(i, (i + d) % count) for i in range(cou...  12.2 us
    ppermute x6, waiting for transfers between devices, exchange(): lax.ppermute(messages[d], 'ang', [(i, (i + d) % count) for i in range(cou...  6.37 us
    pallas_call x1, Pallas kernels, on_device(): call(inner_kernel, [VMEM] * 8, [field, field], [patch, (N + 2 * SHIFT, N)...  2.41 us
    ppermute x1, starting transfers between devices, across_chips(): return lax.ppermute(value, ('rows', 'ang'), pairs)  1.55 us
    pallas_call x1, Pallas kernels, on_device(): call(edge_kernel, [VMEM] * 9, [message, field], [patch, frame, padded], a...  1.31 us
    pallas_call x1, Pallas kernels, on_device(): call(functools.partial(first_kernel, angles), [HBM] * 5, [(slab, f32), (s...  1.24 us
    pallas_call x1, Pallas kernels, on_device(): call(load_kernel, [SMEM] + [VMEM] * 4 + [HBM] * 3, [message, ((8, N), i32...  1.21 us
    pallas_call x1, Pallas kernels, on_device(): call(functools.partial(slab_kernel, angles, [angles - 1], True), [VMEM] *...  0.87 us
  transfers between devices with their start and end apart: 9, of which 6 were waited for; matrix products, arithmetic and copies ran while one was open for 0% of the time, Pallas kernels for 15%

profile of v9, /device:TPU:0, one launch (start us, length us, event | category | flops | bytes accessed | tf_op | source)
XLA Modules:
  0.0 30.8 jit_solution(11147765625508140426)
XLA Ops:
  0.6 1.2 %shard_map.95 = (f32[272,128]{1,0:T(8,128)S(1)}, f32[272,128]{1,0:T(8,128)S(1)}, s32[8,128]{1,0:T(8,128)S(1)}, bf16[312,128]{1,0:T(8,128)(2,1)S(1)}, f32[144,128]{1,0:T(8,128)S(1)}) custom-call(s32[2,4]{1,0:T(2,128)} %bitcast.13, s32[2,4]{1,0:T(2,128)} %bitcast.14, f32[272,128]{1,0:T(8,128)} %bitcast.11, f32[272,128]{1,0:T(8,128)} %bitcast.12, ...), custom_call_target="tpu_custom_call" | custom-call | tf_op jit(solution)/shard_map/pallas_call | solution.py:502
  1.9 3.1 %collective-permute-start.2 = (bf16[312,128]{1,0:T(8,128)(2,1)S(1)}, bf16[312,128]{1,0:T(8,128)(2,1)S(1)}, u32[]{:S(2)}, u32[]{:S(2)}) collective-permute-start(bf16[312,128]{1,0:T(8,128)(2,1)S(1)} %get-tuple-element.37), channel_id=1, source_target_pairs={{0,1},{1,2},{2,3},{3,0},{4,5},{5,6},{6,7},{7,4},{8,9},{9,10},{10,1... | collective-permute-start | bytes 239624 | tf_op jit(solution)/shard_map/ppermute | solution.py:464
  5.0 0.4 %shard_map.96 = (bf16[312,128]{1,0:T(8,128)(2,1)S(1)}, bf16[312,128]{1,0:T(8,128)(2,1)S(1)}, f32[144,128]{1,0:T(8,128)S(1)}) custom-call(s32[8,128]{1,0:T(8,128)S(1)} %get-tuple-element.28.shifts, f32[272,128]{1,0:T(8,128)S(1)} %get-tuple-element.29.slab_delta, f32[272,128]{1,0:T(8,128)S(1)} %get-tuple-element.30.slab_beta, ...), custom_call_target="tpu_custom_call", output_to_operand_aliasing={{2}: (3, {})} | custom-call | tf_op jit(solution)/shard_map/pallas_call | solution.py:508
  5.4 2.7 %collective-permute-start.3 = (bf16[312,128]{1,0:T(8,128)(2,1)S(1)}, bf16[312,128]{1,0:T(8,128)(2,1)S(1)}, u32[]{:S(2)}, u32[]{:S(2)}) collective-permute-start(bf16[312,128]{1,0:T(8,128)(2,1)S(1)} %get-tuple-element.38), channel_id=1, source_target_pairs={{0,2},{1,3},{2,0},{3,1},{4,6},{5,7},{6,4},{7,5},{8,10},{9,11},{10,... | collective-permute-start | bytes 239624 | tf_op jit(solution)/shard_map/ppermute | solution.py:464
  8.1 1.3 %collective-permute-start.1 = (bf16[312,128]{1,0:T(8,128)(2,1)S(1)}, bf16[312,128]{1,0:T(8,128)(2,1)S(1)}, u32[]{:S(2)}, u32[]{:S(2)}) collective-permute-start(bf16[312,128]{1,0:T(8,128)(2,1)S(1)} %get-tuple-element.32._), channel_id=1, source_target_pairs={{0,3},{1,0},{2,1},{3,2},{4,7},{5,4},{6,5},{7,6},{8,11},{9,8},{10,9... | collective-permute-start | bytes 239624 | tf_op jit(solution)/shard_map/ppermute | solution.py:464
  10.1 1.2 %shard_map.97 = (bf16[312,128]{1,0:T(8,128)(2,1)S(1)}, s32[8,128]{1,0:T(8,128)S(1)}, s32[2,4]{1,0:T(2,128)S(1)}, f32[2,128,128]{2,1,0:T(8,128)S(1)}, f32[4,128,128]{2,1,0:T(8,128)S(1)}) custom-call(s32[1,1]{1,0:T(1,128)S(6)} %copy.18.counts_in, s32[8,128]{1,0:T(8,128)S(1)} %get-tuple-element.28.shifts, f32[272,128]{1,0:T(8,128)S(1)} %get-tuple-element.29.slab_delta, ...), custom_call_target="tpu_custom_call" | custom-call | flops 1000000000 | bytes 1000000 | tf_op jit(solution)/shard_map/pallas_call | solution.py:511
  11.3 1.2 %collective-permute-done.3.refs_2_ = bf16[312,128]{1,0:T(8,128)(2,1)S(1)} collective-permute-done((bf16[312,128]{1,0:T(8,128)(2,1)S(1)}, bf16[312,128]{1,0:T(8,128)(2,1)S(1)}, u32[]{:S(2)}, u32[]{:S(2)}) %collective-permute-start.3) | collective-permute-done | bytes 79904 | tf_op jit(solution)/shard_map/ppermute | solution.py:464
  12.5 0.2 shard_map.98
  12.7 0.7 %collective-permute-done.1.message = bf16[312,128]{1,0:T(8,128)(2,1)S(1)} collective-permute-done((bf16[312,128]{1,0:T(8,128)(2,1)S(1)}, bf16[312,128]{1,0:T(8,128)(2,1)S(1)}, u32[]{:S(2)}, u32[]{:S(2)}) %collective-permute-start.1) | collective-permute-done | bytes 79904 | tf_op jit(solution)/shard_map/ppermute | solution.py:464
  13.5 0.3 shard_map.99
  13.8 0.5 %collective-permute-start.5 = (bf16[256,128]{1,0:T(8,128)(2,1)S(1)}, bf16[256,128]{1,0:T(8,128)(2,1)S(1)}, u32[]{:S(2)}, u32[]{:S(2)}) collective-permute-start(bf16[256,128]{1,0:T(8,128)(2,1)S(1)} %get-tuple-element.43), channel_id=1, source_target_pairs={{0,4},{4,0},{8,12},{12,8},{16,20},{20,16},{24,28},{28,24},{1,5},{5... | collective-permute-start | bytes 196616 | tf_op jit(solution)/shard_map/ppermute | solution.py:470
  14.3 1.5 %collective-permute-start.4 = (bf16[256,128]{1,0:T(8,128)(2,1)S(1)}, bf16[256,128]{1,0:T(8,128)(2,1)S(1)}, u32[]{:S(2)}, u32[]{:S(2)}) collective-permute-start(bf16[256,128]{1,0:T(8,128)(2,1)S(1)} %get-tuple-element.41), channel_id=1, source_target_pairs={{0,1},{1,0},{2,3},{3,2},{4,8},{5,9},{6,10},{7,11},{8,4},{9,5},{10,... | collective-permute-start | bytes 196616 | tf_op jit(solution)/shard_map/ppermute | solution.py:485
  15.8 2.4 %shard_map.100 = (f32[2,4,136,128]{3,2,1,0:T(8,128)S(1)}, f32[2,4,136,128]{3,2,1,0:T(8,128)S(1)}) custom-call(s32[2,4]{1,0:T(2,128)S(1)} %get-tuple-element.33.spots, s32[8,128]{1,0:T(8,128)S(1)} %get-tuple-element.34.counts, f32[2,4,136,128]{3,2,1,0:T(8,128)S(1)} %get-tuple-element.42.proj, f32[144,128]{1,0:T(8,128)S(1)} %collective-permute-done.slot.slot0, ...), custom_call_target="tpu_custom_call" | custom-call | flops 3000000000 | bytes 3000000 | tf_op jit(solution)/shard_map/pallas_call | solution.py:536
  18.2 0.3 collective-permute-done.4.cross
  18.5 1.3 %shard_map.101 = (bf16[312,128]{1,0:T(8,128)(2,1)S(1)}, f32[2,4,136,128]{3,2,1,0:T(8,128)S(1)}) custom-call(s32[2,4]{1,0:T(2,128)S(1)} %get-tuple-element.33.spots, s32[8,128]{1,0:T(8,128)S(1)} %get-tuple-element.34.counts, f32[144,128]{1,0:T(8,128)S(1)} %collective-permute-done.slot.slot0, ...), custom_call_target="tpu_custom_call", output_to_operand_aliasing={{1}: (5, {})} | custom-call | tf_op jit(solution)/shard_map/pallas_call | solution.py:544
  19.9 1.6 %collective-permute-start.7 = (bf16[312,128]{1,0:T(8,128)(2,1)S(1)}, bf16[312,128]{1,0:T(8,128)(2,1)S(1)}, u32[]{:S(2)}, u32[]{:S(2)}) collective-permute-start(bf16[312,128]{1,0:T(8,128)(2,1)S(1)} %get-tuple-element.50), channel_id=1, source_target_pairs={{0,1},{1,2},{2,3},{3,0},{4,5},{5,6},{6,7},{7,4},{8,9},{9,10},{10,1... | collective-permute-start | bytes 239624 | tf_op jit(solution)/shard_map/ppermute | solution.py:464
  21.5 0.1 shard_map.102
  21.6 2.3 %collective-permute-start.8 = (bf16[312,128]{1,0:T(8,128)(2,1)S(1)}, bf16[312,128]{1,0:T(8,128)(2,1)S(1)}, u32[]{:S(2)}, u32[]{:S(2)}) collective-permute-start(bf16[312,128]{1,0:T(8,128)(2,1)S(1)} %get-tuple-element.51), channel_id=1, source_target_pairs={{0,2},{1,3},{2,0},{3,1},{4,6},{5,7},{6,4},{7,5},{8,10},{9,11},{10,... | collective-permute-start | bytes 239624 | tf_op jit(solution)/shard_map/ppermute | solution.py:464
  24.1 1.1 %collective-permute-start.6 = (bf16[312,128]{1,0:T(8,128)(2,1)S(1)}, bf16[312,128]{1,0:T(8,128)(2,1)S(1)}, u32[]{:S(2)}, u32[]{:S(2)}) collective-permute-start(bf16[312,128]{1,0:T(8,128)(2,1)S(1)} %get-tuple-element.49._), channel_id=1, source_target_pairs={{0,3},{1,0},{2,1},{3,2},{4,7},{5,4},{6,5},{7,6},{8,11},{9,8},{10,9... | collective-permute-start | bytes 239624 | tf_op jit(solution)/shard_map/ppermute | solution.py:464
  25.2 1.9 %collective-permute-done.7.refs_1_ = bf16[312,128]{1,0:T(8,128)(2,1)S(1)} collective-permute-done((bf16[312,128]{1,0:T(8,128)(2,1)S(1)}, bf16[312,128]{1,0:T(8,128)(2,1)S(1)}, u32[]{:S(2)}, u32[]{:S(2)}) %collective-permute-start.7) | collective-permute-done | bytes 79904 | tf_op jit(solution)/shard_map/ppermute | solution.py:464
  27.1 2.2 %collective-permute-done.8.refs_2_ = bf16[312,128]{1,0:T(8,128)(2,1)S(1)} collective-permute-done((bf16[312,128]{1,0:T(8,128)(2,1)S(1)}, bf16[312,128]{1,0:T(8,128)(2,1)S(1)}, u32[]{:S(2)}, u32[]{:S(2)}) %collective-permute-start.8) | collective-permute-done | bytes 79904 | tf_op jit(solution)/shard_map/ppermute | solution.py:464
  29.3 0.3 %shard_map.104.refs_1_ = f32[2,2,136,128]{3,2,1,0:T(8,128)S(1)} custom-call(s32[8,128]{1,0:T(8,128)S(1)} %get-tuple-element.28.shifts, bf16[312,128]{1,0:T(8,128)(2,1)S(1)} %shard_map.103.refs_0_, bf16[312,128]{1,0:T(8,128)(2,1)S(1)} %collective-permute-done.7.refs_1_, bf16[312,128]{1,0:T(8,128)(2,1)S(1)} %collective-permute-done.8.refs_2_), custom_call_target="tpu_custom_call" | custom-call | flops 1000000000 | bytes 1000000 | tf_op jit(solution)/shard_map/pallas_call | solution.py:555
  29.7 0.3 collective-permute-done.6.refs_0_
  29.9 0.9 %shard_map.105 = (f32[272,128]{1,0:T(8,128)}, f32[272,128]{1,0:T(8,128)}) custom-call(s32[8,128]{1,0:T(8,128)S(1)} %get-tuple-element.28.shifts, bf16[312,128]{1,0:T(8,128)(2,1)S(1)} %collective-permute-done.6.refs_0_, f32[2,2,136,128]{3,2,1,0:T(8,128)S(1)} %shard_map.104.refs_1_), custom_call_target="tpu_custom_call" | custom-call | tf_op jit(solution)/shard_map/pallas_call | solution.py:562
  (7 shorter events, 0.2 us)
Async XLA Ops:
  1.9 9.4 %collective-permute-start.2 = (bf16[312,128]{1,0:T(8,128)(2,1)S(1)}, bf16[312,128]{1,0:T(8,128)(2,1)S(1)}, u32[]{:S(2)}, u32[]{:S(2)}) collective-permute-start(bf16[312,128]{1,0:T(8,128)(2,1)S(1)} %get-tuple-element.37), channel_id=1, source_target_pairs={{0,1},{1,2},{2,3},{3,0},{4,5},{5,6},{6,7},{7,4},{8,9},{9,10},{10,1... | collective-permute-start | bytes 239624 | tf_op jit(solution)/shard_map/ppermute | solution.py:464
  5.3 7.4 %collective-permute-start = (f32[144,128]{1,0:T(8,128)S(1)}, f32[144,128]{1,0:T(8,128)S(1)}, u32[]{:S(2)}, u32[]{:S(2)}) collective-permute-start(f32[144,128]{1,0:T(8,128)S(1)} %get-tuple-element.35), channel_id=1, source_target_pairs={{0,4},{4,8},{8,12},{12,16},{16,20},{20,24},{24,28},{28,0},{1,5},{5... | collective-permute-start | bytes 221192 | tf_op jit(solution)/shard_map/ppermute | solution.py:470
  5.4 7.1 %collective-permute-start.3 = (bf16[312,128]{1,0:T(8,128)(2,1)S(1)}, bf16[312,128]{1,0:T(8,128)(2,1)S(1)}, u32[]{:S(2)}, u32[]{:S(2)}) collective-permute-start(bf16[312,128]{1,0:T(8,128)(2,1)S(1)} %get-tuple-element.38), channel_id=1, source_target_pairs={{0,2},{1,3},{2,0},{3,1},{4,6},{5,7},{6,4},{7,5},{8,10},{9,11},{10,... | collective-permute-start | bytes 239624 | tf_op jit(solution)/shard_map/ppermute | solution.py:464
  8.1 5.4 %collective-permute-start.1 = (bf16[312,128]{1,0:T(8,128)(2,1)S(1)}, bf16[312,128]{1,0:T(8,128)(2,1)S(1)}, u32[]{:S(2)}, u32[]{:S(2)}) collective-permute-start(bf16[312,128]{1,0:T(8,128)(2,1)S(1)} %get-tuple-element.32._), channel_id=1, source_target_pairs={{0,3},{1,0},{2,1},{3,2},{4,7},{5,4},{6,5},{7,6},{8,11},{9,8},{10,9... | collective-permute-start | bytes 239624 | tf_op jit(solution)/shard_map/ppermute | solution.py:464
  13.5 2.4 %copy-start = (bf16[4,256,256]{2,1,0:T(8,128)(2,1)S(1)}, bf16[4,256,256]{2,1,0:T(8,128)(2,1)}, u32[]{:S(2)}) copy-start(bf16[4,256,256]{2,1,0:T(8,128)(2,1)} %constant.2.clone.tables) | copy-start | bytes 1572868
  13.8 2.1 %collective-permute-start.5 = (bf16[256,128]{1,0:T(8,128)(2,1)S(1)}, bf16[256,128]{1,0:T(8,128)(2,1)S(1)}, u32[]{:S(2)}, u32[]{:S(2)}) collective-permute-start(bf16[256,128]{1,0:T(8,128)(2,1)S(1)} %get-tuple-element.43), channel_id=1, source_target_pairs={{0,4},{4,0},{8,12},{12,8},{16,20},{20,16},{24,28},{28,24},{1,5},{5... | collective-permute-start | bytes 196616 | tf_op jit(solution)/shard_map/ppermute | solution.py:470
  14.3 4.3 %collective-permute-start.4 = (bf16[256,128]{1,0:T(8,128)(2,1)S(1)}, bf16[256,128]{1,0:T(8,128)(2,1)S(1)}, u32[]{:S(2)}, u32[]{:S(2)}) collective-permute-start(bf16[256,128]{1,0:T(8,128)(2,1)S(1)} %get-tuple-element.41), channel_id=1, source_target_pairs={{0,1},{1,0},{2,3},{3,2},{4,8},{5,9},{6,10},{7,11},{8,4},{9,5},{10,... | collective-permute-start | bytes 196616 | tf_op jit(solution)/shard_map/ppermute | solution.py:485
  19.9 7.2 %collective-permute-start.7 = (bf16[312,128]{1,0:T(8,128)(2,1)S(1)}, bf16[312,128]{1,0:T(8,128)(2,1)S(1)}, u32[]{:S(2)}, u32[]{:S(2)}) collective-permute-start(bf16[312,128]{1,0:T(8,128)(2,1)S(1)} %get-tuple-element.50), channel_id=1, source_target_pairs={{0,1},{1,2},{2,3},{3,0},{4,5},{5,6},{6,7},{7,4},{8,9},{9,10},{10,1... | collective-permute-start | bytes 239624 | tf_op jit(solution)/shard_map/ppermute | solution.py:464
  21.6 7.7 %collective-permute-start.8 = (bf16[312,128]{1,0:T(8,128)(2,1)S(1)}, bf16[312,128]{1,0:T(8,128)(2,1)S(1)}, u32[]{:S(2)}, u32[]{:S(2)}) collective-permute-start(bf16[312,128]{1,0:T(8,128)(2,1)S(1)} %get-tuple-element.51), channel_id=1, source_target_pairs={{0,2},{1,3},{2,0},{3,1},{4,6},{5,7},{6,4},{7,5},{8,10},{9,11},{10,... | collective-permute-start | bytes 239624 | tf_op jit(solution)/shard_map/ppermute | solution.py:464
  24.1 5.9 %collective-permute-start.6 = (bf16[312,128]{1,0:T(8,128)(2,1)S(1)}, bf16[312,128]{1,0:T(8,128)(2,1)S(1)}, u32[]{:S(2)}, u32[]{:S(2)}) collective-permute-start(bf16[312,128]{1,0:T(8,128)(2,1)S(1)} %get-tuple-element.49._), channel_id=1, source_target_pairs={{0,3},{1,0},{2,1},{3,2},{4,7},{5,4},{6,5},{7,6},{8,11},{9,8},{10,9... | collective-permute-start | bytes 239624 | tf_op jit(solution)/shard_map/ppermute | solution.py:464
